TPU v7x, 32 devices: a whole 2x2x4 slice. The times are simulated.
32 devices in a mesh: dp: 2 (over x), seq: 4 (over y, core), tensor: 4 (over z).
Axes of the slice: x: 2, y: 2, z: 4, core: 2. Of those that a mesh axis runs over, the one named last changes fastest.
Arguments:
- attention_output_rows: bfloat16 [2, 4096, 4096], P('dp', 'seq', 'tensor'), may hold values from -6 to 6
- projection_result_gradient: bfloat16 [2, 4096, 4096], P('dp', 'seq'), may hold values from -6 to 6
- adapter_down_weight: bfloat16 [4096, 128], P('tensor'), may hold values from -0.09375 to 0.09375
- adapter_up_weight: bfloat16 [128, 4096], P(None, 'tensor'), may hold values from -0.09375 to 0.09375
- output_projection_weight: bfloat16 [4096, 4096], P('tensor'), may hold values from -0.09375 to 0.09375
- adam_first_moments: float32 [2, 128, 4096], P(None, 'dp', 'tensor'), may hold values from -24 to 24
- adam_second_moments: float32 [2, 128, 4096], P(None, 'dp', 'tensor'), may hold values from 1 to 40
- rank_side_projection: float32 [16, 128], replicated, may hold values from -0.5 to 0.5
- width_side_projection: bfloat16 [4096, 256], replicated, may hold values from -0.09375 to 0.09375
- bounds: int32 [2, 2, 16], P('dp'), may hold values from 0 to 4096, as said below
- example_owner_slot: int32 [2, 16], P('dp'), may hold values from 0 to 15, each once within a row
Outputs:
- attention_out_gradient: bfloat16 [2, 4096, 4096], P('dp', 'seq', 'tensor')
- features: float32 [2, 16, 8192], P('dp', ('seq', 'tensor'))
Inputs may be any that keep to these rules, and one draw needn't show every extreme that they name: bounds[s, 0, e] is the first token of example e of pack s and bounds[s, 1, e] its end (exclusive): the first start is 0, each end is the next start, the last end is 4096, every example has one token or more. The tokens of one aligned block of 1024 tokens of a pack belong to at most 8 examples, and every pack has a block whose tokens belong to exactly 8. `example_owner_slot`: each row names every slot once.
All inputs are finite; a program needn't handle non-finite values.
Results may differ from a plain program's by a relative error of at most 0.014.
Values may be sent and summed in bfloat16 or wider, within the bound.
No kernel may reach another device: no remote copies, remote signals or barrier semaphores. Data moves between devices by JAX's collectives and lax.ppermute only.
A program may use at most 128 MiB of HBM per device.

v0:
```python
import jax
import jax.numpy as jnp
from jax import lax
from jax.sharding import PartitionSpec as P

TOUCH = 8


ADAPTER_SCALE = 4.0
BETA_ONE = 0.9
BETA_TWO = 0.999
EPSILON = 1e-08


def carried_in(shard, axis, join, neutral):
    place = lax.axis_index(axis)
    gathered = jax.tree.map(
        lambda a, kind: lax.all_gather(a.astype(kind), axis), shard, (jnp.bfloat16, jnp.bfloat16)
    )
    state = jax.tree.map(lambda a, e: jnp.zeros_like(a) + jnp.asarray(e, a.dtype), shard, neutral)

    def one(step, state):
        return join(
            state,
            jax.tree.map(
                lambda a, own: lax.dynamic_index_in_dim(a, step, 0, False).astype(own.dtype),
                gathered,
                shard,
            ),
        )

    return lax.fori_loop(0, place, one, state)


def contract_trailing(left, right):
    return lax.dot_general(
        left, right, (((1,), (1,)), ((), ())), preferred_element_type=jnp.float32
    )


def normalize(grads, moments):
    first = BETA_ONE * moments[0] + (1.0 - BETA_ONE) * grads
    second = BETA_TWO * moments[1] + (1.0 - BETA_TWO) * grads * grads
    return (first / (jnp.sqrt(second) + EPSILON)).astype(jnp.bfloat16)


def project(normed, rank_side_projection, right_rows):
    inner = jnp.einsum("kmrd,dc->kmrc", normed, right_rows, preferred_element_type=jnp.float32)
    outer = jnp.einsum(
        "qr,kmrc->kmqc", rank_side_projection, inner, precision=lax.Precision.HIGHEST
    )
    return outer.reshape(outer.shape[0], -1)


def pick_slot(block_parts, index):
    return lax.dynamic_index_in_dim(block_parts, index, 0, keepdims=False)


def carry_on(earlier, later):
    return (later[0] + later[1][:, None, None, None] * earlier[0], earlier[1] * later[1])


def per_device(
    attention_output_rows,
    projection_result_gradient,
    adapter_down_weight,
    adapter_up_weight,
    output_projection_weight,
    adam_first_moments,
    adam_second_moments,
    rank_side_projection,
    width_side_projection,
    bounds,
    example_owner_slot,
):
    packs, blk, width_local = attention_output_rows.shape
    width = projection_result_gradient.shape[2]
    adapter_rank_size = adapter_down_weight.shape[1]
    examples = bounds.shape[2]
    seq_index = lax.axis_index("seq")
    tp_index = lax.axis_index("tensor")
    token_count = attention_output_rows.reshape(packs * blk, width_local)
    gradient_complete = projection_result_gradient.reshape(packs * blk, width)
    gradient_columns = lax.dynamic_slice_in_dim(
        gradient_complete, tp_index * width_local, width_local, 1
    )
    reduced_input = jnp.dot(token_count, adapter_down_weight, preferred_element_type=jnp.float32)
    reduced_gradient = contract_trailing(gradient_columns, adapter_up_weight)
    reduced_input, reduced_gradient = lax.psum((reduced_input, reduced_gradient), "tensor")
    reduced_input = reduced_input.astype(jnp.bfloat16)
    reduced_gradient = reduced_gradient.astype(jnp.bfloat16)
    attention_out_gradient = contract_trailing(
        gradient_complete, output_projection_weight
    ) + ADAPTER_SCALE * contract_trailing(reduced_gradient, adapter_down_weight)
    attention_out_gradient = attention_out_gradient.astype(jnp.bfloat16).reshape(
        packs, blk, width_local
    )
    positions = seq_index * blk + jnp.arange(blk, dtype=jnp.int32)
    starts = bounds[:, 0, :]
    example_id = (
        jnp.sum((starts[:, None, :] <= positions[None, :, None]).astype(jnp.int32), axis=2) - 1
    )
    first_id = example_id[:, 0]
    last_id = example_id[:, blk - 1]
    slot_range = jnp.arange(TOUCH, dtype=jnp.int32)
    in_slot = ((example_id - first_id[:, None])[:, :, None] == slot_range).astype(jnp.bfloat16)
    masked_grad = (
        reduced_gradient.reshape(packs, blk, 1, adapter_rank_size) * in_slot[..., None]
    ).reshape(packs, blk, TOUCH * adapter_rank_size)
    masked_in = (
        reduced_input.reshape(packs, blk, 1, adapter_rank_size) * in_slot[..., None]
    ).reshape(packs, blk, TOUCH * adapter_rank_size)
    part_a = jnp.einsum(
        "ptk,ptd->pkd", masked_grad, attention_output_rows, preferred_element_type=jnp.float32
    )
    part_b = jnp.einsum(
        "ptk,ptd->pkd",
        masked_in,
        gradient_columns.reshape(packs, blk, width_local),
        preferred_element_type=jnp.float32,
    )
    parts = ADAPTER_SCALE * jnp.stack(
        [
            part_a.reshape(packs, TOUCH, adapter_rank_size, width_local),
            part_b.reshape(packs, TOUCH, adapter_rank_size, width_local),
        ],
        axis=2,
    )
    block_parts = parts.astype(jnp.bfloat16)
    owner_row = example_owner_slot[0]
    slots = owner_row.shape[0]
    slot_ids = jnp.arange(slots, dtype=jnp.int32)
    stacked_moments = jnp.stack([adam_first_moments, adam_second_moments])
    moments = lax.all_gather(stacked_moments.astype(jnp.bfloat16), "dp", axis=2, tiled=True).astype(
        stacked_moments.dtype
    )
    right_rows = lax.dynamic_slice_in_dim(
        width_side_projection, tp_index * width_local, width_local, 0
    )
    example_range = jnp.arange(examples, dtype=jnp.int32)
    ends = bounds[:, 1, :]
    block_low = seq_index * blk
    start_first = jnp.sum(jnp.where(example_range[None, :] == first_id[:, None], starts, 0), axis=1)
    continued = start_first < block_low
    single = first_id == last_id
    keep_flag = (single & continued).astype(jnp.float32)
    last_part = jax.vmap(pick_slot)(block_parts, last_id - first_id).astype(jnp.float32)
    identity = (jnp.zeros_like(last_part), jnp.ones_like(keep_flag))
    carried, unused_flag = carried_in((last_part, keep_flag), "seq", carry_on, identity)
    incoming = jnp.where(continued[:, None, None, None], carried, jnp.zeros_like(carried))
    head_mask = (slot_range == 0).astype(jnp.float32)
    totals = (
        block_parts.astype(jnp.float32) + head_mask[None, :, None, None, None] * incoming[:, None]
    )
    normed = normalize(totals.reshape(packs * TOUCH, 2, adapter_rank_size, width_local), moments)
    partial_features = project(normed, rank_side_projection, right_rows)
    slot_example = first_id[:, None] + slot_range[None, :]
    clipped = jnp.clip(slot_example, 0, examples - 1)
    end_of = jnp.sum(
        jnp.where(clipped[:, :, None] == example_range[None, None, :], ends[:, None, :], 0), axis=2
    )
    finished = (slot_range[None, :] <= (last_id - first_id)[:, None]) & (end_of <= block_low + blk)
    flat_example = jnp.arange(packs, dtype=jnp.int32)[:, None] * examples + clipped
    target = jnp.take(owner_row, flat_example.reshape(-1))
    placing = ((target[None, :] == slot_ids[:, None]) & finished.reshape(-1)[None, :]).astype(
        jnp.float32
    )
    buffer = jnp.dot(placing, partial_features, precision=lax.Precision.HIGHEST)
    features = lax.psum_scatter(
        buffer.astype(jnp.bfloat16), ("seq", "tensor"), scatter_dimension=0, tiled=True
    ).astype(jnp.float32)
    return (attention_out_gradient, features[None])


def solution(mesh):
    return jax.shard_map(
        per_device,
        mesh=mesh,
        in_specs=(
            P("dp", "seq", "tensor"),
            P("dp", "seq", None),
            P("tensor", None),
            P(None, "tensor"),
            P("tensor", None),
            P(None, "dp", "tensor"),
            P(None, "dp", "tensor"),
            P(),
            P(),
            P("dp", None, None),
            P("dp", None),
        ),
        out_specs=(P("dp", "seq", "tensor"), P("dp", ("seq", "tensor"), None)),
        check_vma=False,
    )
```

profile of v0, /device:TPU:0, one launch (start us, length us, event | category | flops | bytes accessed | tf_op | source)
XLA Modules:
  0.0 219.5 jit_solution(2836785838095157247)
XLA Ops:
  7.2 1.4 convert_bitcast_fusion
  8.7 0.8 pad_maximum_fusion
  9.6 0.8 slice_bitcast_fusion
  10.5 0.6 fusion.51
  12.4 0.6 broadcast_subtract_fusion
  13.0 2.3 %fusion.18 = f32[1024,128]{1,0:T(8,128)S(1)} fusion(bf16[128,1024]{1,0:T(8,128)(2,1)} %param.16, bf16[1,1024,4096]{2,1,0:T(8,128)(2,1)} %param.14, s32[]{:T(128)S(6)} %select_n.71), kind=kOutput, calls=%fused_computation.27 | convolution fusion | flops 268435456 | bytes 2883588 | tf_op jit(solution)/shard_map/dot_general | solution.py:36
  15.3 0.7 fusion.16
  16.1 45.6 %all-reduce.7 = (bf16[1024,128]{1,0:T(8,128)(2,1)S(1)}, bf16[1024,128]{1,0:T(8,128)(2,1)}) all-reduce(f32[1024,128]{1,0:T(8,128)S(1)} %fusion.18, f32[1024,128]{1,0:T(8,128)S(1)} %fusion.16), channel_id=1, replica_groups=mesh['dp'=2,'seq'=4,'tensor'=4] {'tensor'}, use_global_device_ids=true, to_apply=%region_0.0 | all-reduce | flops 262144 | bytes 1572864 | tf_op jit(solution)/shard_map/psum | solution.py:89
  61.7 1.1 copy.24
  62.9 3.9 %fusion.10 = f32[8,128,1024]{2,1,0:T(8,128)S(1)} fusion(bf16[1,1024,4096]{2,1,0:T(8,128)(2,1)} %param.14, s32[]{:T(128)S(6)} %select_n.71, bf16[1024,128]{0,1:T(8,128)(2,1)S(1)} %copy.24, bf16[1024,8]{0,1:T(8,128)(2,1)S(1)} %fusion.37), kind=kOutput, calls=%fused_computation.19 | convolution fusion | flops 2148532224 | bytes 6569988 | tf_op jit(solution)/shard_map/ptk,ptd->pkd/dot_general | solution.py:116
  66.9 2.3 %fusion.12 = f32[8,128,1024]{2,1,0:T(8,128)S(1)} fusion(bf16[1,1024,1024]{2,1,0:T(8,128)(2,1)S(1)} %copy-done, bf16[1024,8]{0,1:T(8,128)(2,1)S(1)} %fusion.37, bf16[1024,128]{0,1:T(8,128)(2,1)S(1)} %copy.23), kind=kOutput, calls=%fused_computation.21 | convolution fusion | flops 2148532224 | bytes 6569984 | tf_op jit(solution)/shard_map/ptk,ptd->pkd/dot_general | solution.py:113
  69.2 2.0 copy-done.3
  71.2 0.9 fusion.36
  73.4 1.3 fusion.48
  74.7 0.6 fusion.50
  76.0 0.6 fusion.49
  76.6 0.6 dynamic-slice.5
  77.2 1.3 dynamic-update-slice.1
  78.5 6.1 %all-reduce = bf16[4]{0:T(256)(128)(2,1)S(1)} all-reduce(bf16[4]{0:T(256)(128)(2,1)S(1)} %dynamic-update-slice.1), channel_id=2, replica_groups=mesh['dp'=2,'seq'=4,'tensor'=4] {'seq'}, use_global_device_ids=true, to_apply=%add | all-reduce | flops 4 | bytes 16
  84.6 0.6 gather_fusion
  85.3 0.6 and_select_fusion
  86.1 15.2 %fusion.5 = f32[1024,1024]{1,0:T(8,128)} fusion(bf16[1024,4096]{1,0:T(8,128)(2,1)} %param.17, bf16[1,1024,4096]{2,1,0:T(8,128)(2,1)} %param.14), kind=kOutput, calls=%fused_computation.13 | convolution fusion | flops 8589934592 | bytes 20971520 | tf_op jit(solution)/shard_map/dot_general | solution.py:36
  101.3 1.5 convert_element_type.98
  102.8 1.6 fusion.29
  104.4 0.2 while.13
  104.8 8.2 %fusion.8 = f32[8,2,128,256]{3,2,1,0:T(8,128)S(1)} fusion(bf16[4096,256]{1,0:T(8,128)(2,1)} %param.21, s32[]{:T(128)S(6)} %select_n.71, f32[8,1,128,1024]{3,2,0,1:T(8,128)} %bitcast.106, f32[8,1,128,1024]{3,2,0,1:T(8,128)} %bitcast.108, f32[2,128,1024]{2,1,0:T(8,128)} %get-tuple-element.81, f32[2,128,1024]{2,1,0:T(8,128)S(1)} %select_bitcast_fusion, ...), kind=kOutput, calls=%fused_computation.16 | convolution fusion | flops 1103101952 | bytes 14155812 | tf_op jit(solution)/shard_map/kmrd,dc->kmrc/dot_general | solution.py:48
  112.9 1.2 fusion.38
  114.3 1.1 convolution_convert_fusion
  115.4 4.2 %fusion.24 = bf16[1,1024,1024]{2,1,0:T(8,128)(2,1)} fusion(f32[1024,1024]{1,0:T(8,128)} %fusion.5, bf16[1024,128]{1,0:T(8,128)(2,1)S(1)} %get-tuple-element.78, bf16[1024,128]{1,0:T(8,128)(2,1)S(1)} %copy-done.5), kind=kOutput, calls=%fused_computation.33 | convolution fusion | flops 271581184 | bytes 6815744 | tf_op jit(solution)/shard_map/dot_general | solution.py:36
  119.6 0.6 dynamic-slice.6
  120.3 90.6 %all-reduce.6.cloned.1.call-done = bf16[16,8192]{1,0:T(8,128)(2,1)} async-done(((bf16[16,8192]{1,0:T(8,128)(2,1)}), bf16[16,8192]{1,0:T(8,128)(2,1)}) %all-reduce.6.cloned.1.call-update) | async-done | bytes 262160
  210.8 2.2 bitcast_convert_fusion
  (40 shorter events, 1.0 us)
Async XLA Ops:
  7.2 8.2 %copy-start = (bf16[1,1024,1024]{2,1,0:T(8,128)(2,1)S(1)}, bf16[1,1024,1024]{2,1,0:T(8,128)(2,1)}, u32[]{:S(2)}) copy-start(bf16[1,1024,1024]{2,1,0:T(8,128)(2,1)} %param.13) | copy-start | bytes 6291460
  7.2 8.2 %copy-start.4 = (bf16[1024,128]{1,0:T(8,128)(2,1)S(1)}, bf16[1024,128]{1,0:T(8,128)(2,1)}, u32[]{:S(2)}) copy-start(bf16[1024,128]{1,0:T(8,128)(2,1)} %param.15) | copy-start | bytes 786436
  7.2 94.1 %all-gather.4.cloned.1.call-start = ((), (), s32[]{:S(2)}) async-start(), calls=%async_computation | async-start | bytes 1572864 | tf_op jit(solution)/shard_map/all_gather | solution.py:134
  9.5 94.8 %all-gather.6.cloned.1.call-start = ((), (), s32[]{:S(2)}) async-start(), calls=%async_computation.1 | async-start | bytes 2621440 | tf_op jit(solution)/shard_map/all_gather | solution.py:18
  66.9 2.4 %copy-start.2 = (f32[8,128,1024]{2,1,0:T(8,128)}, f32[8,128,1024]{2,1,0:T(8,128)S(1)}, u32[]{:S(2)}) copy-start(f32[8,128,1024]{2,1,0:T(8,128)S(1)} %fusion.10) | copy-start | bytes 12582916
  69.2 2.0 copy-start.3
  71.2 2.2 %copy-start.7 = (s32[1,2,16]{2,1,0:T(2,128)S(1)}, s32[1,2,16]{2,1,0:T(2,128)}, u32[]{:S(2)}) copy-start(s32[1,2,16]{2,1,0:T(2,128)} %param.22) | copy-start | bytes 388
  71.2 5.4 %copy-start.9 = (u32[32]{0:T(128)S(1)}, u32[32]{0:T(128)}, u32[]{:S(2)}) copy-start(u32[32]{0:T(128)} %constant.103) | copy-start | bytes 388
  71.2 13.4 %copy-start.1 = (s32[1,16]{1,0:T(1,128)S(1)}, s32[1,16]{1,0:T(1,128)}, u32[]{:S(2)}) copy-start(s32[1,16]{1,0:T(1,128)} %param.23) | copy-start | bytes 196
  72.1 138.7 %all-reduce.6.cloned.1.call-start = ((), (), s32[]{:S(2)}) async-start(), calls=%async_computation.2 | async-start | bytes 524288
  104.7 8.2 %copy-start.6 = (f32[16,128]{1,0:T(8,128)S(1)}, f32[16,128]{1,0:T(8,128)}, u32[]{:S(2)}) copy-start(f32[16,128]{1,0:T(8,128)} %param.20) | copy-start | bytes 24580
  104.7 10.7 %copy-start.5 = (bf16[1024,128]{1,0:T(8,128)(2,1)S(1)}, bf16[1024,128]{1,0:T(8,128)(2,1)}, u32[]{:S(2)}) copy-start(bf16[1024,128]{1,0:T(8,128)(2,1)} %param.15) | copy-start | bytes 786436
  114.1 5.5 %copy-start.8 = (u32[32]{0:T(128)S(1)}, u32[32]{0:T(128)}, u32[]{:S(2)}) copy-start(u32[32]{0:T(128)} %constant.109) | copy-start | bytes 388
Sparse Core Ops, SparseCore 0:
  10.1 23.9 all-gather.3
  72.2 21.9 all-gather.5
  115.5 95.2 all-reduce.5
where the time goes:
time: 220 us
  waiting for transfers between devices  90.6 us (41%)
  blocking collectives  51.8 us (24%)
  matrix products  39.1 us (18%)
  between operations  17.1 us (8%)
  other arithmetic  12.5 us (6%)
  local copies, waits for them, and re-layouts  8.07 us (4%)
    unnamed x4, waiting for transfers between devices  90.6 us
    psum x1, blocking collectives, per_device(): lax.psum((reduced_input, reduced_gradient), 'tensor')  45.6 us
    dot_general x3, matrix products, contract_trailing(): lax.dot_general(left, right, (((1,), (1,)), ((), ())), preferred_element_...  21.7 us
    dot_general x1, matrix products, project(): jnp.einsum('kmrd,dc->kmrc', normed, right_rows, preferred_element_type=jn...  8.15 us
    unnamed x1, blocking collectives  6.13 us
    unnamed x25, local copies, waits for them, and re-layouts  4.7 us
  transfers between devices with their start and end apart: 3, of which 1 were waited for; matrix products, arithmetic and copies ran while one was open for 19% of the time, Pallas kernels for 0%

commit v1 on v0

--- a/solution.py
+++ b/solution.py
@@ -12,24 +12,53 @@
 EPSILON = 1e-08
 
 
-def carried_in(shard, axis, join, neutral):
+def shifted(value, axis, shift):
+    size = lax.axis_size(axis)
+    return lax.ppermute(value, axis, [(i, (i + shift) % size) for i in range(size)])
+
+
+def sum_over(partial, axis):
+    size = lax.axis_size(axis)
     place = lax.axis_index(axis)
-    gathered = jax.tree.map(
-        lambda a, kind: lax.all_gather(a.astype(kind), axis), shard, (jnp.bfloat16, jnp.bfloat16)
-    )
-    state = jax.tree.map(lambda a, e: jnp.zeros_like(a) + jnp.asarray(e, a.dtype), shard, neutral)
-
-    def one(step, state):
-        return join(
-            state,
-            jax.tree.map(
-                lambda a, own: lax.dynamic_index_in_dim(a, step, 0, False).astype(own.dtype),
-                gathered,
-                shard,
-            ),
+    rows = partial.shape[0] // size
+
+    def block(index):
+        return lax.dynamic_slice_in_dim(partial, (index % size) * rows, rows, 0)
+
+    arrived = [shifted(block(place + k), axis, k) for k in range(1, size)]
+    total = block(place).astype(jnp.float32)
+    for term in arrived:
+        total = total + term.astype(jnp.float32)
+    total = total.astype(jnp.bfloat16)
+    whole = jnp.zeros_like(partial)
+    whole = lax.dynamic_update_slice_in_dim(whole, total, place * rows, 0)
+    for k in range(1, size):
+        whole = lax.dynamic_update_slice_in_dim(
+            whole, shifted(total, axis, k), ((place - k) % size) * rows, 0
         )
-
-    return lax.fori_loop(0, place, one, state)
+    return whole
+
+
+def carried_in(own, keep, axis):
+    size = lax.axis_size(axis)
+    place = lax.axis_index(axis)
+    incoming = jnp.zeros_like(own)
+    for k in range(size - 1):
+        outgoing = (
+            own.astype(jnp.float32) + keep[:, None, None, None] * incoming.astype(jnp.float32)
+        ).astype(jnp.bfloat16)
+        arrived = lax.ppermute(outgoing, axis, [(k, k + 1)])
+        incoming = jnp.where(place == k + 1, arrived, incoming)
+    return incoming
+
+
+def gather_rows(value, axis, dim):
+    size = lax.axis_size(axis)
+    if size != 2:
+        return lax.all_gather(value, axis, axis=dim, tiled=True)
+    other = shifted(value, axis, 1)
+    low = lax.axis_index(axis) == 0
+    return jnp.concatenate([jnp.where(low, value, other), jnp.where(low, other, value)], axis=dim)
 
 
 def contract_trailing(left, right):
@@ -54,10 +83,6 @@
 
 def pick_slot(block_parts, index):
     return lax.dynamic_index_in_dim(block_parts, index, 0, keepdims=False)
-
-
-def carry_on(earlier, later):
-    return (later[0] + later[1][:, None, None, None] * earlier[0], earlier[1] * later[1])
 
 
 def per_device(
@@ -86,9 +111,8 @@
     )
     reduced_input = jnp.dot(token_count, adapter_down_weight, preferred_element_type=jnp.float32)
     reduced_gradient = contract_trailing(gradient_columns, adapter_up_weight)
-    reduced_input, reduced_gradient = lax.psum((reduced_input, reduced_gradient), "tensor")
-    reduced_input = reduced_input.astype(jnp.bfloat16)
-    reduced_gradient = reduced_gradient.astype(jnp.bfloat16)
+    reduced_input = sum_over(reduced_input.astype(jnp.bfloat16), "tensor")
+    reduced_gradient = sum_over(reduced_gradient.astype(jnp.bfloat16), "tensor")
     attention_out_gradient = contract_trailing(
         gradient_complete, output_projection_weight
     ) + ADAPTER_SCALE * contract_trailing(reduced_gradient, adapter_down_weight)
@@ -131,7 +155,7 @@
     slots = owner_row.shape[0]
     slot_ids = jnp.arange(slots, dtype=jnp.int32)
     stacked_moments = jnp.stack([adam_first_moments, adam_second_moments])
-    moments = lax.all_gather(stacked_moments.astype(jnp.bfloat16), "dp", axis=2, tiled=True).astype(
+    moments = gather_rows(stacked_moments.astype(jnp.bfloat16), "dp", 2).astype(
         stacked_moments.dtype
     )
     right_rows = lax.dynamic_slice_in_dim(
@@ -144,9 +168,8 @@
     continued = start_first < block_low
     single = first_id == last_id
     keep_flag = (single & continued).astype(jnp.float32)
-    last_part = jax.vmap(pick_slot)(block_parts, last_id - first_id).astype(jnp.float32)
-    identity = (jnp.zeros_like(last_part), jnp.ones_like(keep_flag))
-    carried, unused_flag = carried_in((last_part, keep_flag), "seq", carry_on, identity)
+    last_part = jax.vmap(pick_slot)(block_parts, last_id - first_id)
+    carried = carried_in(last_part, keep_flag, "seq").astype(jnp.float32)
     incoming = jnp.where(continued[:, None, None, None], carried, jnp.zeros_like(carried))
     head_mask = (slot_range == 0).astype(jnp.float32)
     totals = (
@@ -166,9 +189,10 @@
         jnp.float32
     )
     buffer = jnp.dot(placing, partial_features, precision=lax.Precision.HIGHEST)
-    features = lax.psum_scatter(
-        buffer.astype(jnp.bfloat16), ("seq", "tensor"), scatter_dimension=0, tiled=True
-    ).astype(jnp.float32)
+    arrived = lax.all_to_all(
+        buffer.astype(jnp.bfloat16), ("seq", "tensor"), split_axis=0, concat_axis=0, tiled=True
+    )
+    features = jnp.sum(arrived.astype(jnp.float32), axis=0, keepdims=True)
     return (attention_out_gradient, features[None])
 
 

time: 220 us -> 102 us (0.46)
  waiting for transfers between devices: 90.6 us -> 6.76 us
  blocking collectives: 51.8 us -> 0 us
  starting transfers between devices: 0.12 us -> 37.4 us
  between operations: 17.1 us -> 4.68 us
  matrix products: 39.1 us -> 33.2 us
  other arithmetic: 12.5 us -> 9.94 us
    unnamed x4 -> x0, waiting for transfers between devices: 90.6 us -> none
    psum x1 -> x0, blocking collectives: 45.6 us -> none  [per_device(): lax.psum((reduced_input, reduced_gradient), 'tensor')]
    ppermute x0 -> x16, starting transfers between devices: none -> 23.6 us  [the longest x13 20 us: shifted(): lax.ppermute(value, axis, [(i, (i + shift) % size) for i in range(size)])]
    all_to_all x0 -> x1, starting transfers between devices: none -> 13.8 us  [per_device(): lax.all_to_all(buffer.astype(jnp.bfloat16), ('seq', 'tensor'), split_axis...]
    ppermute x0 -> x16, waiting for transfers between devices: none -> 6.76 us  [the longest x13 6.75 us: shifted(): lax.ppermute(value, axis, [(i, (i + shift) % size) for i in range(size)])]
    unnamed x1 -> x0, blocking collectives: 6.13 us -> none
    dot_general x3, matrix products: 21.7 us -> 17.2 us  [contract_trailing(): lax.dot_general(left, right, (((1,), (1,)), ((), ())), preferred_element_...]
    unnamed x25 -> x31, local copies, waits for them, and re-layouts: 4.7 us -> 6.81 us
  transfers between devices with their start and end apart: 3 -> 17, of which waited for: 1 -> 4; matrix products, arithmetic and copies ran while one was open for 19% -> 26% of each run, Pallas kernels for 0% -> 0%
where the time goes in v1:
time: 102 us
  starting transfers between devices  37.4 us (37%)
  matrix products  33.2 us (33%)
  other arithmetic  9.94 us (10%)
  local copies, waits for them, and re-layouts  9.59 us (9%)
  waiting for transfers between devices  6.76 us (7%)
  between operations  4.68 us (5%)
    ppermute x13, starting transfers between devices, shifted(): lax.ppermute(value, axis, [(i, (i + shift) % size) for i in range(size)])  20 us
    dot_general x3, matrix products, contract_trailing(): lax.dot_general(left, right, (((1,), (1,)), ((), ())), preferred_element_...  17.2 us
    all_to_all x1, starting transfers between devices, per_device(): lax.all_to_all(buffer.astype(jnp.bfloat16), ('seq', 'tensor'), split_axis...  13.8 us
    unnamed x31, local copies, waits for them, and re-layouts  6.81 us
    ppermute x13, waiting for transfers between devices, shifted(): lax.ppermute(value, axis, [(i, (i + shift) % size) for i in range(size)])  6.75 us
    dot_general x1, matrix products, project(): jnp.einsum('kmrd,dc->kmrc', normed, right_rows, preferred_element_type=jn...  6.38 us
    dot_general x1, matrix products, per_device(): jnp.einsum('ptk,ptd->pkd', masked_in, gradient_columns.reshape(packs, blk...  4.03 us
    ppermute x3, starting transfers between devices, carried_in(): arrived = lax.ppermute(outgoing, axis, [(k, k + 1)])  3.64 us
  transfers between devices with their start and end apart: 17, of which 4 were waited for; matrix products, arithmetic and copies ran while one was open for 26% of the time, Pallas kernels for 0%

profile of v1, /device:TPU:0, one launch (start us, length us, event | category | flops | bytes accessed | tf_op | source)
XLA Modules:
  0.0 101.6 jit_solution(4162424266534079442)
XLA Ops:
  0.7 2.4 %fusion.26 = bf16[1024,128]{1,0:T(8,128)(2,1)S(1)} fusion(bf16[128,1024]{1,0:T(8,128)(2,1)} %param.14, bf16[1,1024,4096]{2,1,0:T(8,128)(2,1)} %param.12, s32[]{:T(128)S(6)} %select_n.173), kind=kOutput, calls=%fused_computation.35 | convolution fusion | flops 268566528 | bytes 2621444 | tf_op jit(solution)/shard_map/dot_general | solution.py:65
  3.2 3.1 %collective-permute-start = (bf16[256,128]{1,0:T(8,128)(2,1)S(1)}, bf16[256,128]{1,0:T(8,128)(2,1)S(1)}, u32[]{:S(2)}, u32[]{:S(2)}) collective-permute-start(bf16[256,128]{1,0:T(8,128)(2,1)S(1)} %get-tuple-element.20), channel_id=1, source_target_pairs={{0,1},{1,2},{2,3},{3,0},{4,5},{5,6},{6,7},{7,4},{8,9},{9,10},{10,1... | collective-permute-start | bytes 196616 | tf_op jit(solution)/shard_map/ppermute | solution.py:17
  6.3 2.1 %collective-permute-start.2 = (bf16[256,128]{1,0:T(8,128)(2,1)S(1)}, bf16[256,128]{1,0:T(8,128)(2,1)S(1)}, u32[]{:S(2)}, u32[]{:S(2)}) collective-permute-start(bf16[256,128]{1,0:T(8,128)(2,1)S(1)} %get-tuple-element.21), channel_id=1, source_target_pairs={{0,3},{1,0},{2,1},{3,2},{4,7},{5,4},{6,5},{7,6},{8,11},{9,8},{10,9... | collective-permute-start | bytes 196616 | tf_op jit(solution)/shard_map/ppermute | solution.py:17
  8.4 0.9 collective-permute-start.1
  9.3 1.7 %fusion.29 = bf16[1024,128]{1,0:T(8,128)(2,1)S(1)} fusion(bf16[1024,128]{1,0:T(8,128)(2,1)} %param.13, bf16[1,1024,1024]{2,1,0:T(8,128)(2,1)S(1)} %copy-done), kind=kOutput, calls=%fused_computation.36 | convolution fusion | flops 268566528 | bytes 2621440 | tf_op jit(solution)/shard_map/dot_general | solution.py:112
  11.0 1.6 %collective-permute-start.7 = (bf16[256,128]{1,0:T(8,128)(2,1)S(1)}, bf16[256,128]{1,0:T(8,128)(2,1)S(1)}, u32[]{:S(2)}, u32[]{:S(2)}) collective-permute-start(bf16[256,128]{1,0:T(8,128)(2,1)S(1)} %get-tuple-element.17), channel_id=1, source_target_pairs={{0,1},{1,2},{2,3},{3,0},{4,5},{5,6},{6,7},{7,4},{8,9},{9,10},{10,1... | collective-permute-start | bytes 196616 | tf_op jit(solution)/shard_map/ppermute | solution.py:17
  12.6 2.2 %collective-permute-start.9 = (bf16[256,128]{1,0:T(8,128)(2,1)S(1)}, bf16[256,128]{1,0:T(8,128)(2,1)S(1)}, u32[]{:S(2)}, u32[]{:S(2)}) collective-permute-start(bf16[256,128]{1,0:T(8,128)(2,1)S(1)} %get-tuple-element.18), channel_id=1, source_target_pairs={{0,3},{1,0},{2,1},{3,2},{4,7},{5,4},{6,5},{7,6},{8,11},{9,8},{10,9... | collective-permute-start | bytes 196616 | tf_op jit(solution)/shard_map/ppermute | solution.py:17
  18.1 2.0 %collective-permute-start.5 = (bf16[256,128]{1,0:T(8,128)(2,1)S(1)}, bf16[256,128]{1,0:T(8,128)(2,1)S(1)}, u32[]{:S(2)}, u32[]{:S(2)}) collective-permute-start(bf16[256,128]{1,0:T(8,128)(2,1)S(1)} %add_convert_fusion.2), channel_id=1, source_target_pairs={{0,3},{1,0},{2,1},{3,2},{4,7},{5,4},{6,5},{7,6},{8,11},{9,8},{10,9... | collective-permute-start | bytes 196616 | tf_op jit(solution)/shard_map/ppermute | solution.py:17
  21.0 1.9 %collective-permute-start.3 = (bf16[256,128]{1,0:T(8,128)(2,1)S(1)}, bf16[256,128]{1,0:T(8,128)(2,1)S(1)}, u32[]{:S(2)}, u32[]{:S(2)}) collective-permute-start(bf16[256,128]{1,0:T(8,128)(2,1)S(1)} %add_convert_fusion.2), channel_id=1, source_target_pairs={{0,1},{1,2},{2,3},{3,0},{4,5},{5,6},{6,7},{7,4},{8,9},{9,10},{10,1... | collective-permute-start | bytes 196616 | tf_op jit(solution)/shard_map/ppermute | solution.py:17
  22.9 2.5 %collective-permute-done.8 = bf16[256,128]{1,0:T(8,128)(2,1)S(1)} collective-permute-done((bf16[256,128]{1,0:T(8,128)(2,1)S(1)}, bf16[256,128]{1,0:T(8,128)(2,1)S(1)}, u32[]{:S(2)}, u32[]{:S(2)}) %collective-permute-start.8) | collective-permute-done | bytes 65568 | tf_op jit(solution)/shard_map/ppermute | solution.py:17
  25.6 2.0 %collective-permute-start.10 = (bf16[256,128]{1,0:T(8,128)(2,1)S(1)}, bf16[256,128]{1,0:T(8,128)(2,1)S(1)}, u32[]{:S(2)}, u32[]{:S(2)}) collective-permute-start(bf16[256,128]{1,0:T(8,128)(2,1)S(1)} %add_convert_fusion.1), channel_id=1, source_target_pairs={{0,1},{1,2},{2,3},{3,0},{4,5},{5,6},{6,7},{7,4},{8,9},{9,10},{10,1... | collective-permute-start | bytes 196616 | tf_op jit(solution)/shard_map/ppermute | solution.py:17
  27.7 1.3 %collective-permute-start.11 = (bf16[256,128]{1,0:T(8,128)(2,1)S(1)}, bf16[256,128]{1,0:T(8,128)(2,1)S(1)}, u32[]{:S(2)}, u32[]{:S(2)}) collective-permute-start(bf16[256,128]{1,0:T(8,128)(2,1)S(1)} %add_convert_fusion.1), channel_id=1, source_target_pairs={{0,2},{1,3},{2,0},{3,1},{4,6},{5,7},{6,4},{7,5},{8,10},{9,11},{10,... | collective-permute-start | bytes 196616 | tf_op jit(solution)/shard_map/ppermute | solution.py:17
  29.2 2.6 %collective-permute-done.10 = bf16[256,128]{1,0:T(8,128)(2,1)S(1)} collective-permute-done((bf16[256,128]{1,0:T(8,128)(2,1)S(1)}, bf16[256,128]{1,0:T(8,128)(2,1)S(1)}, u32[]{:S(2)}, u32[]{:S(2)}) %collective-permute-start.10) | collective-permute-done | bytes 65568 | tf_op jit(solution)/shard_map/ppermute | solution.py:17
  33.4 4.0 %fusion.11 = f32[8,128,1024]{2,1,0:T(8,128)S(1)} fusion(bf16[1,1024,4096]{2,1,0:T(8,128)(2,1)} %param.12, s32[]{:T(128)S(6)} %select_n.173, bf16[1024,128]{0,1:T(8,128)(2,1)S(1)} %get-tuple-element.29, bf16[1024,8]{0,1:T(8,128)(2,1)S(1)} %fusion.46), kind=kOutput, calls=%fused_computation.18 | convolution fusion | flops 2148532224 | bytes 6569988 | tf_op jit(solution)/shard_map/ptk,ptd->pkd/dot_general | solution.py:140
  37.5 2.3 %fusion.13 = f32[8,128,1024]{2,1,0:T(8,128)S(1)} fusion(bf16[1,1024,1024]{2,1,0:T(8,128)(2,1)S(1)} %copy-done, bf16[1024,8]{0,1:T(8,128)(2,1)S(1)} %fusion.46, bf16[1024,128]{0,1:T(8,128)(2,1)S(1)} %get-tuple-element.30), kind=kOutput, calls=%fused_computation.20 | convolution fusion | flops 2148532224 | bytes 6569984 | tf_op jit(solution)/shard_map/ptk,ptd->pkd/dot_general | solution.py:137
  40.0 1.9 %copy-done.4 = f32[8,128,1024]{2,1,0:T(8,128)} copy-done((f32[8,128,1024]{2,1,0:T(8,128)}, f32[8,128,1024]{2,1,0:T(8,128)S(1)}, u32[]{:S(2)}) %copy-start.4) | copy-done | bytes 4194328
  41.8 1.3 %collective-permute-start.13 = (bf16[1,2,128,1024]{3,2,1,0:T(8,128)(2,1)S(1)}, bf16[1,2,128,1024]{3,2,1,0:T(8,128)(2,1)S(1)}, u32[]{:S(2)}, u32[]{:S(2)}) collective-permute-start(bf16[1,2,128,1024]{3,2,1,0:T(8,128)(2,1)S(1)} %fusion.45), channel_id=1, source_target_pairs={{0,4},{1,5},{2,6},{3,7},{16,20},{17,21},{18,22},{19,23}} | collective-permute-start | bytes 1572872 | tf_op jit(solution)/shard_map/ppermute | solution.py:50
  44.8 1.5 %collective-permute-start.6 = (bf16[2,2,64,1024]{3,2,1,0:T(8,128)(2,1)}, bf16[2,2,64,1024]{3,2,1,0:T(8,128)(2,1)}, u32[]{:S(2)}, u32[]{:S(2)}) collective-permute-start(bf16[2,2,64,1024]{3,2,1,0:T(8,128)(2,1)} %pad_maximum_fusion), channel_id=1, source_target_pairs={{0,16},{16,0},{1,17},{17,1},{2,18},{18,2},{3,19},{19,3},{4,20},{20... | collective-permute-start | bytes 1572872 | tf_op jit(solution)/shard_map/ppermute | solution.py:17
  47.6 1.3 %fusion.56 = s32[]{:T(128)} fusion(s32[1,2,16]{2,1,0:T(2,128)S(1)} %copy-done.13, s32[]{:T(128)} %bitcast.5), kind=kLoop, calls=%fused_computation.103 | loop fusion | flops 47 | bytes 72 | tf_op jit(solution)/shard_map/reduce_sum | solution.py:167
  50.9 1.0 fusion.33
  51.9 1.5 %collective-permute-start.14 = (bf16[1,2,128,1024]{3,2,1,0:T(8,128)(2,1)}, bf16[1,2,128,1024]{3,2,1,0:T(8,128)(2,1)}, u32[]{:S(2)}, u32[]{:S(2)}) collective-permute-start(bf16[1,2,128,1024]{3,2,1,0:T(8,128)(2,1)} %fusion.33), channel_id=1, source_target_pairs={{4,8},{5,9},{6,10},{7,11},{20,24},{21,25},{22,26},{23,27}} | collective-permute-start | bytes 1572872 | tf_op jit(solution)/shard_map/ppermute | solution.py:50
  54.7 0.9 collective-permute-start.15
  56.3 1.2 %broadcast_select_fusion.3 = (bf16[2,2,64,1024]{3,2,1,0:T(8,128)(2,1)S(1)}, bf16[2,2,64,1024]{3,2,1,0:T(8,128)(2,1)S(1)}) fusion(bf16[2,2,64,1024]{3,2,1,0:T(8,128)(2,1)} %collective-permute-done.6, pred[]{:T(512)S(6)} %eq.115, bf16[1,2,64,1024]{3,2,1,0:T(8,128)(2,1)S(1)} %get-tuple-element.31, bf16[1,2,64,1024]{3,2,1,0:T(8,128)(2,1)} %copy-done.6), kind=kLoop, calls=%fused_computation.59 | loop fusion | flops 786432 | bytes 2097153 | tf_op jit(solution)/shard_map/jit(_where)/select_n | solution.py:61
  58.2 1.5 %copy-done.5 = f32[8,128,1024]{2,1,0:T(8,128)S(1)} copy-done((f32[8,128,1024]{2,1,0:T(8,128)S(1)}, f32[8,128,1024]{2,1,0:T(8,128)}, u32[]{:S(2)}) %copy-start.5) | copy-done | bytes 4194328
  59.7 1.3 %copy-done.3 = f32[8,128,1024]{2,1,0:T(8,128)S(1)} copy-done((f32[8,128,1024]{2,1,0:T(8,128)S(1)}, f32[8,128,1024]{2,1,0:T(8,128)}, u32[]{:S(2)}) %copy-start.3) | copy-done | bytes 4194328
  61.0 6.4 %fusion.9 = f32[8,2,128,256]{3,2,1,0:T(8,128)S(1)} fusion(bf16[4096,256]{1,0:T(8,128)(2,1)} %param.19, s32[]{:T(128)S(6)} %select_n.173, f32[8,1,128,1024]{3,2,0,1:T(8,128)S(1)} %bitcast.94, f32[8,1,128,1024]{3,2,0,1:T(8,128)S(1)} %bitcast.96, f32[2,128,1024]{2,1,0:T(8,128)S(1)} %get-tuple-element.14, f32[2,128,1024]{2,1,0:T(8,128)S(1)} %select_bitcast_fusion, ...), kind=kOutput, calls=%fused_computation.15 | convolution fusion | flops 1103101952 | bytes 14155812 | tf_op jit(solution)/shard_map/kmrd,dc->kmrc/dot_general | solution.py:77
  67.4 1.2 %fusion.47 = f32[8,2,256,16]{2,3,1,0:T(8,128)S(1)} fusion(f32[8,2,128,256]{3,2,1,0:T(8,128)S(1)} %fusion.9, f32[16,128]{1,0:T(8,128)S(1)} %copy-done.12), kind=kOutput, calls=%fused_computation.68 | convolution fusion | flops 100663296 | bytes 2367488 | tf_op jit(solution)/shard_map/qr,kmrc->kmqc/dot_general | solution.py:78
  70.5 0.9 reshape.509
  71.4 13.8 %all-to-all-start = ((bf16[16,2,4096]{2,1,0:T(2,128)(2,1)}), bf16[16,2,4096]{2,1,0:T(2,128)(2,1)S(1)}, u32[]{:S(2)}, u32[]{:S(2)}) async-start(bf16[16,2,4096]{2,1,0:T(2,128)(2,1)} %reshape.509), calls=%async_computation | async-start | bytes 524288 | tf_op jit(solution)/shard_map/all_to_all | solution.py:192
  85.2 12.7 %fusion.6 = f32[1024,1024]{1,0:T(8,128)S(1)} fusion(bf16[1024,4096]{1,0:T(8,128)(2,1)} %param.15, bf16[1,1024,4096]{2,1,0:T(8,128)(2,1)} %param.12), kind=kOutput, calls=%fused_computation.12 | convolution fusion | flops 8589934592 | bytes 20971520 | tf_op jit(solution)/shard_map/dot_general | solution.py:65
  97.9 2.1 %fusion.25 = bf16[1,1024,1024]{2,1,0:T(8,128)(2,1)} fusion(f32[1024,1024]{1,0:T(8,128)S(1)} %fusion.6, bf16[1024,128]{0,1:T(8,128)(2,1)S(1)} %copy-done.9, bf16[1024,128]{1,0:T(8,128)(2,1)S(1)} %copy-done.7), kind=kOutput, calls=%fused_computation.32 | convolution fusion | flops 271581184 | bytes 6815744 | tf_op jit(solution)/shard_map/dot_general | solution.py:65
  100.3 1.3 %convert_reduce_fusion = f32[8192]{0:T(1024)} fusion(bf16[16,1,8192]{2,1,0:T(2,128)(2,1)S(1)} %reshape.510), kind=kLoop, calls=%fused_computation.54 | loop fusion | flops 253952 | bytes 294912 | tf_op jit(solution)/shard_map/reduce_sum | solution.py:195
  (90 shorter events, 12.3 us)
Async XLA Ops:
  0.6 8.7 %copy-start = (bf16[1,1024,1024]{2,1,0:T(8,128)(2,1)S(1)}, bf16[1,1024,1024]{2,1,0:T(8,128)(2,1)}, u32[]{:S(2)}) copy-start(bf16[1,1024,1024]{2,1,0:T(8,128)(2,1)} %param.11) | copy-start | bytes 6291460
  0.6 14.2 %copy-start.13 = (s32[1,2,16]{2,1,0:T(2,128)S(1)}, s32[1,2,16]{2,1,0:T(2,128)}, u32[]{:S(2)}) copy-start(s32[1,2,16]{2,1,0:T(2,128)} %param.20) | copy-start | bytes 388
  3.2 14.5 %collective-permute-start = (bf16[256,128]{1,0:T(8,128)(2,1)S(1)}, bf16[256,128]{1,0:T(8,128)(2,1)S(1)}, u32[]{:S(2)}, u32[]{:S(2)}) collective-permute-start(bf16[256,128]{1,0:T(8,128)(2,1)S(1)} %get-tuple-element.20), channel_id=1, source_target_pairs={{0,1},{1,2},{2,3},{3,0},{4,5},{5,6},{6,7},{7,4},{8,9},{9,10},{10,1... | collective-permute-start | bytes 196616 | tf_op jit(solution)/shard_map/ppermute | solution.py:17
  6.3 11.7 %collective-permute-start.2 = (bf16[256,128]{1,0:T(8,128)(2,1)S(1)}, bf16[256,128]{1,0:T(8,128)(2,1)S(1)}, u32[]{:S(2)}, u32[]{:S(2)}) collective-permute-start(bf16[256,128]{1,0:T(8,128)(2,1)S(1)} %get-tuple-element.21), channel_id=1, source_target_pairs={{0,3},{1,0},{2,1},{3,2},{4,7},{5,4},{6,5},{7,6},{8,11},{9,8},{10,9... | collective-permute-start | bytes 196616 | tf_op jit(solution)/shard_map/ppermute | solution.py:17
  8.4 9.6 %collective-permute-start.1 = (bf16[256,128]{1,0:T(8,128)(2,1)S(1)}, bf16[256,128]{1,0:T(8,128)(2,1)S(1)}, u32[]{:S(2)}, u32[]{:S(2)}) collective-permute-start(bf16[256,128]{1,0:T(8,128)(2,1)S(1)} %get-tuple-element.22), channel_id=1, source_target_pairs={{0,2},{1,3},{2,0},{3,1},{4,6},{5,7},{6,4},{7,5},{8,10},{9,11},{10,... | collective-permute-start | bytes 196616 | tf_op jit(solution)/shard_map/ppermute | solution.py:17
  11.0 10.0 %collective-permute-start.7 = (bf16[256,128]{1,0:T(8,128)(2,1)S(1)}, bf16[256,128]{1,0:T(8,128)(2,1)S(1)}, u32[]{:S(2)}, u32[]{:S(2)}) collective-permute-start(bf16[256,128]{1,0:T(8,128)(2,1)S(1)} %get-tuple-element.17), channel_id=1, source_target_pairs={{0,1},{1,2},{2,3},{3,0},{4,5},{5,6},{6,7},{7,4},{8,9},{9,10},{10,1... | collective-permute-start | bytes 196616 | tf_op jit(solution)/shard_map/ppermute | solution.py:17
  12.6 10.3 %collective-permute-start.9 = (bf16[256,128]{1,0:T(8,128)(2,1)S(1)}, bf16[256,128]{1,0:T(8,128)(2,1)S(1)}, u32[]{:S(2)}, u32[]{:S(2)}) collective-permute-start(bf16[256,128]{1,0:T(8,128)(2,1)S(1)} %get-tuple-element.18), channel_id=1, source_target_pairs={{0,3},{1,0},{2,1},{3,2},{4,7},{5,4},{6,5},{7,6},{8,11},{9,8},{10,9... | collective-permute-start | bytes 196616 | tf_op jit(solution)/shard_map/ppermute | solution.py:17
  17.7 7.7 %collective-permute-start.8 = (bf16[256,128]{1,0:T(8,128)(2,1)S(1)}, bf16[256,128]{1,0:T(8,128)(2,1)S(1)}, u32[]{:S(2)}, u32[]{:S(2)}) collective-permute-start(bf16[256,128]{1,0:T(8,128)(2,1)S(1)} %get-tuple-element.19), channel_id=1, source_target_pairs={{0,2},{1,3},{2,0},{3,1},{4,6},{5,7},{6,4},{7,5},{8,10},{9,11},{10,... | collective-permute-start | bytes 196616 | tf_op jit(solution)/shard_map/ppermute | solution.py:17
  18.1 9.6 %collective-permute-start.5 = (bf16[256,128]{1,0:T(8,128)(2,1)S(1)}, bf16[256,128]{1,0:T(8,128)(2,1)S(1)}, u32[]{:S(2)}, u32[]{:S(2)}) collective-permute-start(bf16[256,128]{1,0:T(8,128)(2,1)S(1)} %add_convert_fusion.2), channel_id=1, source_target_pairs={{0,3},{1,0},{2,1},{3,2},{4,7},{5,4},{6,5},{7,6},{8,11},{9,8},{10,9... | collective-permute-start | bytes 196616 | tf_op jit(solution)/shard_map/ppermute | solution.py:17
  20.1 13.0 %collective-permute-start.4 = (bf16[256,128]{1,0:T(8,128)(2,1)S(1)}, bf16[256,128]{1,0:T(8,128)(2,1)S(1)}, u32[]{:S(2)}, u32[]{:S(2)}) collective-permute-start(bf16[256,128]{1,0:T(8,128)(2,1)S(1)} %add_convert_fusion.2), channel_id=1, source_target_pairs={{0,2},{1,3},{2,0},{3,1},{4,6},{5,7},{6,4},{7,5},{8,10},{9,11},{10,... | collective-permute-start | bytes 196616 | tf_op jit(solution)/shard_map/ppermute | solution.py:17
  21.0 11.0 %collective-permute-start.3 = (bf16[256,128]{1,0:T(8,128)(2,1)S(1)}, bf16[256,128]{1,0:T(8,128)(2,1)S(1)}, u32[]{:S(2)}, u32[]{:S(2)}) collective-permute-start(bf16[256,128]{1,0:T(8,128)(2,1)S(1)} %add_convert_fusion.2), channel_id=1, source_target_pairs={{0,1},{1,2},{2,3},{3,0},{4,5},{5,6},{6,7},{7,4},{8,9},{9,10},{10,1... | collective-permute-start | bytes 196616 | tf_op jit(solution)/shard_map/ppermute | solution.py:17
  25.6 7.7 %collective-permute-start.12 = (bf16[256,128]{1,0:T(8,128)(2,1)S(1)}, bf16[256,128]{1,0:T(8,128)(2,1)S(1)}, u32[]{:S(2)}, u32[]{:S(2)}) collective-permute-start(bf16[256,128]{1,0:T(8,128)(2,1)S(1)} %add_convert_fusion.1), channel_id=1, source_target_pairs={{0,3},{1,0},{2,1},{3,2},{4,7},{5,4},{6,5},{7,6},{8,11},{9,8},{10,9... | collective-permute-start | bytes 196616 | tf_op jit(solution)/shard_map/ppermute | solution.py:17
  25.6 6.2 %collective-permute-start.10 = (bf16[256,128]{1,0:T(8,128)(2,1)S(1)}, bf16[256,128]{1,0:T(8,128)(2,1)S(1)}, u32[]{:S(2)}, u32[]{:S(2)}) collective-permute-start(bf16[256,128]{1,0:T(8,128)(2,1)S(1)} %add_convert_fusion.1), channel_id=1, source_target_pairs={{0,1},{1,2},{2,3},{3,0},{4,5},{5,6},{6,7},{7,4},{8,9},{9,10},{10,1... | collective-permute-start | bytes 196616 | tf_op jit(solution)/shard_map/ppermute | solution.py:17
  27.7 5.2 %collective-permute-start.11 = (bf16[256,128]{1,0:T(8,128)(2,1)S(1)}, bf16[256,128]{1,0:T(8,128)(2,1)S(1)}, u32[]{:S(2)}, u32[]{:S(2)}) collective-permute-start(bf16[256,128]{1,0:T(8,128)(2,1)S(1)} %add_convert_fusion.1), channel_id=1, source_target_pairs={{0,2},{1,3},{2,0},{3,1},{4,6},{5,7},{6,4},{7,5},{8,10},{9,11},{10,... | collective-permute-start | bytes 196616 | tf_op jit(solution)/shard_map/ppermute | solution.py:17
  33.4 4.1 %copy-start.8 = (bf16[1024,128]{0,1:T(8,128)(2,1)}, bf16[1024,128]{0,1:T(8,128)(2,1)S(1)}, u32[]{:S(2)}) copy-start(bf16[1024,128]{0,1:T(8,128)(2,1)S(1)} %get-tuple-element.30) | copy-start | bytes 786436
  37.4 2.4 %copy-start.2 = (f32[8,128,1024]{2,1,0:T(8,128)}, f32[8,128,1024]{2,1,0:T(8,128)S(1)}, u32[]{:S(2)}) copy-start(f32[8,128,1024]{2,1,0:T(8,128)S(1)} %fusion.11) | copy-start | bytes 12582916
  39.8 2.0 %copy-start.4 = (f32[8,128,1024]{2,1,0:T(8,128)}, f32[8,128,1024]{2,1,0:T(8,128)S(1)}, u32[]{:S(2)}) copy-start(f32[8,128,1024]{2,1,0:T(8,128)S(1)} %fusion.13) | copy-start | bytes 12582916
  39.8 3.3 %copy-start.10 = (f32[2,64,1024]{2,1,0:T(8,128)S(1)}, f32[2,64,1024]{2,1,0:T(8,128)}, u32[]{:S(2)}) copy-start(f32[2,64,1024]{2,1,0:T(8,128)} %param.17) | copy-start | bytes 1572868
  39.8 3.3 %copy-start.11 = (f32[2,64,1024]{2,1,0:T(8,128)S(1)}, f32[2,64,1024]{2,1,0:T(8,128)}, u32[]{:S(2)}) copy-start(f32[2,64,1024]{2,1,0:T(8,128)} %param.16) | copy-start | bytes 1572868
  39.8 10.4 %copy-start.1 = (s32[1,16]{1,0:T(1,128)S(1)}, s32[1,16]{1,0:T(1,128)}, u32[]{:S(2)}) copy-start(s32[1,16]{1,0:T(1,128)} %param.21) | copy-start | bytes 196
  41.8 9.1 %collective-permute-start.13 = (bf16[1,2,128,1024]{3,2,1,0:T(8,128)(2,1)S(1)}, bf16[1,2,128,1024]{3,2,1,0:T(8,128)(2,1)S(1)}, u32[]{:S(2)}, u32[]{:S(2)}) collective-permute-start(bf16[1,2,128,1024]{3,2,1,0:T(8,128)(2,1)S(1)} %fusion.45), channel_id=1, source_target_pairs={{0,4},{1,5},{2,6},{3,7},{16,20},{17,21},{18,22},{19,23}} | collective-permute-start | bytes 1572872 | tf_op jit(solution)/shard_map/ppermute | solution.py:50
  43.2 0.7 copy-start.6
  44.8 11.5 %collective-permute-start.6 = (bf16[2,2,64,1024]{3,2,1,0:T(8,128)(2,1)}, bf16[2,2,64,1024]{3,2,1,0:T(8,128)(2,1)}, u32[]{:S(2)}, u32[]{:S(2)}) collective-permute-start(bf16[2,2,64,1024]{3,2,1,0:T(8,128)(2,1)} %pad_maximum_fusion), channel_id=1, source_target_pairs={{0,16},{16,0},{1,17},{17,1},{2,18},{18,2},{3,19},{19,3},{4,20},{20... | collective-permute-start | bytes 1572872 | tf_op jit(solution)/shard_map/ppermute | solution.py:17
  51.9 2.4 %collective-permute-start.14 = (bf16[1,2,128,1024]{3,2,1,0:T(8,128)(2,1)}, bf16[1,2,128,1024]{3,2,1,0:T(8,128)(2,1)}, u32[]{:S(2)}, u32[]{:S(2)}) collective-permute-start(bf16[1,2,128,1024]{3,2,1,0:T(8,128)(2,1)} %fusion.33), channel_id=1, source_target_pairs={{4,8},{5,9},{6,10},{7,11},{20,24},{21,25},{22,26},{23,27}} | collective-permute-start | bytes 1572872 | tf_op jit(solution)/shard_map/ppermute | solution.py:50
  54.7 3.3 %collective-permute-start.15 = (bf16[1,2,128,1024]{3,2,1,0:T(8,128)(2,1)S(1)}, bf16[1,2,128,1024]{3,2,1,0:T(8,128)(2,1)S(1)}, u32[]{:S(2)}, u32[]{:S(2)}) collective-permute-start(bf16[1,2,128,1024]{3,2,1,0:T(8,128)(2,1)S(1)} %fusion.32), channel_id=1, source_target_pairs={{8,12},{9,13},{10,14},{11,15},{24,28},{25,29},{26,30},{27,31}} | collective-permute-start | bytes 1572872 | tf_op jit(solution)/shard_map/ppermute | solution.py:50
  57.5 2.2 %copy-start.5 = (f32[8,128,1024]{2,1,0:T(8,128)S(1)}, f32[8,128,1024]{2,1,0:T(8,128)}, u32[]{:S(2)}) copy-start(f32[8,128,1024]{2,1,0:T(8,128)} %copy-done.4) | copy-start | bytes 12582916
  57.7 3.3 %copy-start.3 = (f32[8,128,1024]{2,1,0:T(8,128)S(1)}, f32[8,128,1024]{2,1,0:T(8,128)}, u32[]{:S(2)}) copy-start(f32[8,128,1024]{2,1,0:T(8,128)} %copy-done.2) | copy-start | bytes 12582916
  61.0 6.4 %copy-start.12 = (f32[16,128]{1,0:T(8,128)S(1)}, f32[16,128]{1,0:T(8,128)}, u32[]{:S(2)}) copy-start(f32[16,128]{1,0:T(8,128)} %param.18) | copy-start | bytes 24580
  71.4 28.6 %all-to-all-start = ((bf16[16,2,4096]{2,1,0:T(2,128)(2,1)}), bf16[16,2,4096]{2,1,0:T(2,128)(2,1)S(1)}, u32[]{:S(2)}, u32[]{:S(2)}) async-start(bf16[16,2,4096]{2,1,0:T(2,128)(2,1)} %reshape.509), calls=%async_computation | async-start | bytes 524288 | tf_op jit(solution)/shard_map/all_to_all | solution.py:192
  85.2 12.8 %copy-start.7 = (bf16[1024,128]{1,0:T(8,128)(2,1)S(1)}, bf16[1024,128]{1,0:T(8,128)(2,1)}, u32[]{:S(2)}) copy-start(bf16[1024,128]{1,0:T(8,128)(2,1)} %param.13) | copy-start | bytes 786436
  85.2 12.8 %copy-start.9 = (bf16[1024,128]{0,1:T(8,128)(2,1)S(1)}, bf16[1024,128]{0,1:T(8,128)(2,1)}, u32[]{:S(2)}) copy-start(bf16[1024,128]{0,1:T(8,128)(2,1)} %copy-done.8) | copy-start | bytes 786436

commit v2 on v1

v2 whole, which is shorter than its diff:
```python
import functools

import jax
import jax.numpy as jnp
from jax import lax
from jax.experimental import pallas as pl
from jax.experimental.pallas import tpu as pltpu
from jax.sharding import PartitionSpec as P

TOUCH = 8
ADAPTER_SCALE = 4.0
BETA_ONE = 0.9
BETA_TWO = 0.999
EPSILON = 1e-08
VMEM_LIMIT = 48 * 2**20
BF16 = jnp.bfloat16
F32 = jnp.float32

ANY = pl.BlockSpec(memory_space=pl.ANY)
VMEM = pl.BlockSpec(memory_space=pltpu.VMEM)
SMEM = pl.BlockSpec(memory_space=pltpu.SMEM)


def dot_trailing(left, right):
    return lax.dot_general(left, right, (((1,), (1,)), ((), ())), preferred_element_type=F32)


def call(kernel, out_shape, in_specs, out_specs, scratch, flops, nbytes, name, aliases=None):
    return pl.pallas_call(
        kernel,
        out_shape=out_shape,
        in_specs=in_specs,
        out_specs=out_specs,
        scratch_shapes=scratch,
        input_output_aliases=aliases or {},
        compiler_params=pltpu.CompilerParams(vmem_limit_bytes=VMEM_LIMIT),
        cost_estimate=pl.CostEstimate(flops=flops, bytes_accessed=nbytes, transcendentals=0),
        name=name,
    )


def pieces_kernel(along_rows, source, weight, *rest):
    *outs, buf, sem = rest
    size = len(outs)
    place = lax.axis_index("tensor")
    rows, width = buf.shape[1:]
    first = 0 if source.shape[1] == width else pl.multiple_of(place * width, width)

    def copy(k):
        block = pl.multiple_of(lax.rem(place + k, size) * rows, rows)
        return pltpu.make_async_copy(
            source.at[pl.ds(block, rows), pl.ds(first, width)], buf.at[k], sem.at[k]
        )

    order = list(range(1, size)) + [0]
    for k in order:
        copy(k).start()
    for k in order:
        copy(k).wait()
        if along_rows:
            outs[k][...] = jnp.dot(buf[k], weight[...], preferred_element_type=F32).T.astype(BF16)
        else:
            outs[k][...] = dot_trailing(weight[...], buf[k]).astype(BF16)


def rank_pieces(source, weight, along_rows, size, width, name):
    tokens = source.shape[0]
    rank = weight.shape[1] if along_rows else weight.shape[0]
    rows = tokens // size
    return call(
        functools.partial(pieces_kernel, along_rows),
        [jax.ShapeDtypeStruct((rank, rows), BF16)] * size,
        [ANY, VMEM],
        [VMEM] * size,
        [pltpu.VMEM((size, rows, width), BF16), pltpu.SemaphoreType.DMA((size,))],
        2 * tokens * width * rank,
        2 * tokens * width,
        name,
    )(source, weight)


def shifted(value, axis, shift):
    size = lax.axis_size(axis)
    return lax.ppermute(value, axis, [(i, (i + shift) % size) for i in range(size)])


def scatter_sum(pieces):
    arrived = [shifted(piece, "tensor", k) for k, piece in enumerate(pieces) if k]
    total = pieces[0].astype(F32)
    for term in arrived:
        total = total + term.astype(F32)
    return total.astype(BF16)


def gather_pieces(total):
    size = lax.axis_size("tensor")
    return [total] + [shifted(total, "tensor", k) for k in range(1, size)]


def example_scalars(bounds, block):
    low = lax.axis_index("seq") * block
    count = bounds.shape[2]
    first = jnp.int32(-1)
    last = jnp.int32(-1)
    for e in range(count):
        start = bounds[0, 0, e]
        first = first + (start <= low).astype(jnp.int32)
        last = last + (start <= low + block - 1).astype(jnp.int32)
    return low, first, last


def place_pieces(pieces, low_scratch):
    size = len(pieces)
    place = lax.axis_index("tensor")
    for k, piece in enumerate(pieces):
        low_scratch[lax.rem(place + size - k, size)] = piece[...]


def masked(low_piece, offset, start, end):
    tokens = offset + lax.broadcasted_iota(jnp.int32, low_piece.shape, 1)
    return jnp.where((tokens >= start) & (tokens < end), low_piece.astype(F32), 0.0).astype(BF16)


def column_copies(source, buf, sem):
    tiles, tokens, columns = buf.shape
    width = tiles * columns
    first = 0 if source.shape[1] == width else lax.axis_index("tensor") * width
    return [
        pltpu.make_async_copy(
            source.at[:, pl.ds(pl.multiple_of(first + t * columns, columns), columns)],
            buf.at[t],
            sem.at[t],
        )
        for t in range(tiles)
    ]


def tail_kernel(size, bounds, source, *rest):
    pieces = rest[:size]
    out, buf, low_scratch, left, sem = rest[size:]
    copies = column_copies(source, buf, sem)
    for c in copies:
        c.start()
    tokens, columns = buf.shape[1:]
    rows = tokens // size
    low, _, last = example_scalars(bounds, tokens)
    start, end = bounds[0, 0, last], bounds[0, 1, last]
    place_pieces(pieces, low_scratch)
    for c in range(size):
        left[:, c * rows : (c + 1) * rows] = masked(low_scratch[c], low + c * rows, start, end)
    for t, c in enumerate(copies):
        c.wait()
        part = jnp.dot(left[...], buf[t], preferred_element_type=F32)
        out[:, t * columns : (t + 1) * columns] = (ADAPTER_SCALE * part).astype(BF16)


def tail_part(bounds, source, pieces, width, name):
    size = len(pieces)
    rank, rows = pieces[0].shape
    tokens = source.shape[0]
    tiles = width // 256
    return call(
        functools.partial(tail_kernel, size),
        jax.ShapeDtypeStruct((rank, width), BF16),
        [SMEM, ANY] + [VMEM] * size,
        VMEM,
        [
            pltpu.VMEM((tiles, tokens, width // tiles), BF16),
            pltpu.VMEM((size, rank, rows), BF16),
            pltpu.VMEM((rank, tokens), BF16),
            pltpu.SemaphoreType.DMA((tiles,)),
        ],
        2 * tokens * width * rank,
        2 * tokens * width,
        name,
    )(bounds, source, *pieces)


def normalize(grads, first_moment, second_moment):
    first = BETA_ONE * first_moment + (1.0 - BETA_ONE) * grads
    second = BETA_TWO * second_moment + ((1.0 - BETA_TWO) * grads) * grads
    guess = lax.rsqrt(second)
    below = second * guess + EPSILON
    return first * (guess * (2.0 - below * guess))


def split_two(value):
    high = value.astype(BF16)
    return high, (value - high.astype(F32)).astype(BF16)


def rank_side_blocks(rank_side, blocks):
    high, low = split_two(rank_side[...])
    rows, rank = high.shape
    blocks[...] = jnp.zeros_like(blocks)
    for i, term in enumerate((high, low)):
        for m in range(2):
            at = (2 * i + m) * rows
            blocks[at : at + rows, m * rank : (m + 1) * rank] = term


def project_rank(blocks, normed):
    both = jnp.dot(blocks[...], normed[...], preferred_element_type=F32)
    half = both.shape[0] // 2
    return both[:half] + both[half:]


def project_width(value, right):
    high, low = split_two(value)
    return jnp.dot(high, right, preferred_element_type=F32) + jnp.dot(
        low, right, preferred_element_type=F32
    )


def slot_end(bounds, index):
    return bounds[0, 1, jnp.minimum(index, bounds.shape[2] - 1)]


def slots_kernel(size, bounds, owner, source_grad, source_in, moments, rank_side, width_side, *rest):
    pieces_grad, pieces_in = rest[:size], rest[size : 2 * size]
    out, head, buf, low_scratch, left, parts, normed, blocks, ranked, wide, right, sem, right_sem = rest[
        2 * size :
    ]
    copies = [column_copies(s, buf.at[m], sem.at[m]) for m, s in enumerate((source_grad, source_in))]
    rows_here = right.shape[0]
    right_copy = pltpu.make_async_copy(
        width_side.at[
            pl.ds(pl.multiple_of(lax.axis_index("tensor") * rows_here, rows_here), rows_here)
        ],
        right,
        right_sem,
    )
    for m in range(2):
        for c in copies[m]:
            c.start()
    right_copy.start()
    tokens, columns = buf.shape[2:]
    rank = head.shape[1]
    rows = tokens // size
    low, first, last = example_scalars(bounds, tokens)
    count = bounds.shape[2]
    rank_side_blocks(rank_side, blocks)
    for m, pieces in enumerate((pieces_grad, pieces_in)):
        place_pieces(pieces, low_scratch.at[m])
        for j in range(TOUCH):
            index = jnp.minimum(first + j, count - 1)
            used = first + j <= last
            start = jnp.where(used, bounds[0, 0, index], 0)
            end = jnp.where(used, bounds[0, 1, index], 0)
            for c in range(size):
                left[m, j * rank : (j + 1) * rank, c * rows : (c + 1) * rows] = masked(
                    low_scratch[m, c], low + c * rows, start, end
                )
        for t, c in enumerate(copies[m]):
            c.wait()
            part = jnp.dot(left[m], buf[m, t], preferred_element_type=F32)
            parts[:, m, :, t * columns : (t + 1) * columns] = (
                (ADAPTER_SCALE * part).astype(BF16).reshape(TOUCH, rank, columns)
            )
        head[m] = parts[0, m]

    def ends_here(j):
        return (first + j <= last) & (slot_end(bounds, first + j) <= low + tokens)

    step = 16

    @pl.loop(1, TOUCH)
    def _(j):
        @pl.when(ends_here(j))
        def _():
            for m in range(2):
                for r in range(0, rank, step):
                    grads = parts[j, m, r : r + step, :].astype(F32)
                    normed[m * rank + r : m * rank + r + step, :] = normalize(
                        grads,
                        moments[0, m, r : r + step, :].astype(F32),
                        moments[1, m, r : r + step, :].astype(F32),
                    ).astype(BF16)
            ranked[j] = project_rank(blocks, normed)

    right_copy.wait()
    width = ranked.shape[2]
    wide[...] = project_width(ranked[...].reshape(-1, width), right[...]).reshape(wide.shape)
    out[...] = jnp.zeros_like(out)
    for j in range(1, TOUCH):

        @pl.when(ends_here(j))
        def _():
            out[owner[0, jnp.minimum(first + j, count - 1)]] = wide[j].astype(BF16)


def slot_features(
    bounds, owner, source_grad, source_in, moments, rank_side, width_side, pieces_grad, pieces_in
):
    size = len(pieces_in)
    rank, rows = pieces_in[0].shape
    tokens, width = source_grad.shape
    tiles = width // 256
    lines = rank_side.shape[0]
    columns = width_side.shape[1]
    return call(
        functools.partial(slots_kernel, size),
        [
            jax.ShapeDtypeStruct((owner.shape[1], 2 * lines, columns), BF16),
            jax.ShapeDtypeStruct((2, rank, width), BF16),
        ],
        [SMEM, SMEM, ANY, ANY, VMEM, VMEM, ANY] + [VMEM] * (2 * size),
        [VMEM, VMEM],
        [
            pltpu.VMEM((2, tiles, tokens, width // tiles), BF16),
            pltpu.VMEM((2, size, rank, rows), BF16),
            pltpu.VMEM((2, TOUCH * rank, tokens), BF16),
            pltpu.VMEM((TOUCH, 2, rank, width), BF16),
            pltpu.VMEM((2 * rank, width), BF16),
            pltpu.VMEM((4 * lines, 2 * rank), BF16),
            pltpu.VMEM((TOUCH, 2 * lines, width), F32),
            pltpu.VMEM((TOUCH, 2 * lines, columns), F32),
            pltpu.VMEM((width, columns), BF16),
            pltpu.SemaphoreType.DMA((2, tiles)),
            pltpu.SemaphoreType.DMA,
        ],
        4 * tokens * width * rank * TOUCH,
        4 * tokens * width,
        "slot_features",
    )(
        bounds,
        owner,
        source_grad,
        source_in,
        moments,
        rank_side,
        width_side,
        *pieces_grad,
        *pieces_in,
    )


def head_kernel(hops, block, bounds, owner, filled, head, moments, rank_side, width_side, *rest):
    arrived = rest[: 2 * hops]
    out, normed, blocks, right, right_sem = rest[2 * hops :]
    rows_here = right.shape[0]
    right_copy = pltpu.make_async_copy(
        width_side.at[
            pl.ds(pl.multiple_of(lax.axis_index("tensor") * rows_here, rows_here), rows_here)
        ],
        right,
        right_sem,
    )
    right_copy.start()
    low, first, last = example_scalars(bounds, block)
    rank = head.shape[1]
    continued = (bounds[0, 0, first] < low).astype(F32)
    rank_side_blocks(rank_side, blocks)
    step = 16
    for m in range(2):
        for r in range(0, rank, step):
            incoming = arrived[m * hops][r : r + step, :].astype(F32)
            for k in range(1, hops):
                incoming = incoming + arrived[m * hops + k][r : r + step, :].astype(F32)
            grads = head[m, r : r + step, :].astype(F32) + continued * incoming
            normed[m * rank + r : m * rank + r + step, :] = normalize(
                grads,
                moments[0, m, r : r + step, :].astype(F32),
                moments[1, m, r : r + step, :].astype(F32),
            ).astype(BF16)
    out[...] = filled[...]
    ranked = project_rank(blocks, normed)
    right_copy.wait()
    wide = project_width(ranked, right[...])

    @pl.when(slot_end(bounds, first) <= low + block)
    def _():
        out[owner[0, first]] = wide.astype(BF16)


def head_features(bounds, owner, filled, head, moments, rank_side, width_side, arrived, block):
    hops = len(arrived[0])
    rank, width = head.shape[1:]
    lines = rank_side.shape[0]
    columns = width_side.shape[1]
    return call(
        functools.partial(head_kernel, hops, block),
        jax.ShapeDtypeStruct(filled.shape, BF16),
        [SMEM, SMEM, VMEM, VMEM, VMEM, VMEM, ANY] + [VMEM] * (2 * hops),
        VMEM,
        [
            pltpu.VMEM((2 * rank, width), BF16),
            pltpu.VMEM((4 * lines, 2 * rank), BF16),
            pltpu.VMEM((width, columns), BF16),
            pltpu.SemaphoreType.DMA,
        ],
        2 * width * 2 * rank * 4 * lines,
        8 * rank * width,
        "head_features",
    )(bounds, owner, filled, head, moments, rank_side, width_side, *arrived[0], *arrived[1])


def first_kernel(steps, rows_ref, weight, out):
    k = pl.program_id(0)
    term = dot_trailing(rows_ref[...], weight[...])

    @pl.when(k == 0)
    def _():
        out[...] = term

    @pl.when(k > 0)
    def _():
        out[...] += term


def second_kernel(steps, split, size, rows_ref, weight, down, done, *rest):
    pieces, out, acc, low_scratch = rest[:size], rest[size], rest[size + 1], rest[size + 2]
    k = pl.program_id(0)
    term = dot_trailing(rows_ref[...], weight[...])

    @pl.when(k == 0)
    def _():
        acc[...] = term

    @pl.when((k > 0) & (k < steps - 1))
    def _():
        acc[...] += term

    @pl.when(k == steps - 1)
    def _():
        place_pieces(pieces, low_scratch)
        rows = out.shape[0] // size
        for c in range(size):
            here = slice(c * rows, (c + 1) * rows)
            extra = ADAPTER_SCALE * dot_trailing(low_scratch[c].astype(F32).T.astype(BF16), down[...])
            out[here, :split] = (done[here, :] + extra[:, :split]).astype(BF16)
            out[here, split:] = (acc[here, :] + term[here, :] + extra[:, split:]).astype(BF16)


def first_product(rows, weight, split, tile):
    tokens, depth = rows.shape
    steps = depth // tile
    return pl.pallas_call(
        functools.partial(first_kernel, steps),
        out_shape=jax.ShapeDtypeStruct((tokens, split), F32),
        grid=(steps,),
        in_specs=[
            pl.BlockSpec((tokens, tile), lambda k: (0, k)),
            pl.BlockSpec((split, tile), lambda k: (0, k)),
        ],
        out_specs=pl.BlockSpec((tokens, split), lambda k: (0, 0)),
        compiler_params=pltpu.CompilerParams(vmem_limit_bytes=VMEM_LIMIT),
        cost_estimate=pl.CostEstimate(
            flops=2 * tokens * depth * split,
            bytes_accessed=2 * depth * (tokens + split),
            transcendentals=0,
        ),
        name="first_product",
    )(rows, weight)


def second_product(rows, weight, down, done, pieces, tile):
    tokens, depth = rows.shape
    width, rank = down.shape
    split = done.shape[1]
    rest = width - split
    steps = depth // tile
    size = len(pieces)
    whole = lambda k: (0, 0)
    return pl.pallas_call(
        functools.partial(second_kernel, steps, split, size),
        out_shape=jax.ShapeDtypeStruct((tokens, width), BF16),
        grid=(steps,),
        in_specs=[
            pl.BlockSpec((tokens, tile), lambda k: (0, k)),
            pl.BlockSpec((rest, tile), lambda k: (split // rest, k)),
            pl.BlockSpec((width, rank), whole),
            pl.BlockSpec((tokens, split), whole),
        ]
        + [pl.BlockSpec(pieces[0].shape, whole)] * size,
        out_specs=pl.BlockSpec((tokens, width), whole),
        scratch_shapes=[
            pltpu.VMEM((tokens, rest), F32),
            pltpu.VMEM((size,) + pieces[0].shape, BF16),
        ],
        compiler_params=pltpu.CompilerParams(vmem_limit_bytes=VMEM_LIMIT),
        cost_estimate=pl.CostEstimate(
            flops=2 * tokens * depth * rest,
            bytes_accessed=2 * depth * (tokens + rest),
            transcendentals=0,
        ),
        name="second_product",
    )(rows, weight, down, done, *pieces)


def carry_chain(tail, keep):
    arrived = []
    outgoing = tail
    for k in range(lax.axis_size("seq") - 1):
        arrived.append(lax.ppermute(outgoing, "seq", [(k, k + 1)]))
        outgoing = (tail.astype(F32) + keep * arrived[-1].astype(F32)).astype(BF16)
    return arrived


def gather_rows(value, axis, dim):
    size = lax.axis_size(axis)
    if size != 2:
        return lax.all_gather(value, axis, axis=dim, tiled=True)
    other = shifted(value, axis, 1)
    low = lax.axis_index(axis) == 0
    return jnp.concatenate([jnp.where(low, value, other), jnp.where(low, other, value)], axis=dim)


def per_device(
    attention_output_rows,
    projection_result_gradient,
    adapter_down_weight,
    adapter_up_weight,
    output_projection_weight,
    adam_first_moments,
    adam_second_moments,
    rank_side_projection,
    width_side_projection,
    bounds,
    example_owner_slot,
):
    packs, blk, width_local = attention_output_rows.shape
    assert packs == 1
    width = projection_result_gradient.shape[2]
    size = lax.axis_size("tensor")
    rows_in = attention_output_rows.reshape(blk, width_local)
    rows_grad = projection_result_gradient.reshape(blk, width)

    partial_in = rank_pieces(rows_in, adapter_down_weight, True, size, width_local, "pieces_in")
    partial_grad = rank_pieces(rows_grad, adapter_up_weight, False, size, width_local, "pieces_grad")
    low_in = gather_pieces(scatter_sum(partial_in))
    low_grad = gather_pieces(scatter_sum(partial_grad))
    stacked = jnp.stack([adam_first_moments, adam_second_moments]).astype(BF16)
    moments = gather_rows(stacked, "dp", 2)
    done = first_product(rows_grad, output_projection_weight, width_local // 2, 1024)

    low = lax.axis_index("seq") * blk
    starts, ends = bounds[0, 0], bounds[0, 1]
    spans = jnp.any((starts < low) & (ends >= low + blk)).astype(F32)

    tail_in = tail_part(bounds, rows_grad, low_in, width_local, "tail_in")
    tail_grad = tail_part(bounds, rows_in, low_grad, width_local, "tail_grad")
    arrived_in = carry_chain(tail_in, spans)
    arrived_grad = carry_chain(tail_grad, spans)
    filled, head = slot_features(
        bounds,
        example_owner_slot,
        rows_in,
        rows_grad,
        moments,
        rank_side_projection,
        width_side_projection,
        low_grad,
        low_in,
    )
    buffer = head_features(
        bounds,
        example_owner_slot,
        filled,
        head,
        moments,
        rank_side_projection,
        width_side_projection,
        (arrived_grad, arrived_in),
        blk,
    )
    arrived = lax.all_to_all(buffer, ("seq", "tensor"), split_axis=0, concat_axis=0, tiled=True)
    features = jnp.sum(arrived.astype(F32), axis=0).reshape(1, 1, -1)
    out = second_product(
        rows_grad, output_projection_weight, adapter_down_weight, done, low_grad, 1024
    )
    return (out.reshape(attention_output_rows.shape), features)


def solution(mesh):
    return jax.shard_map(
        per_device,
        mesh=mesh,
        in_specs=(
            P("dp", "seq", "tensor"),
            P("dp", "seq", None),
            P("tensor", None),
            P(None, "tensor"),
            P("tensor", None),
            P(None, "dp", "tensor"),
            P(None, "dp", "tensor"),
            P(),
            P(),
            P("dp", None, None),
            P("dp", None),
        ),
        out_specs=(P("dp", "seq", "tensor"), P("dp", ("seq", "tensor"), None)),
        check_vma=False,
    )
```

time: 102 us -> 97.7 us (0.958); the launches traced: 102 us -> 96.2 us
  Pallas kernels: 0 us -> 46.4 us
  matrix products: 33.2 us -> 0 us
  other arithmetic: 9.94 us -> 3.34 us
  local copies, waits for them, and re-layouts: 9.59 us -> 4.48 us
  starting transfers between devices: 37.4 us -> 32.6 us
  between operations: 4.68 us -> 1.68 us
    pallas_call x0 -> x8, Pallas kernels: none -> 46.4 us  [the longest x1 16 us: slot_features(): call(functools.partial(slots_kernel, size), [jax.ShapeDtypeStruct((owner....]
    dot_general x9 -> x0, matrix products: 33.2 us -> none  [the longest x3 17.2 us: contract_trailing(): lax.dot_general(left, right, (((1,), (1,)), ((), ())), preferred_element_...]
    all_to_all x1, starting transfers between devices: 13.8 us -> 7.64 us  [per_device(): lax.all_to_all(buffer, ('seq', 'tensor'), split_axis=0, concat_axis=0, ti...]
    unnamed x31 -> x34, local copies, waits for them, and re-layouts: 6.81 us -> 3.83 us
    reduce_sum x4 -> x1, other arithmetic: 2.83 us -> 0.04 us  [per_device(): features = jnp.sum(arrived.astype(F32), axis=0).reshape(1, 1, -1)]
    ppermute x3 -> x6, starting transfers between devices: 3.64 us -> 5.62 us  [carry_chain(): arrived.append(lax.ppermute(outgoing, 'seq', [(k, k + 1)]))]
    select_n x2 -> x0, other arithmetic: 1.36 us -> none  [per_device(): target = jnp.take(owner_row, flat_example.reshape(-1))]
    convert_element_type x8 -> x6, other arithmetic: 1.77 us -> 0.41 us  [the longest x4 0.34 us: carry_chain(): outgoing = (tail.astype(F32) + keep * arrived[-1].astype(F32)).astype(BF16)]
  transfers between devices with their start and end apart: 17 -> 20, of which waited for: 4 -> 4; matrix products, arithmetic and copies ran while one was open for 26% -> 3% of each run, Pallas kernels for 0% -> 44%
where the time goes in v2:
time: 97.7 us; the launch traced here: 96.2 us
  Pallas kernels  46.4 us (47%)
  starting transfers between devices  32.6 us (33%)
  waiting for transfers between devices  7.59 us (8%)
  local copies, waits for them, and re-layouts  4.48 us (5%)
  other arithmetic  3.34 us (3%)
  between operations  1.68 us (2%)
    ppermute x13, starting transfers between devices, shifted(): lax.ppermute(value, axis, [(i, (i + shift) % size) for i in range(size)])  19.4 us
    pallas_call x1, Pallas kernels, slot_features(): call(functools.partial(slots_kernel, size), [jax.ShapeDtypeStruct((owner....  16 us
    pallas_call x1, Pallas kernels, second_product(): pl.pallas_call(functools.partial(second_kernel, steps, split, size), out_...  10.1 us
    pallas_call x1, Pallas kernels, first_product(): pl.pallas_call(functools.partial(first_kernel, steps), out_shape=jax.Shap...  8.25 us
    all_to_all x1, starting transfers between devices, per_device(): lax.all_to_all(buffer, ('seq', 'tensor'), split_axis=0, concat_axis=0, ti...  7.64 us
    ppermute x13, waiting for transfers between devices, shifted(): lax.ppermute(value, axis, [(i, (i + shift) % size) for i in range(size)])  7.57 us
    ppermute x6, starting transfers between devices, carry_chain(): arrived.append(lax.ppermute(outgoing, 'seq', [(k, k + 1)]))  5.62 us
    pallas_call x2, Pallas kernels, tail_part(): call(functools.partial(tail_kernel, size), jax.ShapeDtypeStruct((rank, wi...  4.86 us
  transfers between devices with their start and end apart: 20, of which 4 were waited for; matrix products, arithmetic and copies ran while one was open for 3% of the time, Pallas kernels for 44%

profile of v2, /device:TPU:0, one launch (start us, length us, event | category | flops | bytes accessed | tf_op | source)
XLA Modules:
  0.0 96.2 jit_solution(9891096861338650919)
XLA Ops:
  0.6 1.6 %copy-done = bf16[1,1024,1024]{2,1,0:T(8,128)(2,1)S(1)} copy-done((bf16[1,1024,1024]{2,1,0:T(8,128)(2,1)S(1)}, bf16[1,1024,1024]{2,1,0:T(8,128)(2,1)}, u32[]{:S(2)}) %copy-start) | copy-done | bytes 2097176
  2.2 0.9 copy-done.3
  3.2 1.6 %pieces_in.1 = (bf16[128,256]{1,0:T(8,128)(2,1)S(1)}, bf16[128,256]{1,0:T(8,128)(2,1)S(1)}, bf16[128,256]{1,0:T(8,128)(2,1)S(1)}, bf16[128,256]{1,0:T(8,128)(2,1)S(1)}) custom-call(bf16[1024,1024]{1,0:T(8,128)(2,1)S(1)} %bitcast.7, bf16[1024,128]{1,0:T(8,128)(2,1)S(1)} %copy-done.3), custom_call_target="tpu_custom_call" | custom-call | flops 268435456 | bytes 2097152 | tf_op jit(solution)/shard_map/pieces_in/pallas_call | solution.py:70
  4.8 3.1 %collective-permute-start.7 = (bf16[128,256]{1,0:T(8,128)(2,1)S(1)}, bf16[128,256]{1,0:T(8,128)(2,1)S(1)}, u32[]{:S(2)}, u32[]{:S(2)}) collective-permute-start(bf16[128,256]{1,0:T(8,128)(2,1)S(1)} %get-tuple-element.17), channel_id=1, source_target_pairs={{0,1},{1,2},{2,3},{3,0},{4,5},{5,6},{6,7},{7,4},{8,9},{9,10},{10,1... | collective-permute-start | bytes 196616 | tf_op jit(solution)/shard_map/ppermute | solution.py:84
  7.9 2.6 %collective-permute-start.8 = (bf16[128,256]{1,0:T(8,128)(2,1)S(1)}, bf16[128,256]{1,0:T(8,128)(2,1)S(1)}, u32[]{:S(2)}, u32[]{:S(2)}) collective-permute-start(bf16[128,256]{1,0:T(8,128)(2,1)S(1)} %get-tuple-element.18), channel_id=1, source_target_pairs={{0,2},{1,3},{2,0},{3,1},{4,6},{5,7},{6,4},{7,5},{8,10},{9,11},{10,... | collective-permute-start | bytes 196616 | tf_op jit(solution)/shard_map/ppermute | solution.py:84
  10.5 2.9 %pieces_grad.1 = (bf16[128,256]{1,0:T(8,128)(2,1)S(1)}, bf16[128,256]{1,0:T(8,128)(2,1)S(1)}, bf16[128,256]{1,0:T(8,128)(2,1)S(1)}, bf16[128,256]{1,0:T(8,128)(2,1)S(1)}) custom-call(bf16[1024,4096]{1,0:T(8,128)(2,1)} %bitcast.10, bf16[128,1024]{1,0:T(8,128)(2,1)S(1)} %copy-done.5), custom_call_target="tpu_custom_call" | custom-call | flops 268435456 | bytes 2097152 | tf_op jit(solution)/shard_map/pieces_grad/pallas_call | solution.py:70
  13.6 1.8 %collective-permute-start.1 = (bf16[128,256]{1,0:T(8,128)(2,1)S(1)}, bf16[128,256]{1,0:T(8,128)(2,1)S(1)}, u32[]{:S(2)}, u32[]{:S(2)}) collective-permute-start(bf16[128,256]{1,0:T(8,128)(2,1)S(1)} %get-tuple-element.14), channel_id=1, source_target_pairs={{0,2},{1,3},{2,0},{3,1},{4,6},{5,7},{6,4},{7,5},{8,10},{9,11},{10,... | collective-permute-start | bytes 196616 | tf_op jit(solution)/shard_map/ppermute | solution.py:84
  15.4 1.9 %collective-permute-start.2 = (bf16[128,256]{1,0:T(8,128)(2,1)S(1)}, bf16[128,256]{1,0:T(8,128)(2,1)S(1)}, u32[]{:S(2)}, u32[]{:S(2)}) collective-permute-start(bf16[128,256]{1,0:T(8,128)(2,1)S(1)} %get-tuple-element.15), channel_id=1, source_target_pairs={{0,3},{1,0},{2,1},{3,2},{4,7},{5,4},{6,5},{7,6},{8,11},{9,8},{10,9... | collective-permute-start | bytes 196616 | tf_op jit(solution)/shard_map/ppermute | solution.py:84
  17.4 2.6 %collective-permute-done = bf16[128,256]{1,0:T(8,128)(2,1)S(1)} collective-permute-done((bf16[128,256]{1,0:T(8,128)(2,1)S(1)}, bf16[128,256]{1,0:T(8,128)(2,1)S(1)}, u32[]{:S(2)}, u32[]{:S(2)}) %collective-permute-start) | collective-permute-done | bytes 65568 | tf_op jit(solution)/shard_map/ppermute | solution.py:84
  20.0 1.3 %collective-permute-done.1 = bf16[128,256]{1,0:T(8,128)(2,1)S(1)} collective-permute-done((bf16[128,256]{1,0:T(8,128)(2,1)S(1)}, bf16[128,256]{1,0:T(8,128)(2,1)S(1)}, u32[]{:S(2)}, u32[]{:S(2)}) %collective-permute-start.1) | collective-permute-done | bytes 65568 | tf_op jit(solution)/shard_map/ppermute | solution.py:84
  21.3 2.9 %collective-permute-start.5 = (bf16[128,256]{1,0:T(8,128)(2,1)S(1)}, bf16[128,256]{1,0:T(8,128)(2,1)S(1)}, u32[]{:S(2)}, u32[]{:S(2)}) collective-permute-start(bf16[128,256]{1,0:T(8,128)(2,1)S(1)} %add_convert_fusion.1.rest_0_), channel_id=1, source_target_pairs={{0,3},{1,0},{2,1},{3,2},{4,7},{5,4},{6,5},{7,6},{8,11},{9,8},{10,9... | collective-permute-start | bytes 196616 | tf_op jit(solution)/shard_map/ppermute | solution.py:84
  25.0 3.7 %collective-permute-start.12 = (bf16[128,256]{1,0:T(8,128)(2,1)S(1)}, bf16[128,256]{1,0:T(8,128)(2,1)S(1)}, u32[]{:S(2)}, u32[]{:S(2)}) collective-permute-start(bf16[128,256]{1,0:T(8,128)(2,1)S(1)} %add_convert_fusion.rest_4_.rest_0_), channel_id=1, source_target_pairs={{0,3},{1,0},{2,1},{3,2},{4,7},{5,4},{6,5},{7,6},{8,11},{9,8},{10,9... | collective-permute-start | bytes 196616 | tf_op jit(solution)/shard_map/ppermute | solution.py:84
  29.7 3.6 %collective-permute-done.4.rest_2_ = bf16[128,256]{1,0:T(8,128)(2,1)S(1)} collective-permute-done((bf16[128,256]{1,0:T(8,128)(2,1)S(1)}, bf16[128,256]{1,0:T(8,128)(2,1)S(1)}, u32[]{:S(2)}, u32[]{:S(2)}) %collective-permute-start.4) | collective-permute-done | bytes 65568 | tf_op jit(solution)/shard_map/ppermute | solution.py:84
  33.4 2.1 %tail_grad.1 = bf16[128,1024]{1,0:T(8,128)(2,1)S(1)} custom-call(s32[1,2,16]{2,1,0:T(2,128)S(1)} %copy-done.10, bf16[1024,1024]{1,0:T(8,128)(2,1)S(1)} %bitcast.8, bf16[128,256]{1,0:T(8,128)(2,1)S(1)} %add_convert_fusion.1.rest_0_, bf16[128,256]{1,0:T(8,128)(2,1)S(1)} %collective-permute-done.3.rest_1_, bf16[128,256]{1,0:T(8,128)(2,1)S(1)} %collective-permute-done.4.rest_2_, ...), custom_call_target="tpu_custom_call" | custom-call | flops 268435456 | bytes 2097152 | tf_op jit(solution)/shard_map/tail_grad/pallas_call | solution.py:162
  35.5 1.3 %collective-permute-start.13 = (bf16[128,1024]{1,0:T(8,128)(2,1)S(1)}, bf16[128,1024]{1,0:T(8,128)(2,1)S(1)}, u32[]{:S(2)}, u32[]{:S(2)}) collective-permute-start(bf16[128,1024]{1,0:T(8,128)(2,1)S(1)} %tail_grad.1), channel_id=1, source_target_pairs={{0,4},{1,5},{2,6},{3,7},{16,20},{17,21},{18,22},{19,23}} | collective-permute-start | bytes 786440 | tf_op jit(solution)/shard_map/ppermute | solution.py:495
  36.8 0.8 pad_maximum_fusion.1
  37.6 1.5 %collective-permute-start.6 = (bf16[2,2,64,1024]{3,2,1,0:T(8,128)(2,1)}, bf16[2,2,64,1024]{3,2,1,0:T(8,128)(2,1)}, u32[]{:S(2)}, u32[]{:S(2)}) collective-permute-start(bf16[2,2,64,1024]{3,2,1,0:T(8,128)(2,1)} %pad_maximum_fusion.1), channel_id=1, source_target_pairs={{0,16},{16,0},{1,17},{17,1},{2,18},{18,2},{3,19},{19,3},{4,20},{20... | collective-permute-start | bytes 1572872 | tf_op jit(solution)/shard_map/ppermute | solution.py:84
  39.2 2.8 %tail_in.1 = bf16[128,1024]{1,0:T(8,128)(2,1)S(1)} custom-call(s32[1,2,16]{2,1,0:T(2,128)S(1)} %copy-done.10, bf16[1024,4096]{1,0:T(8,128)(2,1)} %bitcast.11, bf16[128,256]{1,0:T(8,128)(2,1)S(1)} %add_convert_fusion.rest_4_.rest_0_, bf16[128,256]{1,0:T(8,128)(2,1)S(1)} %collective-permute-done.10.rest_5_.rest_1_, ...), custom_call_target="tpu_custom_call" | custom-call | flops 268435456 | bytes 2097152 | tf_op jit(solution)/shard_map/tail_in/pallas_call | solution.py:162
  42.6 0.6 copy-done.8
  43.2 1.3 %collective-permute-start.16 = (bf16[128,1024]{1,0:T(8,128)(2,1)S(1)}, bf16[128,1024]{1,0:T(8,128)(2,1)S(1)}, u32[]{:S(2)}, u32[]{:S(2)}) collective-permute-start(bf16[128,1024]{1,0:T(8,128)(2,1)S(1)} %tail_in.1), channel_id=1, source_target_pairs={{0,4},{1,5},{2,6},{3,7},{16,20},{17,21},{18,22},{19,23}} | collective-permute-start | bytes 786440 | tf_op jit(solution)/shard_map/ppermute | solution.py:495
  44.5 0.6 and_reduce_fusion
  45.9 0.7 collective-permute-start.14
  46.7 0.7 collective-permute-start.17
  47.4 1.3 %broadcast_select_fusion.1 = (bf16[2,2,64,1024]{3,2,1,0:T(8,128)(2,1)S(1)}, bf16[2,2,64,1024]{3,2,1,0:T(8,128)(2,1)S(1)}) fusion(bf16[2,2,64,1024]{3,2,1,0:T(8,128)(2,1)} %collective-permute-done.6, pred[]{:T(512)S(6)} %eq.3, bf16[1,2,64,1024]{3,2,1,0:T(8,128)(2,1)} %copy-done.13, bf16[1,2,64,1024]{3,2,1,0:T(8,128)(2,1)} %copy-done.14), kind=kLoop, calls=%fused_computation.12 | loop fusion | flops 786432 | bytes 2097153 | tf_op jit(solution)/shard_map/jit(_where)/select_n | solution.py:506
  48.9 0.7 collective-permute-start.15
  49.7 1.0 %collective-permute-start.18 = (bf16[128,1024]{1,0:T(8,128)(2,1)S(1)}, bf16[128,1024]{1,0:T(8,128)(2,1)S(1)}, u32[]{:S(2)}, u32[]{:S(2)}) collective-permute-start(bf16[128,1024]{1,0:T(8,128)(2,1)S(1)} %fusion.3), channel_id=1, source_target_pairs={{8,12},{9,13},{10,14},{11,15},{24,28},{25,29},{26,30},{27,31}} | collective-permute-start | bytes 786440 | tf_op jit(solution)/shard_map/ppermute | solution.py:495
  50.7 16.0 %slot_features.1 = (bf16[16,32,256]{2,1,0:T(8,128)(2,1)S(1)}, bf16[2,128,1024]{2,1,0:T(8,128)(2,1)S(1)}) custom-call(s32[1,2,16]{2,1,0:T(2,128)S(1)} %copy-done.10, s32[1,16]{1,0:T(1,128)S(1)} %copy-done.12, bf16[1024,1024]{1,0:T(8,128)(2,1)S(1)} %bitcast.9, bf16[1024,4096]{1,0:T(8,128)(2,1)} %bitcast.12, ...), custom_call_target="tpu_custom_call" | custom-call | flops 4294967296 | bytes 4194304 | tf_op jit(solution)/shard_map/slot_features/pallas_call | solution.py:301
  66.8 2.6 %head_features.1 = bf16[16,32,256]{2,1,0:T(8,128)(2,1)} custom-call(s32[1,2,16]{2,1,0:T(2,128)S(1)} %copy-done.10, s32[1,16]{1,0:T(1,128)S(1)} %copy-done.12, bf16[16,32,256]{2,1,0:T(8,128)(2,1)S(1)} %get-tuple-element.20.filled, bf16[2,128,1024]{2,1,0:T(8,128)(2,1)S(1)} %get-tuple-element.21.head, bf16[2,2,128,1024]{3,2,1,0:T(8,128)(2,1)S(1)} %pad_maximum_fusion.moments, ...), custom_call_target="tpu_custom_call" | custom-call | flops 33554432 | bytes 1048576 | tf_op jit(solution)/shard_map/head_features/pallas_call | solution.py:381
  69.4 7.6 %all-to-all-start = ((bf16[16,32,256]{2,1,0:T(8,128)(2,1)}), bf16[16,32,256]{2,1,0:T(8,128)(2,1)S(1)}, u32[]{:S(2)}, u32[]{:S(2)}) async-start(bf16[16,32,256]{2,1,0:T(8,128)(2,1)} %head_features.1), calls=%async_computation | async-start | bytes 524288 | tf_op jit(solution)/shard_map/all_to_all | solution.py:567
  77.1 8.2 %first_product.1.done = f32[1024,512]{1,0:T(8,128)S(1)} custom-call(bf16[1024,4096]{1,0:T(8,128)(2,1)} %bitcast.13, bf16[1024,4096]{1,0:T(8,128)(2,1)} %weight.6), custom_call_target="tpu_custom_call" | custom-call | flops 4294967296 | bytes 12582912 | tf_op jit(solution)/shard_map/first_product/pallas_call | solution.py:438
  85.3 10.1 %second_product.1 = bf16[1024,1024]{1,0:T(8,128)(2,1)} custom-call(bf16[1024,4096]{1,0:T(8,128)(2,1)} %bitcast.14, bf16[1024,4096]{1,0:T(8,128)(2,1)} %weight.6, bf16[1024,128]{1,0:T(8,128)(2,1)S(1)} %copy-done.4, f32[1024,512]{1,0:T(8,128)S(1)} %first_product.1.done, bf16[128,256]{1,0:T(8,128)(2,1)S(1)} %add_convert_fusion.1.rest_0_, ...), custom_call_target="tpu_custom_call" | custom-call | flops 4294967296 | bytes 12582912 | tf_op jit(solution)/shard_map/second_product/pallas_call | solution.py:465
  95.5 0.6 reshape.24
  (63 shorter events, 3.2 us)
Async XLA Ops:
  3.2 7.3 %copy-start.5 = (bf16[128,1024]{1,0:T(8,128)(2,1)S(1)}, bf16[128,1024]{1,0:T(8,128)(2,1)}, u32[]{:S(2)}) copy-start(bf16[128,1024]{1,0:T(8,128)(2,1)} %weight.5) | copy-start | bytes 786436
  4.8 20.0 %collective-permute-start.7 = (bf16[128,256]{1,0:T(8,128)(2,1)S(1)}, bf16[128,256]{1,0:T(8,128)(2,1)S(1)}, u32[]{:S(2)}, u32[]{:S(2)}) collective-permute-start(bf16[128,256]{1,0:T(8,128)(2,1)S(1)} %get-tuple-element.17), channel_id=1, source_target_pairs={{0,1},{1,2},{2,3},{3,0},{4,5},{5,6},{6,7},{7,4},{8,9},{9,10},{10,1... | collective-permute-start | bytes 196616 | tf_op jit(solution)/shard_map/ppermute | solution.py:84
  7.9 17.0 %collective-permute-start.8 = (bf16[128,256]{1,0:T(8,128)(2,1)S(1)}, bf16[128,256]{1,0:T(8,128)(2,1)S(1)}, u32[]{:S(2)}, u32[]{:S(2)}) collective-permute-start(bf16[128,256]{1,0:T(8,128)(2,1)S(1)} %get-tuple-element.18), channel_id=1, source_target_pairs={{0,2},{1,3},{2,0},{3,1},{4,6},{5,7},{6,4},{7,5},{8,10},{9,11},{10,... | collective-permute-start | bytes 196616 | tf_op jit(solution)/shard_map/ppermute | solution.py:84
  10.5 6.8 %copy-start.15 = (f32[2,64,1024]{2,1,0:T(8,128)S(1)}, f32[2,64,1024]{2,1,0:T(8,128)}, u32[]{:S(2)}) copy-start(f32[2,64,1024]{2,1,0:T(8,128)} %param.17) | copy-start | bytes 1572868
  10.5 6.8 %copy-start.16 = (f32[2,64,1024]{2,1,0:T(8,128)S(1)}, f32[2,64,1024]{2,1,0:T(8,128)}, u32[]{:S(2)}) copy-start(f32[2,64,1024]{2,1,0:T(8,128)} %param.16) | copy-start | bytes 1572868
  13.4 20.0 %copy-start.1 = (bf16[1,1024,1024]{2,1,0:T(8,128)(2,1)S(1)}, bf16[1,1024,1024]{2,1,0:T(8,128)(2,1)}, u32[]{:S(2)}) copy-start(bf16[1,1024,1024]{2,1,0:T(8,128)(2,1)} %param.11) | copy-start | bytes 6291460
  13.4 20.0 %copy-start.10 = (s32[1,2,16]{2,1,0:T(2,128)S(1)}, s32[1,2,16]{2,1,0:T(2,128)}, u32[]{:S(2)}) copy-start(s32[1,2,16]{2,1,0:T(2,128)} %bounds.7) | copy-start | bytes 388
  13.4 6.6 %collective-permute-start = (bf16[128,256]{1,0:T(8,128)(2,1)S(1)}, bf16[128,256]{1,0:T(8,128)(2,1)S(1)}, u32[]{:S(2)}, u32[]{:S(2)}) collective-permute-start(bf16[128,256]{1,0:T(8,128)(2,1)S(1)} %get-tuple-element.13), channel_id=1, source_target_pairs={{0,1},{1,2},{2,3},{3,0},{4,5},{5,6},{6,7},{7,4},{8,9},{9,10},{10,1... | collective-permute-start | bytes 196616 | tf_op jit(solution)/shard_map/ppermute | solution.py:84
  13.6 7.7 %collective-permute-start.1 = (bf16[128,256]{1,0:T(8,128)(2,1)S(1)}, bf16[128,256]{1,0:T(8,128)(2,1)S(1)}, u32[]{:S(2)}, u32[]{:S(2)}) collective-permute-start(bf16[128,256]{1,0:T(8,128)(2,1)S(1)} %get-tuple-element.14), channel_id=1, source_target_pairs={{0,2},{1,3},{2,0},{3,1},{4,6},{5,7},{6,4},{7,5},{8,10},{9,11},{10,... | collective-permute-start | bytes 196616 | tf_op jit(solution)/shard_map/ppermute | solution.py:84
  15.4 5.9 %collective-permute-start.2 = (bf16[128,256]{1,0:T(8,128)(2,1)S(1)}, bf16[128,256]{1,0:T(8,128)(2,1)S(1)}, u32[]{:S(2)}, u32[]{:S(2)}) collective-permute-start(bf16[128,256]{1,0:T(8,128)(2,1)S(1)} %get-tuple-element.15), channel_id=1, source_target_pairs={{0,3},{1,0},{2,1},{3,2},{4,7},{5,4},{6,5},{7,6},{8,11},{9,8},{10,9... | collective-permute-start | bytes 196616 | tf_op jit(solution)/shard_map/ppermute | solution.py:84
  17.4 20.3 %copy-start.13 = (bf16[1,2,64,1024]{3,2,1,0:T(8,128)(2,1)}, bf16[1,2,64,1024]{3,2,1,0:T(8,128)(2,1)S(1)}, u32[]{:S(2)}) copy-start(bf16[1,2,64,1024]{3,2,1,0:T(8,128)(2,1)S(1)} %get-tuple-element.24) | copy-start | bytes 786436
  17.4 20.2 %copy-start.14 = (bf16[1,2,64,1024]{3,2,1,0:T(8,128)(2,1)}, bf16[1,2,64,1024]{3,2,1,0:T(8,128)(2,1)S(1)}, u32[]{:S(2)}) copy-start(bf16[1,2,64,1024]{3,2,1,0:T(8,128)(2,1)S(1)} %get-tuple-element.25) | copy-start | bytes 786436
  20.0 5.0 %collective-permute-start.9 = (bf16[128,256]{1,0:T(8,128)(2,1)S(1)}, bf16[128,256]{1,0:T(8,128)(2,1)S(1)}, u32[]{:S(2)}, u32[]{:S(2)}) collective-permute-start(bf16[128,256]{1,0:T(8,128)(2,1)S(1)} %get-tuple-element.19), channel_id=1, source_target_pairs={{0,3},{1,0},{2,1},{3,2},{4,7},{5,4},{6,5},{7,6},{8,11},{9,8},{10,9... | collective-permute-start | bytes 196616 | tf_op jit(solution)/shard_map/ppermute | solution.py:84
  21.3 8.0 %collective-permute-start.5 = (bf16[128,256]{1,0:T(8,128)(2,1)S(1)}, bf16[128,256]{1,0:T(8,128)(2,1)S(1)}, u32[]{:S(2)}, u32[]{:S(2)}) collective-permute-start(bf16[128,256]{1,0:T(8,128)(2,1)S(1)} %add_convert_fusion.1.rest_0_), channel_id=1, source_target_pairs={{0,3},{1,0},{2,1},{3,2},{4,7},{5,4},{6,5},{7,6},{8,11},{9,8},{10,9... | collective-permute-start | bytes 196616 | tf_op jit(solution)/shard_map/ppermute | solution.py:84
  24.3 9.1 %collective-permute-start.4 = (bf16[128,256]{1,0:T(8,128)(2,1)S(1)}, bf16[128,256]{1,0:T(8,128)(2,1)S(1)}, u32[]{:S(2)}, u32[]{:S(2)}) collective-permute-start(bf16[128,256]{1,0:T(8,128)(2,1)S(1)} %add_convert_fusion.1.rest_0_), channel_id=1, source_target_pairs={{0,2},{1,3},{2,0},{3,1},{4,6},{5,7},{6,4},{7,5},{8,10},{9,11},{10,... | collective-permute-start | bytes 196616 | tf_op jit(solution)/shard_map/ppermute | solution.py:84
  24.8 8.6 %collective-permute-start.3 = (bf16[128,256]{1,0:T(8,128)(2,1)S(1)}, bf16[128,256]{1,0:T(8,128)(2,1)S(1)}, u32[]{:S(2)}, u32[]{:S(2)}) collective-permute-start(bf16[128,256]{1,0:T(8,128)(2,1)S(1)} %add_convert_fusion.1.rest_0_), channel_id=1, source_target_pairs={{0,1},{1,2},{2,3},{3,0},{4,5},{5,6},{6,7},{7,4},{8,9},{9,10},{10,1... | collective-permute-start | bytes 196616 | tf_op jit(solution)/shard_map/ppermute | solution.py:84
  25.0 14.2 %collective-permute-start.12 = (bf16[128,256]{1,0:T(8,128)(2,1)S(1)}, bf16[128,256]{1,0:T(8,128)(2,1)S(1)}, u32[]{:S(2)}, u32[]{:S(2)}) collective-permute-start(bf16[128,256]{1,0:T(8,128)(2,1)S(1)} %add_convert_fusion.rest_4_.rest_0_), channel_id=1, source_target_pairs={{0,3},{1,0},{2,1},{3,2},{4,7},{5,4},{6,5},{7,6},{8,11},{9,8},{10,9... | collective-permute-start | bytes 196616 | tf_op jit(solution)/shard_map/ppermute | solution.py:84
  28.7 10.4 %collective-permute-start.11 = (bf16[128,256]{1,0:T(8,128)(2,1)S(1)}, bf16[128,256]{1,0:T(8,128)(2,1)S(1)}, u32[]{:S(2)}, u32[]{:S(2)}) collective-permute-start(bf16[128,256]{1,0:T(8,128)(2,1)S(1)} %add_convert_fusion.rest_4_.rest_0_), channel_id=1, source_target_pairs={{0,2},{1,3},{2,0},{3,1},{4,6},{5,7},{6,4},{7,5},{8,10},{9,11},{10,... | collective-permute-start | bytes 196616 | tf_op jit(solution)/shard_map/ppermute | solution.py:84
  29.4 9.8 %collective-permute-start.10 = (bf16[128,256]{1,0:T(8,128)(2,1)S(1)}, bf16[128,256]{1,0:T(8,128)(2,1)S(1)}, u32[]{:S(2)}, u32[]{:S(2)}) collective-permute-start(bf16[128,256]{1,0:T(8,128)(2,1)S(1)} %add_convert_fusion.rest_4_.rest_0_), channel_id=1, source_target_pairs={{0,1},{1,2},{2,3},{3,0},{4,5},{5,6},{6,7},{7,4},{8,9},{9,10},{10,1... | collective-permute-start | bytes 196616 | tf_op jit(solution)/shard_map/ppermute | solution.py:84
  35.5 10.3 %collective-permute-start.13 = (bf16[128,1024]{1,0:T(8,128)(2,1)S(1)}, bf16[128,1024]{1,0:T(8,128)(2,1)S(1)}, u32[]{:S(2)}, u32[]{:S(2)}) collective-permute-start(bf16[128,1024]{1,0:T(8,128)(2,1)S(1)} %tail_grad.1), channel_id=1, source_target_pairs={{0,4},{1,5},{2,6},{3,7},{16,20},{17,21},{18,22},{19,23}} | collective-permute-start | bytes 786440 | tf_op jit(solution)/shard_map/ppermute | solution.py:495
  37.6 9.7 %collective-permute-start.6 = (bf16[2,2,64,1024]{3,2,1,0:T(8,128)(2,1)}, bf16[2,2,64,1024]{3,2,1,0:T(8,128)(2,1)}, u32[]{:S(2)}, u32[]{:S(2)}) collective-permute-start(bf16[2,2,64,1024]{3,2,1,0:T(8,128)(2,1)} %pad_maximum_fusion.1), channel_id=1, source_target_pairs={{0,16},{16,0},{1,17},{17,1},{2,18},{18,2},{3,19},{19,3},{4,20},{20... | collective-permute-start | bytes 1572872 | tf_op jit(solution)/shard_map/ppermute | solution.py:84
  43.2 3.4 %collective-permute-start.16 = (bf16[128,1024]{1,0:T(8,128)(2,1)S(1)}, bf16[128,1024]{1,0:T(8,128)(2,1)S(1)}, u32[]{:S(2)}, u32[]{:S(2)}) collective-permute-start(bf16[128,1024]{1,0:T(8,128)(2,1)S(1)} %tail_in.1), channel_id=1, source_target_pairs={{0,4},{1,5},{2,6},{3,7},{16,20},{17,21},{18,22},{19,23}} | collective-permute-start | bytes 786440 | tf_op jit(solution)/shard_map/ppermute | solution.py:495
  45.9 2.9 %collective-permute-start.14 = (bf16[128,1024]{1,0:T(8,128)(2,1)S(1)}, bf16[128,1024]{1,0:T(8,128)(2,1)S(1)}, u32[]{:S(2)}, u32[]{:S(2)}) collective-permute-start(bf16[128,1024]{1,0:T(8,128)(2,1)S(1)} %fusion), channel_id=1, source_target_pairs={{4,8},{5,9},{6,10},{7,11},{20,24},{21,25},{22,26},{23,27}} | collective-permute-start | bytes 786440 | tf_op jit(solution)/shard_map/ppermute | solution.py:495
  46.7 2.9 %collective-permute-start.17 = (bf16[128,1024]{1,0:T(8,128)(2,1)S(1)}, bf16[128,1024]{1,0:T(8,128)(2,1)S(1)}, u32[]{:S(2)}, u32[]{:S(2)}) collective-permute-start(bf16[128,1024]{1,0:T(8,128)(2,1)S(1)} %fusion.2), channel_id=1, source_target_pairs={{4,8},{5,9},{6,10},{7,11},{20,24},{21,25},{22,26},{23,27}} | collective-permute-start | bytes 786440 | tf_op jit(solution)/shard_map/ppermute | solution.py:495
  48.6 2.0 %copy-start.7 = (bf16[128,256]{1,0:T(8,128)(2,1)S(1)}, bf16[128,256]{1,0:T(8,128)(2,1)}, u32[]{:S(2)}) copy-start(bf16[128,256]{1,0:T(8,128)(2,1)} %copy-done.6) | copy-start | bytes 196612
  48.6 2.0 %copy-start.9 = (bf16[128,256]{1,0:T(8,128)(2,1)S(1)}, bf16[128,256]{1,0:T(8,128)(2,1)}, u32[]{:S(2)}) copy-start(bf16[128,256]{1,0:T(8,128)(2,1)} %copy-done.8) | copy-start | bytes 196612
  48.7 2.0 %copy-start.11 = (f32[16,128]{1,0:T(8,128)S(1)}, f32[16,128]{1,0:T(8,128)}, u32[]{:S(2)}) copy-start(f32[16,128]{1,0:T(8,128)} %rank_side.3) | copy-start | bytes 24580
  48.9 17.9 %collective-permute-start.15 = (bf16[128,1024]{1,0:T(8,128)(2,1)S(1)}, bf16[128,1024]{1,0:T(8,128)(2,1)S(1)}, u32[]{:S(2)}, u32[]{:S(2)}) collective-permute-start(bf16[128,1024]{1,0:T(8,128)(2,1)S(1)} %fusion.1), channel_id=1, source_target_pairs={{8,12},{9,13},{10,14},{11,15},{24,28},{25,29},{26,30},{27,31}} | collective-permute-start | bytes 786440 | tf_op jit(solution)/shard_map/ppermute | solution.py:495
  49.6 17.1 %copy-start.2 = (bf16[4096,256]{1,0:T(8,128)(2,1)S(1)}, bf16[4096,256]{1,0:T(8,128)(2,1)}, u32[]{:S(2)}) copy-start(bf16[4096,256]{1,0:T(8,128)(2,1)} %width_side.3) | copy-start | bytes 6291460
  49.7 17.1 %collective-permute-start.18 = (bf16[128,1024]{1,0:T(8,128)(2,1)S(1)}, bf16[128,1024]{1,0:T(8,128)(2,1)S(1)}, u32[]{:S(2)}, u32[]{:S(2)}) collective-permute-start(bf16[128,1024]{1,0:T(8,128)(2,1)S(1)} %fusion.3), channel_id=1, source_target_pairs={{8,12},{9,13},{10,14},{11,15},{24,28},{25,29},{26,30},{27,31}} | collective-permute-start | bytes 786440 | tf_op jit(solution)/shard_map/ppermute | solution.py:495
  69.4 26.1 %all-to-all-start = ((bf16[16,32,256]{2,1,0:T(8,128)(2,1)}), bf16[16,32,256]{2,1,0:T(8,128)(2,1)S(1)}, u32[]{:S(2)}, u32[]{:S(2)}) async-start(bf16[16,32,256]{2,1,0:T(8,128)(2,1)} %head_features.1), calls=%async_computation | async-start | bytes 524288 | tf_op jit(solution)/shard_map/all_to_all | solution.py:567
  77.1 8.3 %copy-start.4 = (bf16[1024,128]{1,0:T(8,128)(2,1)S(1)}, bf16[1024,128]{1,0:T(8,128)(2,1)}, u32[]{:S(2)}) copy-start(bf16[1024,128]{1,0:T(8,128)(2,1)} %weight.7) | copy-start | bytes 786436
  (5 other events, 5.8 us)

commit v3 on v0

v3 whole, which is shorter than its diff:
```python
import functools

import jax
import jax.numpy as jnp
from jax import lax
from jax.experimental import pallas as pl
from jax.experimental.pallas import tpu as pltpu
from jax.sharding import PartitionSpec as P

TOUCH = 8
ADAPTER_SCALE = 4.0
BETA_ONE = 0.9
BETA_TWO = 0.999
EPSILON = 1e-08
VMEM_LIMIT = 32 * 2**20
BF16 = jnp.bfloat16
F32 = jnp.float32

HBM = pl.BlockSpec(memory_space=pltpu.HBM)
VMEM = pl.BlockSpec(memory_space=pltpu.VMEM)
SMEM = pl.BlockSpec(memory_space=pltpu.SMEM)


def dot_trailing(left, right):
    return lax.dot_general(left, right, (((1,), (1,)), ((), ())), preferred_element_type=F32)


def call(kernel, out_shape, in_specs, out_specs, scratch, flops, nbytes, name, aliases=None):
    return pl.pallas_call(
        kernel,
        out_shape=out_shape,
        in_specs=in_specs,
        out_specs=out_specs,
        scratch_shapes=scratch,
        input_output_aliases=aliases or {},
        compiler_params=pltpu.CompilerParams(vmem_limit_bytes=VMEM_LIMIT),
        cost_estimate=pl.CostEstimate(flops=flops, bytes_accessed=nbytes, transcendentals=0),
        name=name,
    )


def pieces_kernel(along_rows, source, weight, *rest):
    *outs, columns, weight_buf, sem, weight_sem = rest
    size = len(outs)
    place = lax.axis_index("tensor")
    tokens, width = columns.shape
    rows = tokens // size
    first = 0 if source.shape[1] == width else pl.multiple_of(place * width, width)

    def rows_of(k):
        return pl.ds(pl.multiple_of(lax.rem(place + k, size) * rows, rows), rows)

    def copy(k):
        return pltpu.make_async_copy(
            source.at[rows_of(k), pl.ds(first, width)], columns.at[rows_of(k)], sem.at[k]
        )

    order = list(range(1, size)) + [0]
    weight_copy = pltpu.make_async_copy(weight, weight_buf, weight_sem)
    weight_copy.start()
    for k in order:
        copy(k).start()
    weight_copy.wait()
    for k in order:
        copy(k).wait()
        block = columns[rows_of(k), :]
        if along_rows:
            product = jnp.dot(block, weight_buf[...], preferred_element_type=F32)
        else:
            product = dot_trailing(block, weight_buf[...])
        outs[k][...] = product.T.astype(BF16)


def rank_pieces(source, weight, along_rows, size, width, name):
    tokens = source.shape[0]
    rank = weight.shape[1] if along_rows else weight.shape[0]
    rows = tokens // size
    *pieces, columns = call(
        functools.partial(pieces_kernel, along_rows),
        [jax.ShapeDtypeStruct((rank, rows), BF16)] * size
        + [jax.ShapeDtypeStruct((tokens, width), BF16)],
        [HBM, HBM],
        [VMEM] * (size + 1),
        [
            pltpu.VMEM(weight.shape, BF16),
            pltpu.SemaphoreType.DMA((size,)),
            pltpu.SemaphoreType.DMA,
        ],
        2 * tokens * width * rank,
        2 * tokens * width,
        name,
    )(source, weight)
    return pieces, columns


def shifted(value, axis, shift):
    size = lax.axis_size(axis)
    return lax.ppermute(value, axis, [(i, (i + shift) % size) for i in range(size)])


def scatter(pieces):
    return [shifted(piece, "tensor", k) if k else piece for k, piece in enumerate(pieces)]


def total_of(terms):
    total = terms[0].astype(F32)
    for term in terms[1:]:
        total = total + term.astype(F32)
    return total.astype(BF16)


def gather_pieces(total):
    size = lax.axis_size("tensor")
    return [total] + [shifted(total, "tensor", k) for k in range(1, size)]


def example_scalars(bounds, block):
    low = lax.axis_index("seq") * block
    count = bounds.shape[2]
    first = jnp.int32(-1)
    last = jnp.int32(-1)
    for e in range(count):
        start = bounds[0, 0, e]
        first = first + (start <= low).astype(jnp.int32)
        last = last + (start <= low + block - 1).astype(jnp.int32)
    return low, first, last


def place_pieces(pieces, low_scratch):
    size = len(pieces)
    place = lax.axis_index("tensor")
    for k, piece in enumerate(pieces):
        low_scratch[lax.rem(place + size - k, size)] = piece[...]


def masked(low_piece, offset, start, end):
    tokens = offset + lax.broadcasted_iota(jnp.int32, low_piece.shape, 1)
    return jnp.where((tokens >= start) & (tokens < end), low_piece.astype(F32), 0.0).astype(BF16)


def tails_kernel(size, bounds, rows_in, rows_grad, *rest):
    pieces = rest[: 2 * size]
    out, low_scratch, acc = rest[2 * size :]
    tokens, width = rows_in.shape
    rows = tokens // size
    low, _, last = example_scalars(bounds, tokens)
    start = bounds[0, 0, last]
    for m, source in enumerate((rows_in, rows_grad)):
        place_pieces(pieces[m * size : (m + 1) * size], low_scratch)

        def chunk(c):
            left = masked(low_scratch[c], low + c * rows, start, low + tokens)
            return jnp.dot(left, source[c * rows : (c + 1) * rows, :], preferred_element_type=F32)

        acc[...] = chunk(size - 1)
        for c in range(size - 1):

            @pl.when(start < low + (c + 1) * rows)
            def _():
                acc[...] += chunk(c)

        out[m] = (ADAPTER_SCALE * acc[...]).astype(BF16)


def tail_parts(bounds, rows_in, rows_grad, low_grad, low_in):
    size = len(low_in)
    rank, rows = low_in[0].shape
    tokens, width = rows_in.shape
    return call(
        functools.partial(tails_kernel, size),
        jax.ShapeDtypeStruct((2, rank, width), BF16),
        [SMEM] + [VMEM] * (2 + 2 * size),
        VMEM,
        [pltpu.VMEM((size, rank, rows), BF16), pltpu.VMEM((rank, width), F32)],
        4 * tokens * width * rank,
        4 * tokens * width,
        "tail_parts",
    )(bounds, rows_in, rows_grad, *low_grad, *low_in)


def normalize(grads, first_moment, second_moment):
    first = BETA_ONE * first_moment + (1.0 - BETA_ONE) * grads
    second = BETA_TWO * second_moment + ((1.0 - BETA_TWO) * grads) * grads
    guess = lax.rsqrt(second)
    below = second * guess + EPSILON
    return first * (guess * (2.0 - below * guess))


def split_two(value):
    high = value.astype(BF16)
    return high, (value - high.astype(F32)).astype(BF16)


def project_rank(rank_side, normed):
    both = jnp.dot(
        jnp.concatenate(split_two(rank_side[...]), axis=0), normed, preferred_element_type=F32
    )
    half = both.shape[0] // 2
    return both[:half] + both[half:]


def project_width(value, right):
    high, low = split_two(value)
    return jnp.dot(high, right, preferred_element_type=F32) + jnp.dot(
        low, right, preferred_element_type=F32
    )


def right_rows_copy(width_side, right, sem):
    rows = right.shape[0]
    first = pl.multiple_of(lax.axis_index("tensor") * rows, rows)
    return pltpu.make_async_copy(width_side.at[pl.ds(first, rows)], right, sem)


def slots_kernel(m, size, bounds, owner, source, moments, rank_side, width_side, *rest):
    pieces = rest[:size]
    out, head, low_scratch, acc, normed, ranked, wide, right, sem = rest[size:]
    right_copy = right_rows_copy(width_side, right, sem)
    right_copy.start()
    tokens, width = source.shape
    rank = head.shape[0]
    rows = tokens // size
    low, first, last = example_scalars(bounds, tokens)
    count = bounds.shape[2]
    place_pieces(pieces, low_scratch)
    step = 16

    def slot(j):
        return jnp.minimum(first + j, count - 1)

    def ends_here(j):
        return (first + j <= last) & (bounds[0, 1, slot(j)] <= low + tokens)

    @pl.loop(0, TOUCH)
    def _(j):
        start, end = bounds[0, 0, slot(j)], bounds[0, 1, slot(j)]

        @pl.when(ends_here(j) | (j == 0))
        def _():
            for c in range(size):
                begin = low + c * rows

                @pl.when((start < begin + rows) & (end > begin))
                def _():
                    left = masked(low_scratch[c], begin, start, end)
                    term = jnp.dot(
                        left, source[c * rows : (c + 1) * rows, :], preferred_element_type=F32
                    )
                    fresh = (start >= begin) | (c == 0)
                    acc[...] = jnp.where(fresh, 0.0, acc[...]) + term

            @pl.when(j == 0)
            def _():
                head[...] = (ADAPTER_SCALE * acc[...]).astype(BF16)

            @pl.when(j > 0)
            def _():
                for r in range(0, rank, step):
                    normed[r : r + step, :] = normalize(
                        ADAPTER_SCALE * acc[r : r + step, :],
                        moments[0, m, r : r + step, :].astype(F32),
                        moments[1, m, r : r + step, :].astype(F32),
                    ).astype(BF16)
                ranked[j] = project_rank(rank_side, normed[...])

    right_copy.wait()
    wide[...] = project_width(ranked[...].reshape(-1, width), right[...]).reshape(wide.shape)
    out[...] = jnp.zeros_like(out)
    for j in range(1, TOUCH):

        @pl.when(ends_here(j))
        def _():
            out[owner[0, slot(j)]] = wide[j].astype(BF16)


def slot_features(
    m, bounds, owner, source, moments, rank_side, width_side, pieces, name
):
    size = len(pieces)
    rank, rows = pieces[0].shape
    tokens, width = source.shape
    lines = rank_side.shape[0]
    columns = width_side.shape[1]
    return call(
        functools.partial(slots_kernel, m, size),
        [
            jax.ShapeDtypeStruct((owner.shape[1], lines, columns), BF16),
            jax.ShapeDtypeStruct((rank, width), BF16),
        ],
        [SMEM, SMEM, VMEM, VMEM, VMEM, HBM] + [VMEM] * size,
        [VMEM, VMEM],
        [
            pltpu.VMEM((size, rank, rows), BF16),
            pltpu.VMEM((rank, width), F32),
            pltpu.VMEM((rank, width), BF16),
            pltpu.VMEM((TOUCH, lines, width), F32),
            pltpu.VMEM((TOUCH, lines, columns), F32),
            pltpu.VMEM((width, columns), BF16),
            pltpu.SemaphoreType.DMA,
        ],
        2 * tokens * width * rank * TOUCH,
        4 * tokens * width,
        name,
    )(bounds, owner, source, moments, rank_side, width_side, *pieces)


def head_kernel(
    hops, block, bounds, owner, filled_grad, filled_in, head_grad, head_in, moments, rank_side, width_side, *rest
):
    arrived = rest[:hops]
    out, normed, ranked, right, sem = rest[hops:]
    right_copy = right_rows_copy(width_side, right, sem)
    right_copy.start()
    low, first, last = example_scalars(bounds, block)
    rank = head_in.shape[0]
    lines = rank_side.shape[0]
    continued = (bounds[0, 0, first] < low).astype(F32)
    step = 16
    out[:, :lines] = filled_grad[...]
    out[:, lines:] = filled_in[...]
    ends = bounds[0, 1, first] <= low + block

    @pl.when(ends)
    def _():
        for m, head in enumerate((head_grad, head_in)):
            for r in range(0, rank, step):
                here = slice(r, r + step)
                incoming = arrived[0][m, here, :].astype(F32)
                for k in range(1, hops):
                    incoming = incoming + arrived[k][m, here, :].astype(F32)
                normed[here, :] = normalize(
                    head[here, :].astype(F32) + continued * incoming,
                    moments[0, m, here, :].astype(F32),
                    moments[1, m, here, :].astype(F32),
                ).astype(BF16)
            ranked[m * lines : (m + 1) * lines, :] = project_rank(rank_side, normed[...])

    right_copy.wait()

    @pl.when(ends)
    def _():
        out[owner[0, first]] = project_width(ranked[...], right[...]).astype(BF16)


def head_features(
    bounds, owner, filled_grad, filled_in, head_grad, head_in, moments, rank_side, width_side, arrived, block
):
    hops = len(arrived)
    rank, width = head_in.shape
    slots, lines, columns = filled_in.shape
    return call(
        functools.partial(head_kernel, hops, block),
        jax.ShapeDtypeStruct((slots, 2 * lines, columns), BF16),
        [SMEM, SMEM] + [VMEM] * 6 + [HBM] + [VMEM] * hops,
        VMEM,
        [
            pltpu.VMEM((rank, width), BF16),
            pltpu.VMEM((2 * lines, width), F32),
            pltpu.VMEM((width, columns), BF16),
            pltpu.SemaphoreType.DMA,
        ],
        2 * width * 2 * rank * 4 * lines,
        8 * rank * width,
        "head_features",
    )(
        bounds,
        owner,
        filled_grad,
        filled_in,
        head_grad,
        head_in,
        moments,
        rank_side,
        width_side,
        *arrived,
    )


TILE = 256


def first_kernel(source, weight, out, held, weight_buf, source_sem, weight_sem):
    blocks = held.shape[0] // TILE
    parts = weight_buf.shape[0] // TILE

    def rows_copy(i):
        here = pl.ds(pl.multiple_of(i * TILE, TILE), TILE)
        return pltpu.make_async_copy(source.at[here], held.at[here], source_sem.at[i])

    def weight_copy(n):
        here = pl.ds(n * TILE, TILE)
        return pltpu.make_async_copy(weight.at[here], weight_buf.at[here], weight_sem.at[n])

    weight_copy(0).start()
    rows_copy(0).start()
    for n in range(1, parts):
        weight_copy(n).start()
    for i in range(1, blocks):
        rows_copy(i).start()

    @pl.loop(0, blocks)
    def _(i):
        rows_copy(i).wait()
        here = pl.ds(pl.multiple_of(i * TILE, TILE), TILE)
        for n in range(parts):

            @pl.when(i == 0)
            def _():
                weight_copy(n).wait()

            there = slice(n * TILE, (n + 1) * TILE)
            out[here, there] = dot_trailing(held[here, :], weight_buf[there, :])


def second_kernel(size, held, weight, down, done, *rest):
    pieces = rest[:size]
    out, result, low_scratch, low_rows, weight_buf, weight_sem, out_sem = rest[size:]
    tokens, width = result.shape
    split = done.shape[1]
    parts = weight_buf.shape[0] // TILE
    rows = tokens // size

    def weight_copy(n):
        return pltpu.make_async_copy(
            weight.at[pl.ds(split + n * TILE, TILE)],
            weight_buf.at[pl.ds(n * TILE, TILE)],
            weight_sem.at[n],
        )

    def out_copy(first, columns, k):
        here = pl.ds(first, columns)
        return pltpu.make_async_copy(result.at[:, here], out.at[:, here], out_sem.at[k])

    for n in range(parts):
        weight_copy(n).start()
    place_pieces(pieces, low_scratch)
    for c in range(size):
        here = slice(c * rows, (c + 1) * rows)
        low_rows[here, :] = low_scratch[c].astype(F32).T.astype(BF16)
        extra = ADAPTER_SCALE * dot_trailing(low_rows[here, :], down[:split, :])
        result[here, :split] = (done[here, :] + extra).astype(BF16)
    out_copy(0, split, 0).start()
    for n in range(parts):
        weight_copy(n).wait()

        @pl.loop(0, tokens // TILE)
        def _(i):
            here = pl.ds(pl.multiple_of(i * TILE, TILE), TILE)
            first = split + n * TILE
            extra = dot_trailing(low_rows[here, :], down[first : first + TILE, :])
            term = dot_trailing(held[here, :], weight_buf[n * TILE : (n + 1) * TILE, :])
            result[here, first : first + TILE] = (term + ADAPTER_SCALE * extra).astype(BF16)

        out_copy(split + n * TILE, TILE, n + 1).start()
    out_copy(0, split, 0).wait()
    for n in range(parts):
        out_copy(split + n * TILE, TILE, n + 1).wait()


def first_product(rows, weight, split):
    tokens, depth = rows.shape
    return call(
        first_kernel,
        [jax.ShapeDtypeStruct((tokens, split), F32), jax.ShapeDtypeStruct((tokens, depth), BF16)],
        [HBM, HBM],
        [VMEM, VMEM],
        [
            pltpu.VMEM((split, depth), BF16),
            pltpu.SemaphoreType.DMA((tokens // TILE,)),
            pltpu.SemaphoreType.DMA((split // TILE,)),
        ],
        2 * tokens * depth * split,
        2 * depth * (tokens + split),
        "first_product",
    )(rows, weight)


def second_product(held, weight, down, done, pieces):
    tokens, depth = held.shape
    width, rank = down.shape
    split = done.shape[1]
    parts = (width - split) // TILE
    size = len(pieces)
    return call(
        functools.partial(second_kernel, size),
        jax.ShapeDtypeStruct((tokens, width), BF16),
        [VMEM, HBM, VMEM, VMEM] + [VMEM] * size,
        HBM,
        [
            pltpu.VMEM((tokens, width), BF16),
            pltpu.VMEM((size,) + pieces[0].shape, BF16),
            pltpu.VMEM((tokens, rank), BF16),
            pltpu.VMEM((width - split, depth), BF16),
            pltpu.SemaphoreType.DMA((parts,)),
            pltpu.SemaphoreType.DMA((parts + 1,)),
        ],
        2 * tokens * depth * (width - split),
        2 * depth * (tokens + width - split),
        "second_product",
    )(held, weight, down, done, *pieces)


def gather_rows(value, axis, dim):
    size = lax.axis_size(axis)
    if size != 2:
        return lax.all_gather(value, axis, axis=dim, tiled=True)
    other = shifted(value, axis, 1)
    low = lax.axis_index(axis) == 0
    return jnp.concatenate([jnp.where(low, value, other), jnp.where(low, other, value)], axis=dim)


def per_device(
    attention_output_rows,
    projection_result_gradient,
    adapter_down_weight,
    adapter_up_weight,
    output_projection_weight,
    adam_first_moments,
    adam_second_moments,
    rank_side_projection,
    width_side_projection,
    bounds,
    example_owner_slot,
):
    packs, blk, width_local = attention_output_rows.shape
    assert packs == 1
    width = projection_result_gradient.shape[2]
    size = lax.axis_size("tensor")
    rows_in = attention_output_rows.reshape(blk, width_local)
    rows_grad = projection_result_gradient.reshape(blk, width)

    partial_in, rows_in = rank_pieces(
        rows_in, adapter_down_weight, True, size, width_local, "pieces_in"
    )
    partial_grad, columns_grad = rank_pieces(
        rows_grad, adapter_up_weight, False, size, width_local, "pieces_grad"
    )
    stacked = jnp.stack([adam_first_moments, adam_second_moments]).astype(BF16)
    moments = gather_rows(stacked, "dp", 2)
    low = lax.axis_index("seq") * blk
    starts, ends = bounds[0, 0], bounds[0, 1]
    spans = jnp.any((starts < low) & (ends >= low + blk)).astype(F32)

    sent_in = scatter(partial_in)
    sent_grad = scatter(partial_grad)
    low_in = gather_pieces(total_of(sent_in))
    rows_here, low_in[0] = lax.optimization_barrier((rows_grad, low_in[0]))
    done, held = first_product(rows_here, output_projection_weight, width_local // 2)
    sent_grad, done = lax.optimization_barrier((sent_grad, done))
    low_grad = gather_pieces(total_of(sent_grad))

    low_in, low_grad, moments, spans = lax.optimization_barrier((low_in, low_grad, moments, spans))
    tails = tail_parts(bounds, rows_in, columns_grad, low_grad, low_in)
    shared = (rank_side_projection, width_side_projection)

    def hop(outgoing, k):
        return lax.ppermute(outgoing, "seq", [(k, k + 1)])

    def onward(arrived):
        return (tails.astype(F32) + spans * arrived.astype(F32)).astype(BF16)

    arrived = [hop(tails, 0)]
    filled_in, head_in = slot_features(
        1, bounds, example_owner_slot, columns_grad, moments, *shared, low_in, "slots_in"
    )
    arrived[0], head_in = lax.optimization_barrier((arrived[0], head_in))
    arrived.append(hop(onward(arrived[0]), 1))
    filled_grad, head_grad = slot_features(
        0, bounds, example_owner_slot, rows_in, moments, *shared, low_grad, "slots_grad"
    )
    arrived[1], head_grad = lax.optimization_barrier((arrived[1], head_grad))
    for k in range(2, lax.axis_size("seq") - 1):
        arrived.append(hop(onward(arrived[-1]), k))
    buffer = head_features(
        bounds,
        example_owner_slot,
        filled_grad,
        filled_in,
        head_grad,
        head_in,
        moments,
        *shared,
        arrived,
        blk,
    )
    arrived = lax.all_to_all(buffer, ("seq", "tensor"), split_axis=0, concat_axis=0, tiled=True)
    features = jnp.sum(arrived.astype(F32), axis=0).reshape(1, 1, -1)
    out = second_product(held, output_projection_weight, adapter_down_weight, done, low_grad)
    return (out.reshape(attention_output_rows.shape), features)


def solution(mesh):
    return jax.shard_map(
        per_device,
        mesh=mesh,
        in_specs=(
            P("dp", "seq", "tensor"),
            P("dp", "seq", None),
            P("tensor", None),
            P(None, "tensor"),
            P("tensor", None),
            P(None, "dp", "tensor"),
            P(None, "dp", "tensor"),
            P(),
            P(),
            P("dp", None, None),
            P("dp", None),
        ),
        out_specs=(P("dp", "seq", "tensor"), P("dp", ("seq", "tensor"), None)),
        check_vma=False,
    )
```

time: 220 us -> 101 us (0.46)
  waiting for transfers between devices: 90.6 us -> 6.03 us
  blocking collectives: 51.8 us -> 0 us
  matrix products: 39.1 us -> 0 us
  Pallas kernels: 0 us -> 35.1 us
  starting transfers between devices: 0.12 us -> 33.3 us
  between operations: 17.1 us -> 1.63 us
  local copies, waits for them, and re-layouts: 8.07 us -> 21.4 us
  other arithmetic: 12.5 us -> 2.62 us
    unnamed x4 -> x0, waiting for transfers between devices: 90.6 us -> none
    psum x1 -> x0, blocking collectives: 45.6 us -> none  [per_device(): lax.psum((reduced_input, reduced_gradient), 'tensor')]
    dot_general x9 -> x0, matrix products: 39.1 us -> none  [the longest x3 21.7 us: contract_trailing(): lax.dot_general(left, right, (((1,), (1,)), ((), ())), preferred_element_...]
    pallas_call x0 -> x8, Pallas kernels: none -> 35.1 us  [the longest x1 11.7 us: first_product(): call(first_kernel, [jax.ShapeDtypeStruct((tokens, split), F32), jax.Shape...]
    ppermute x0 -> x16, starting transfers between devices: none -> 22.6 us  [the longest x13 19.9 us: shifted(): lax.ppermute(value, axis, [(i, (i + shift) % size) for i in range(size)])]
    unnamed x25 -> x34, local copies, waits for them, and re-layouts: 4.7 us -> 20.7 us
    all_to_all x0 -> x1, starting transfers between devices: none -> 10.8 us  [per_device(): lax.all_to_all(buffer, ('seq', 'tensor'), split_axis=0, concat_axis=0, ti...]
    unnamed x1 -> x0, blocking collectives: 6.13 us -> none
  transfers between devices with their start and end apart: 3 -> 17, of which waited for: 1 -> 4; matrix products, arithmetic and copies ran while one was open for 19% -> 2% of each run, Pallas kernels for 0% -> 30%
where the time goes in v3:
time: 101 us; the launch traced here: 100 us
  Pallas kernels  35.1 us (35%)
  starting transfers between devices  33.3 us (33%)
  local copies, waits for them, and re-layouts  21.4 us (21%)
  waiting for transfers between devices  6.03 us (6%)
  other arithmetic  2.62 us (3%)
  between operations  1.63 us (2%)
    unnamed x34, local copies, waits for them, and re-layouts  20.7 us
    ppermute x13, starting transfers between devices, shifted(): lax.ppermute(value, axis, [(i, (i + shift) % size) for i in range(size)])  19.9 us
    pallas_call x1, Pallas kernels, first_product(): call(first_kernel, [jax.ShapeDtypeStruct((tokens, split), F32), jax.Shape...  11.7 us
    all_to_all x1, starting transfers between devices, per_device(): lax.all_to_all(buffer, ('seq', 'tensor'), split_axis=0, concat_axis=0, ti...  10.8 us
    pallas_call x2, Pallas kernels, slot_features(): call(functools.partial(slots_kernel, m, size), [jax.ShapeDtypeStruct((own...  8.13 us
    pallas_call x1, Pallas kernels, second_product(): call(functools.partial(second_kernel, size), jax.ShapeDtypeStruct((tokens...  7.68 us
    ppermute x13, waiting for transfers between devices, shifted(): lax.ppermute(value, axis, [(i, (i + shift) % size) for i in range(size)])  6.02 us
    pallas_call x2, Pallas kernels, rank_pieces(): call(functools.partial(pieces_kernel, along_rows), [jax.ShapeDtypeStruct(...  3.86 us
  transfers between devices with their start and end apart: 17, of which 4 were waited for; matrix products, arithmetic and copies ran while one was open for 2% of the time, Pallas kernels for 30%

profile of v3, /device:TPU:0, one launch (start us, length us, event | category | flops | bytes accessed | tf_op | source)
XLA Modules:
  0.0 100.1 jit_solution(15827746803791365012)
XLA Ops:
  0.6 1.6 %copy-done.5 = bf16[1,1024,1024]{2,1,0:T(8,128)(2,1)S(1)} copy-done((bf16[1,1024,1024]{2,1,0:T(8,128)(2,1)S(1)}, bf16[1,1024,1024]{2,1,0:T(8,128)(2,1)}, u32[]{:S(2)}) %copy-start.5) | copy-done | bytes 2097176
  2.2 0.9 copy-done.11
  3.2 1.7 %pieces_in.1 = (bf16[128,256]{1,0:T(8,128)(2,1)S(1)}, bf16[128,256]{1,0:T(8,128)(2,1)S(1)}, bf16[128,256]{1,0:T(8,128)(2,1)S(1)}, bf16[128,256]{1,0:T(8,128)(2,1)S(1)}, bf16[1024,1024]{1,0:T(8,128)(2,1)S(1)}) custom-call(bf16[1024,1024]{1,0:T(8,128)(2,1)S(1)} %bitcast.9, bf16[1024,128]{1,0:T(8,128)(2,1)S(1)} %copy-done.11), custom_call_target="tpu_custom_call" | custom-call | flops 268435456 | bytes 2097152 | tf_op jit(solution)/shard_map/pieces_in/pallas_call | solution.py:78
  4.8 3.1 %collective-permute-start = (bf16[128,256]{1,0:T(8,128)(2,1)S(1)}, bf16[128,256]{1,0:T(8,128)(2,1)S(1)}, u32[]{:S(2)}, u32[]{:S(2)}) collective-permute-start(bf16[128,256]{1,0:T(8,128)(2,1)S(1)} %get-tuple-element.40), channel_id=1, source_target_pairs={{0,1},{1,2},{2,3},{3,0},{4,5},{5,6},{6,7},{7,4},{8,9},{9,10},{10,1... | collective-permute-start | bytes 196616 | tf_op jit(solution)/shard_map/ppermute | solution.py:98
  7.9 2.6 %collective-permute-start.1 = (bf16[128,256]{1,0:T(8,128)(2,1)S(1)}, bf16[128,256]{1,0:T(8,128)(2,1)S(1)}, u32[]{:S(2)}, u32[]{:S(2)}) collective-permute-start(bf16[128,256]{1,0:T(8,128)(2,1)S(1)} %get-tuple-element.41), channel_id=1, source_target_pairs={{0,2},{1,3},{2,0},{3,1},{4,6},{5,7},{6,4},{7,5},{8,10},{9,11},{10,... | collective-permute-start | bytes 196616 | tf_op jit(solution)/shard_map/ppermute | solution.py:98
  10.5 1.3 %collective-permute-start.2 = (bf16[128,256]{1,0:T(8,128)(2,1)S(1)}, bf16[128,256]{1,0:T(8,128)(2,1)S(1)}, u32[]{:S(2)}, u32[]{:S(2)}) collective-permute-start(bf16[128,256]{1,0:T(8,128)(2,1)S(1)} %get-tuple-element.42), channel_id=1, source_target_pairs={{0,3},{1,0},{2,1},{3,2},{4,7},{5,4},{6,5},{7,6},{8,11},{9,8},{10,9... | collective-permute-start | bytes 196616 | tf_op jit(solution)/shard_map/ppermute | solution.py:98
  11.9 3.4 %copy-done = bf16[1,1024,4096]{2,1,0:T(8,128)(2,1)S(1)} copy-done((bf16[1,1024,4096]{2,1,0:T(8,128)(2,1)S(1)}, bf16[1,1024,4096]{2,1,0:T(8,128)(2,1)}, u32[]{:S(2)}) %copy-start) | copy-done | bytes 8388632
  15.2 2.2 %pieces_grad.1 = (bf16[128,256]{1,0:T(8,128)(2,1)S(1)}, bf16[128,256]{1,0:T(8,128)(2,1)S(1)}, bf16[128,256]{1,0:T(8,128)(2,1)S(1)}, bf16[128,256]{1,0:T(8,128)(2,1)S(1)}, bf16[1024,1024]{1,0:T(8,128)(2,1)S(1)}) custom-call(bf16[1024,4096]{1,0:T(8,128)(2,1)S(1)} %bitcast.7, bf16[128,1024]{1,0:T(8,128)(2,1)S(1)} %copy-done.13), custom_call_target="tpu_custom_call" | custom-call | flops 268435456 | bytes 2097152 | tf_op jit(solution)/shard_map/pieces_grad/pallas_call | solution.py:78
  17.5 1.4 %copy-done.7 = bf16[1024,1024]{1,0:T(8,128)(2,1)} copy-done((bf16[1024,1024]{1,0:T(8,128)(2,1)}, bf16[1024,1024]{1,0:T(8,128)(2,1)S(1)}, u32[]{:S(2)}) %copy-start.7) | copy-done | bytes 2097176
  21.1 1.3 %convert_bitcast_fusion = (bf16[1,2,64,1024]{3,2,1,0:T(8,128)(2,1)S(1)}, bf16[1,2,64,1024]{3,2,1,0:T(8,128)(2,1)S(1)}) fusion(f32[2,64,1024]{2,1,0:T(8,128)} %param.17, f32[2,64,1024]{2,1,0:T(8,128)} %param.16), kind=kLoop, calls=%fused_computation.9 | loop fusion | flops 262144 | bytes 1572864 | tf_op jit(solution)/shard_map/stack | solution.py:538
  22.5 2.9 %collective-permute-start.5 = (bf16[128,256]{1,0:T(8,128)(2,1)S(1)}, bf16[128,256]{1,0:T(8,128)(2,1)S(1)}, u32[]{:S(2)}, u32[]{:S(2)}) collective-permute-start(bf16[128,256]{1,0:T(8,128)(2,1)S(1)} %get-tuple-element.48), channel_id=1, source_target_pairs={{0,3},{1,0},{2,1},{3,2},{4,7},{5,4},{6,5},{7,6},{8,11},{9,8},{10,9... | collective-permute-start | bytes 196616 | tf_op jit(solution)/shard_map/ppermute | solution.py:98
  25.4 1.5 %collective-permute-start.12 = (bf16[2,2,64,1024]{3,2,1,0:T(8,128)(2,1)S(1)}, bf16[2,2,64,1024]{3,2,1,0:T(8,128)(2,1)S(1)}, u32[]{:S(2)}, u32[]{:S(2)}) collective-permute-start(bf16[2,2,64,1024]{3,2,1,0:T(8,128)(2,1)S(1)} %pad_maximum_fusion.1), channel_id=1, source_target_pairs={{0,16},{16,0},{1,17},{17,1},{2,18},{18,2},{3,19},{19,3},{4,20},{20... | collective-permute-start | bytes 1572872 | tf_op jit(solution)/shard_map/ppermute | solution.py:98
  26.9 3.4 %copy-done.1 = bf16[1,1024,4096]{2,1,0:T(8,128)(2,1)S(1)} copy-done((bf16[1,1024,4096]{2,1,0:T(8,128)(2,1)S(1)}, bf16[1,1024,4096]{2,1,0:T(8,128)(2,1)}, u32[]{:S(2)}) %copy-start.1) | copy-done | bytes 8388632
  30.3 11.7 %first_product.1 = (f32[1024,512]{1,0:T(8,128)S(1)}, bf16[1024,4096]{1,0:T(8,128)(2,1)S(1)}) custom-call(bf16[1024,4096]{1,0:T(8,128)(2,1)S(1)} %bitcast.8, bf16[1024,4096]{1,0:T(8,128)(2,1)} %weight.7), custom_call_target="tpu_custom_call" | custom-call | flops 4294967296 | bytes 12582912 | tf_op jit(solution)/shard_map/first_product/pallas_call | solution.py:462
  42.0 3.3 %copy-done.3 = bf16[1024,4096]{1,0:T(8,128)(2,1)} copy-done((bf16[1024,4096]{1,0:T(8,128)(2,1)}, bf16[1024,4096]{1,0:T(8,128)(2,1)S(1)}, u32[]{:S(2)}) %copy-start.3) | copy-done | bytes 8388632
  45.4 2.1 %collective-permute-start.10 = (bf16[128,256]{1,0:T(8,128)(2,1)S(1)}, bf16[128,256]{1,0:T(8,128)(2,1)S(1)}, u32[]{:S(2)}, u32[]{:S(2)}) collective-permute-start(bf16[128,256]{1,0:T(8,128)(2,1)S(1)} %add_convert_fusion.rest_0_), channel_id=1, source_target_pairs={{0,2},{1,3},{2,0},{3,1},{4,6},{5,7},{6,4},{7,5},{8,10},{9,11},{10,... | collective-permute-start | bytes 196616 | tf_op jit(solution)/shard_map/ppermute | solution.py:98
  47.5 1.0 collective-permute-start.11
  48.5 1.0 %collective-permute-start.9 = (bf16[128,256]{1,0:T(8,128)(2,1)S(1)}, bf16[128,256]{1,0:T(8,128)(2,1)S(1)}, u32[]{:S(2)}, u32[]{:S(2)}) collective-permute-start(bf16[128,256]{1,0:T(8,128)(2,1)S(1)} %add_convert_fusion.rest_0_), channel_id=1, source_target_pairs={{0,1},{1,2},{2,3},{3,0},{4,5},{5,6},{6,7},{7,4},{8,9},{9,10},{10,1... | collective-permute-start | bytes 196616 | tf_op jit(solution)/shard_map/ppermute | solution.py:98
  49.5 3.3 %collective-permute-start.7 = (bf16[128,256]{1,0:T(8,128)(2,1)S(1)}, bf16[128,256]{1,0:T(8,128)(2,1)S(1)}, u32[]{:S(2)}, u32[]{:S(2)}) collective-permute-start(bf16[128,256]{1,0:T(8,128)(2,1)S(1)} %add_convert_fusion.1.rest_0_.rest_4_), channel_id=1, source_target_pairs={{0,2},{1,3},{2,0},{3,1},{4,6},{5,7},{6,4},{7,5},{8,10},{9,11},{10,... | collective-permute-start | bytes 196616 | tf_op jit(solution)/shard_map/ppermute | solution.py:98
  52.9 1.2 %collective-permute-done.10.rest_2_ = bf16[128,256]{1,0:T(8,128)(2,1)S(1)} collective-permute-done((bf16[128,256]{1,0:T(8,128)(2,1)S(1)}, bf16[128,256]{1,0:T(8,128)(2,1)S(1)}, u32[]{:S(2)}, u32[]{:S(2)}) %collective-permute-start.10) | collective-permute-done | bytes 65568 | tf_op jit(solution)/shard_map/ppermute | solution.py:98
  54.3 1.7 %collective-permute-done.11.rest_3_ = bf16[128,256]{1,0:T(8,128)(2,1)S(1)} collective-permute-done((bf16[128,256]{1,0:T(8,128)(2,1)S(1)}, bf16[128,256]{1,0:T(8,128)(2,1)S(1)}, u32[]{:S(2)}, u32[]{:S(2)}) %collective-permute-start.11) | collective-permute-done | bytes 65568 | tf_op jit(solution)/shard_map/ppermute | solution.py:98
  56.0 2.5 %collective-permute-done.7.rest_2_.rest_6_ = bf16[128,256]{1,0:T(8,128)(2,1)S(1)} collective-permute-done((bf16[128,256]{1,0:T(8,128)(2,1)S(1)}, bf16[128,256]{1,0:T(8,128)(2,1)S(1)}, u32[]{:S(2)}, u32[]{:S(2)}) %collective-permute-start.7) | collective-permute-done | bytes 65568 | tf_op jit(solution)/shard_map/ppermute | solution.py:98
  59.0 1.1 %tail_parts.1 = bf16[2,128,1024]{2,1,0:T(8,128)(2,1)S(1)} custom-call(s32[1,2,16]{2,1,0:T(2,128)S(1)} %copy-done.14, bf16[1024,1024]{1,0:T(8,128)(2,1)S(1)} %get-tuple-element.60.source.rows_in, bf16[1024,1024]{1,0:T(8,128)(2,1)S(1)} %copy-done.8, bf16[128,256]{1,0:T(8,128)(2,1)S(1)} %add_convert_fusion.rest_0_, ...), custom_call_target="tpu_custom_call" | custom-call | flops 536870912 | bytes 4194304 | tf_op jit(solution)/shard_map/tail_parts/pallas_call | solution.py:169
  60.1 1.3 %collective-permute-start.13 = (bf16[2,128,1024]{2,1,0:T(8,128)(2,1)S(1)}, bf16[2,128,1024]{2,1,0:T(8,128)(2,1)S(1)}, u32[]{:S(2)}, u32[]{:S(2)}) collective-permute-start(bf16[2,128,1024]{2,1,0:T(8,128)(2,1)S(1)} %tail_parts.1), channel_id=1, source_target_pairs={{0,4},{1,5},{2,6},{3,7},{16,20},{17,21},{18,22},{19,23}} | collective-permute-start | bytes 1572872 | tf_op jit(solution)/shard_map/ppermute | solution.py:557
  61.5 4.1 %slots_in.1 = (bf16[16,16,256]{2,1,0:T(8,128)(2,1)S(1)}, bf16[128,1024]{1,0:T(8,128)(2,1)S(1)}) custom-call(s32[1,2,16]{2,1,0:T(2,128)S(1)} %copy-done.14, s32[1,16]{1,0:T(1,128)S(1)} %copy-done.16, bf16[1024,1024]{1,0:T(8,128)(2,1)S(1)} %copy-done.8, bf16[2,2,128,1024]{3,2,1,0:T(8,128)(2,1)S(1)} %pad_maximum_fusion.moments, f32[16,128]{1,0:T(8,128)S(1)} %copy-done.15, ...), custom_call_target="tpu_custom_call" | custom-call | flops 2147483648 | bytes 4194304 | tf_op jit(solution)/shard_map/slots_in/pallas_call | solution.py:284
  65.8 0.7 collective-permute-start.14
  66.5 4.1 %slots_grad.1 = (bf16[16,16,256]{2,1,0:T(8,128)(2,1)S(1)}, bf16[128,1024]{1,0:T(8,128)(2,1)S(1)}) custom-call(s32[1,2,16]{2,1,0:T(2,128)S(1)} %copy-done.14, s32[1,16]{1,0:T(1,128)S(1)} %copy-done.16, bf16[1024,1024]{1,0:T(8,128)(2,1)S(1)} %get-tuple-element.60.source.rows_in, bf16[2,2,128,1024]{3,2,1,0:T(8,128)(2,1)S(1)} %pad_maximum_fusion.moments, ...), custom_call_target="tpu_custom_call" | custom-call | flops 2147483648 | bytes 4194304 | tf_op jit(solution)/shard_map/slots_grad/pallas_call | solution.py:284
  71.5 2.6 %head_features.1 = bf16[16,32,256]{2,1,0:T(8,128)(2,1)} custom-call(s32[1,2,16]{2,1,0:T(2,128)S(1)} %copy-done.14, s32[1,16]{1,0:T(1,128)S(1)} %copy-done.16, bf16[16,16,256]{2,1,0:T(8,128)(2,1)S(1)} %get-tuple-element.62.filled_grad, bf16[16,16,256]{2,1,0:T(8,128)(2,1)S(1)} %get-tuple-element.68.filled_in, ...), custom_call_target="tpu_custom_call" | custom-call | flops 33554432 | bytes 1048576 | tf_op jit(solution)/shard_map/head_features/pallas_call | solution.py:351
  74.2 10.8 %all-to-all-start = ((bf16[16,32,256]{2,1,0:T(8,128)(2,1)}), bf16[16,32,256]{2,1,0:T(8,128)(2,1)S(1)}, u32[]{:S(2)}, u32[]{:S(2)}) async-start(bf16[16,32,256]{2,1,0:T(8,128)(2,1)} %head_features.1), calls=%async_computation | async-start | bytes 524288 | tf_op jit(solution)/shard_map/all_to_all | solution.py:586
  85.0 3.4 %copy-done.2 = bf16[1024,4096]{1,0:T(8,128)(2,1)S(1)} copy-done((bf16[1024,4096]{1,0:T(8,128)(2,1)S(1)}, bf16[1024,4096]{1,0:T(8,128)(2,1)}, u32[]{:S(2)}) %copy-start.2) | copy-done | bytes 8388632
  88.3 3.4 %copy-done.4 = bf16[1024,4096]{1,0:T(8,128)(2,1)S(1)} copy-done((bf16[1024,4096]{1,0:T(8,128)(2,1)S(1)}, bf16[1024,4096]{1,0:T(8,128)(2,1)}, u32[]{:S(2)}) %copy-start.4) | copy-done | bytes 8388632
  91.7 7.7 %second_product.1 = bf16[1024,1024]{1,0:T(8,128)(2,1)} custom-call(bf16[1024,4096]{1,0:T(8,128)(2,1)S(1)} %copy-done.4, bf16[1024,4096]{1,0:T(8,128)(2,1)S(1)} %copy-done.2, bf16[1024,128]{1,0:T(8,128)(2,1)S(1)} %copy-done.12, f32[1024,512]{1,0:T(8,128)S(1)} %copy-done.10, bf16[128,256]{1,0:T(8,128)(2,1)S(1)} %add_convert_fusion.rest_0_, ...), custom_call_target="tpu_custom_call" | custom-call | flops 4294967296 | bytes 12582912 | tf_op jit(solution)/shard_map/second_product/pallas_call | solution.py:484
  (55 shorter events, 4.4 us)
Async XLA Ops:
  0.6 1.6 %copy-start.5 = (bf16[1,1024,1024]{2,1,0:T(8,128)(2,1)S(1)}, bf16[1,1024,1024]{2,1,0:T(8,128)(2,1)}, u32[]{:S(2)}) copy-start(bf16[1,1024,1024]{2,1,0:T(8,128)(2,1)} %param.11) | copy-start | bytes 6291460
  3.2 8.7 %copy-start.13 = (bf16[128,1024]{1,0:T(8,128)(2,1)S(1)}, bf16[128,1024]{1,0:T(8,128)(2,1)}, u32[]{:S(2)}) copy-start(bf16[128,1024]{1,0:T(8,128)(2,1)} %weight.6) | copy-start | bytes 786436
  4.8 17.7 %collective-permute-start = (bf16[128,256]{1,0:T(8,128)(2,1)S(1)}, bf16[128,256]{1,0:T(8,128)(2,1)S(1)}, u32[]{:S(2)}, u32[]{:S(2)}) collective-permute-start(bf16[128,256]{1,0:T(8,128)(2,1)S(1)} %get-tuple-element.40), channel_id=1, source_target_pairs={{0,1},{1,2},{2,3},{3,0},{4,5},{5,6},{6,7},{7,4},{8,9},{9,10},{10,1... | collective-permute-start | bytes 196616 | tf_op jit(solution)/shard_map/ppermute | solution.py:98
  7.9 17.4 %collective-permute-start.1 = (bf16[128,256]{1,0:T(8,128)(2,1)S(1)}, bf16[128,256]{1,0:T(8,128)(2,1)S(1)}, u32[]{:S(2)}, u32[]{:S(2)}) collective-permute-start(bf16[128,256]{1,0:T(8,128)(2,1)S(1)} %get-tuple-element.41), channel_id=1, source_target_pairs={{0,2},{1,3},{2,0},{3,1},{4,6},{5,7},{6,4},{7,5},{8,10},{9,11},{10,... | collective-permute-start | bytes 196616 | tf_op jit(solution)/shard_map/ppermute | solution.py:98
  10.5 16.4 %collective-permute-start.2 = (bf16[128,256]{1,0:T(8,128)(2,1)S(1)}, bf16[128,256]{1,0:T(8,128)(2,1)S(1)}, u32[]{:S(2)}, u32[]{:S(2)}) collective-permute-start(bf16[128,256]{1,0:T(8,128)(2,1)S(1)} %get-tuple-element.42), channel_id=1, source_target_pairs={{0,3},{1,0},{2,1},{3,2},{4,7},{5,4},{6,5},{7,6},{8,11},{9,8},{10,9... | collective-permute-start | bytes 196616 | tf_op jit(solution)/shard_map/ppermute | solution.py:98
  11.9 3.4 %copy-start = (bf16[1,1024,4096]{2,1,0:T(8,128)(2,1)S(1)}, bf16[1,1024,4096]{2,1,0:T(8,128)(2,1)}, u32[]{:S(2)}) copy-start(bf16[1,1024,4096]{2,1,0:T(8,128)(2,1)} %param.12) | copy-start | bytes 25165828
  15.2 4.6 %copy-start.14 = (s32[1,2,16]{2,1,0:T(2,128)S(1)}, s32[1,2,16]{2,1,0:T(2,128)}, u32[]{:S(2)}) copy-start(s32[1,2,16]{2,1,0:T(2,128)} %bounds.7) | copy-start | bytes 388
  18.8 26.5 %collective-permute-start.3 = (bf16[128,256]{1,0:T(8,128)(2,1)S(1)}, bf16[128,256]{1,0:T(8,128)(2,1)S(1)}, u32[]{:S(2)}, u32[]{:S(2)}) collective-permute-start(bf16[128,256]{1,0:T(8,128)(2,1)S(1)} %get-tuple-element.46), channel_id=1, source_target_pairs={{0,1},{1,2},{2,3},{3,0},{4,5},{5,6},{6,7},{7,4},{8,9},{9,10},{10,1... | collective-permute-start | bytes 196616 | tf_op jit(solution)/shard_map/ppermute | solution.py:98
  19.5 25.8 %collective-permute-start.4 = (bf16[128,256]{1,0:T(8,128)(2,1)S(1)}, bf16[128,256]{1,0:T(8,128)(2,1)S(1)}, u32[]{:S(2)}, u32[]{:S(2)}) collective-permute-start(bf16[128,256]{1,0:T(8,128)(2,1)S(1)} %get-tuple-element.47), channel_id=1, source_target_pairs={{0,2},{1,3},{2,0},{3,1},{4,6},{5,7},{6,4},{7,5},{8,10},{9,11},{10,... | collective-permute-start | bytes 196616 | tf_op jit(solution)/shard_map/ppermute | solution.py:98
  22.5 22.8 %collective-permute-start.5 = (bf16[128,256]{1,0:T(8,128)(2,1)S(1)}, bf16[128,256]{1,0:T(8,128)(2,1)S(1)}, u32[]{:S(2)}, u32[]{:S(2)}) collective-permute-start(bf16[128,256]{1,0:T(8,128)(2,1)S(1)} %get-tuple-element.48), channel_id=1, source_target_pairs={{0,3},{1,0},{2,1},{3,2},{4,7},{5,4},{6,5},{7,6},{8,11},{9,8},{10,9... | collective-permute-start | bytes 196616 | tf_op jit(solution)/shard_map/ppermute | solution.py:98
  25.4 24.2 %collective-permute-start.12 = (bf16[2,2,64,1024]{3,2,1,0:T(8,128)(2,1)S(1)}, bf16[2,2,64,1024]{3,2,1,0:T(8,128)(2,1)S(1)}, u32[]{:S(2)}, u32[]{:S(2)}) collective-permute-start(bf16[2,2,64,1024]{3,2,1,0:T(8,128)(2,1)S(1)} %pad_maximum_fusion.1), channel_id=1, source_target_pairs={{0,16},{16,0},{1,17},{17,1},{2,18},{18,2},{3,19},{19,3},{4,20},{20... | collective-permute-start | bytes 1572872 | tf_op jit(solution)/shard_map/ppermute | solution.py:98
  26.9 3.4 %copy-start.1 = (bf16[1,1024,4096]{2,1,0:T(8,128)(2,1)S(1)}, bf16[1,1024,4096]{2,1,0:T(8,128)(2,1)}, u32[]{:S(2)}) copy-start(bf16[1,1024,4096]{2,1,0:T(8,128)(2,1)} %param.12) | copy-start | bytes 25165828
  42.0 3.3 %copy-start.3 = (bf16[1024,4096]{1,0:T(8,128)(2,1)}, bf16[1024,4096]{1,0:T(8,128)(2,1)S(1)}, u32[]{:S(2)}) copy-start(bf16[1024,4096]{1,0:T(8,128)(2,1)S(1)} %get-tuple-element.44.held) | copy-start | bytes 25165828
  45.3 9.0 %copy-start.9 = (f32[1024,512]{1,0:T(8,128)}, f32[1024,512]{1,0:T(8,128)S(1)}, u32[]{:S(2)}) copy-start(f32[1024,512]{1,0:T(8,128)S(1)} %get-tuple-element.50.done) | copy-start | bytes 6291460
  45.4 13.7 %copy-start.8 = (bf16[1024,1024]{1,0:T(8,128)(2,1)S(1)}, bf16[1024,1024]{1,0:T(8,128)(2,1)}, u32[]{:S(2)}) copy-start(bf16[1024,1024]{1,0:T(8,128)(2,1)} %copy-done.7) | copy-start | bytes 6291460
  45.4 8.8 %collective-permute-start.10 = (bf16[128,256]{1,0:T(8,128)(2,1)S(1)}, bf16[128,256]{1,0:T(8,128)(2,1)S(1)}, u32[]{:S(2)}, u32[]{:S(2)}) collective-permute-start(bf16[128,256]{1,0:T(8,128)(2,1)S(1)} %add_convert_fusion.rest_0_), channel_id=1, source_target_pairs={{0,2},{1,3},{2,0},{3,1},{4,6},{5,7},{6,4},{7,5},{8,10},{9,11},{10,... | collective-permute-start | bytes 196616 | tf_op jit(solution)/shard_map/ppermute | solution.py:98
  47.5 8.5 %collective-permute-start.11 = (bf16[128,256]{1,0:T(8,128)(2,1)S(1)}, bf16[128,256]{1,0:T(8,128)(2,1)S(1)}, u32[]{:S(2)}, u32[]{:S(2)}) collective-permute-start(bf16[128,256]{1,0:T(8,128)(2,1)S(1)} %add_convert_fusion.rest_0_), channel_id=1, source_target_pairs={{0,3},{1,0},{2,1},{3,2},{4,7},{5,4},{6,5},{7,6},{8,11},{9,8},{10,9... | collective-permute-start | bytes 196616 | tf_op jit(solution)/shard_map/ppermute | solution.py:98
  48.5 7.5 %collective-permute-start.9 = (bf16[128,256]{1,0:T(8,128)(2,1)S(1)}, bf16[128,256]{1,0:T(8,128)(2,1)S(1)}, u32[]{:S(2)}, u32[]{:S(2)}) collective-permute-start(bf16[128,256]{1,0:T(8,128)(2,1)S(1)} %add_convert_fusion.rest_0_), channel_id=1, source_target_pairs={{0,1},{1,2},{2,3},{3,0},{4,5},{5,6},{6,7},{7,4},{8,9},{9,10},{10,1... | collective-permute-start | bytes 196616 | tf_op jit(solution)/shard_map/ppermute | solution.py:98
  49.5 6.5 %collective-permute-start.6 = (bf16[128,256]{1,0:T(8,128)(2,1)S(1)}, bf16[128,256]{1,0:T(8,128)(2,1)S(1)}, u32[]{:S(2)}, u32[]{:S(2)}) collective-permute-start(bf16[128,256]{1,0:T(8,128)(2,1)S(1)} %add_convert_fusion.1.rest_0_.rest_4_), channel_id=1, source_target_pairs={{0,1},{1,2},{2,3},{3,0},{4,5},{5,6},{6,7},{7,4},{8,9},{9,10},{10,1... | collective-permute-start | bytes 196616 | tf_op jit(solution)/shard_map/ppermute | solution.py:98
  49.5 9.0 %collective-permute-start.7 = (bf16[128,256]{1,0:T(8,128)(2,1)S(1)}, bf16[128,256]{1,0:T(8,128)(2,1)S(1)}, u32[]{:S(2)}, u32[]{:S(2)}) collective-permute-start(bf16[128,256]{1,0:T(8,128)(2,1)S(1)} %add_convert_fusion.1.rest_0_.rest_4_), channel_id=1, source_target_pairs={{0,2},{1,3},{2,0},{3,1},{4,6},{5,7},{6,4},{7,5},{8,10},{9,11},{10,... | collective-permute-start | bytes 196616 | tf_op jit(solution)/shard_map/ppermute | solution.py:98
  54.2 4.8 %collective-permute-start.8 = (bf16[128,256]{1,0:T(8,128)(2,1)S(1)}, bf16[128,256]{1,0:T(8,128)(2,1)S(1)}, u32[]{:S(2)}, u32[]{:S(2)}) collective-permute-start(bf16[128,256]{1,0:T(8,128)(2,1)S(1)} %add_convert_fusion.1.rest_0_.rest_4_), channel_id=1, source_target_pairs={{0,3},{1,0},{2,1},{3,2},{4,7},{5,4},{6,5},{7,6},{8,11},{9,8},{10,9... | collective-permute-start | bytes 196616 | tf_op jit(solution)/shard_map/ppermute | solution.py:98
  59.0 2.4 %copy-start.6 = (bf16[4096,256]{1,0:T(8,128)(2,1)S(1)}, bf16[4096,256]{1,0:T(8,128)(2,1)}, u32[]{:S(2)}) copy-start(bf16[4096,256]{1,0:T(8,128)(2,1)} %width_side.5) | copy-start | bytes 6291460
  59.0 2.4 %copy-start.15 = (f32[16,128]{1,0:T(8,128)S(1)}, f32[16,128]{1,0:T(8,128)}, u32[]{:S(2)}) copy-start(f32[16,128]{1,0:T(8,128)} %rank_side.5) | copy-start | bytes 24580
  59.0 2.5 %copy-start.16 = (s32[1,16]{1,0:T(1,128)S(1)}, s32[1,16]{1,0:T(1,128)}, u32[]{:S(2)}) copy-start(s32[1,16]{1,0:T(1,128)} %owner.5) | copy-start | bytes 196
  60.1 5.4 %collective-permute-start.13 = (bf16[2,128,1024]{2,1,0:T(8,128)(2,1)S(1)}, bf16[2,128,1024]{2,1,0:T(8,128)(2,1)S(1)}, u32[]{:S(2)}, u32[]{:S(2)}) collective-permute-start(bf16[2,128,1024]{2,1,0:T(8,128)(2,1)S(1)} %tail_parts.1), channel_id=1, source_target_pairs={{0,4},{1,5},{2,6},{3,7},{16,20},{17,21},{18,22},{19,23}} | collective-permute-start | bytes 1572872 | tf_op jit(solution)/shard_map/ppermute | solution.py:557
  65.8 4.8 %collective-permute-start.14 = (bf16[2,128,1024]{2,1,0:T(8,128)(2,1)S(1)}, bf16[2,128,1024]{2,1,0:T(8,128)(2,1)S(1)}, u32[]{:S(2)}, u32[]{:S(2)}) collective-permute-start(bf16[2,128,1024]{2,1,0:T(8,128)(2,1)S(1)} %fusion), channel_id=1, source_target_pairs={{4,8},{5,9},{6,10},{7,11},{20,24},{21,25},{22,26},{23,27}} | collective-permute-start | bytes 1572872 | tf_op jit(solution)/shard_map/ppermute | solution.py:557
  70.8 0.7 collective-permute-start.15
  71.5 13.4 %copy-start.10 = (f32[1024,512]{1,0:T(8,128)S(1)}, f32[1024,512]{1,0:T(8,128)}, u32[]{:S(2)}) copy-start(f32[1024,512]{1,0:T(8,128)} %copy-done.9) | copy-start | bytes 6291460
  71.5 13.4 %copy-start.12 = (bf16[1024,128]{1,0:T(8,128)(2,1)S(1)}, bf16[1024,128]{1,0:T(8,128)(2,1)}, u32[]{:S(2)}) copy-start(bf16[1024,128]{1,0:T(8,128)(2,1)} %down.1) | copy-start | bytes 786436
  74.2 25.3 %all-to-all-start = ((bf16[16,32,256]{2,1,0:T(8,128)(2,1)}), bf16[16,32,256]{2,1,0:T(8,128)(2,1)S(1)}, u32[]{:S(2)}, u32[]{:S(2)}) async-start(bf16[16,32,256]{2,1,0:T(8,128)(2,1)} %head_features.1), calls=%async_computation | async-start | bytes 524288 | tf_op jit(solution)/shard_map/all_to_all | solution.py:586
  85.0 3.4 %copy-start.2 = (bf16[1024,4096]{1,0:T(8,128)(2,1)S(1)}, bf16[1024,4096]{1,0:T(8,128)(2,1)}, u32[]{:S(2)}) copy-start(bf16[1024,4096]{1,0:T(8,128)(2,1)} %weight.7) | copy-start | bytes 25165828
  88.3 3.4 %copy-start.4 = (bf16[1024,4096]{1,0:T(8,128)(2,1)S(1)}, bf16[1024,4096]{1,0:T(8,128)(2,1)}, u32[]{:S(2)}) copy-start(bf16[1024,4096]{1,0:T(8,128)(2,1)} %copy-done.3) | copy-start | bytes 25165828
  (2 other events, 2.3 us)

commit v4 on v3

v4 whole, which is shorter than its diff:
```python
import functools

import jax
import jax.numpy as jnp
from jax import lax
from jax.experimental import pallas as pl
from jax.experimental.pallas import tpu as pltpu
from jax.sharding import PartitionSpec as P

TOUCH = 8
ADAPTER_SCALE = 4.0
BETA_ONE = 0.9
BETA_TWO = 0.999
EPSILON = 1e-08
MIB = 2**20
BF16 = jnp.bfloat16
F32 = jnp.float32

HBM = pl.BlockSpec(memory_space=pltpu.HBM)
VMEM = pl.BlockSpec(memory_space=pltpu.VMEM)
SMEM = pl.BlockSpec(memory_space=pltpu.SMEM)


def dot_trailing(left, right):
    return lax.dot_general(left, right, (((1,), (1,)), ((), ())), preferred_element_type=F32)


def call(kernel, out_shape, in_specs, out_specs, scratch, flops, nbytes, name, vmem=32):
    return pl.pallas_call(
        kernel,
        out_shape=out_shape,
        in_specs=in_specs,
        out_specs=out_specs,
        scratch_shapes=scratch,
        compiler_params=pltpu.CompilerParams(vmem_limit_bytes=vmem * MIB),
        cost_estimate=pl.CostEstimate(flops=flops, bytes_accessed=nbytes, transcendentals=0),
        name=name,
    )


def pieces_kernel(source_in, source_grad, down, up, *rest):
    *outs, rows_in, rows_grad, down_buf, up_buf, sem, weight_sem = rest
    size = len(outs)
    place = lax.axis_index("tensor")
    rows, width = rows_in.shape[1:]
    rank = up_buf.shape[0]

    def copies(k):
        here = pl.ds(pl.multiple_of(lax.rem(place + k, size) * rows, rows), rows)
        there = pl.ds(pl.multiple_of(place * width, width), width)
        return (
            pltpu.make_async_copy(source_in.at[here], rows_in.at[k], sem.at[0, k]),
            pltpu.make_async_copy(source_grad.at[here, there], rows_grad.at[k], sem.at[1, k]),
        )

    weights = (
        pltpu.make_async_copy(down, down_buf, weight_sem.at[0]),
        pltpu.make_async_copy(up, up_buf, weight_sem.at[1]),
    )
    order = list(range(1, size)) + [0]
    for c in weights:
        c.start()
    for k in order:
        for c in copies(k):
            c.start()
    for c in weights:
        c.wait()
    for k in order:
        wait_in, wait_grad = copies(k)
        wait_in.wait()
        product = jnp.dot(rows_in[k], down_buf[...], preferred_element_type=F32)
        outs[k][:rank, :] = product.T.astype(BF16)
        wait_grad.wait()
        product = dot_trailing(rows_grad[k], up_buf[...])
        outs[k][rank:, :] = product.T.astype(BF16)


def rank_pieces(rows_in, rows_grad, down, up, size):
    tokens, width = rows_in.shape
    rank = up.shape[0]
    rows = tokens // size
    return call(
        pieces_kernel,
        [jax.ShapeDtypeStruct((2 * rank, rows), BF16)] * size,
        [HBM] * 4,
        [VMEM] * size,
        [
            pltpu.VMEM((size, rows, width), BF16),
            pltpu.VMEM((size, rows, width), BF16),
            pltpu.VMEM(down.shape, BF16),
            pltpu.VMEM(up.shape, BF16),
            pltpu.SemaphoreType.DMA((2, size)),
            pltpu.SemaphoreType.DMA((2,)),
        ],
        4 * tokens * width * rank,
        4 * tokens * width,
        "rank_pieces",
        62,
    )(rows_in, rows_grad, down, up)


def shifted(value, axis, shift):
    size = lax.axis_size(axis)
    return lax.ppermute(value, axis, [(i, (i + shift) % size) for i in range(size)])


def scatter(pieces):
    return [shifted(piece, "tensor", k) if k else piece for k, piece in enumerate(pieces)]


def total_of(terms):
    total = terms[0].astype(F32)
    for term in terms[1:]:
        total = total + term.astype(F32)
    return total.astype(BF16)


def gather_pieces(total):
    size = lax.axis_size("tensor")
    return [total] + [shifted(total, "tensor", k) for k in range(1, size)]


def example_scalars(bounds, block):
    low = lax.axis_index("seq") * block
    count = bounds.shape[2]
    first = jnp.int32(-1)
    last = jnp.int32(-1)
    for e in range(count):
        start = bounds[0, 0, e]
        first = first + (start <= low).astype(jnp.int32)
        last = last + (start <= low + block - 1).astype(jnp.int32)
    return low, first, last


def place_pieces(pieces, m, low_scratch):
    size = len(pieces)
    place = lax.axis_index("tensor")
    rank = low_scratch.shape[1]
    first = (1 - m) * rank
    for k, piece in enumerate(pieces):
        low_scratch[lax.rem(place + size - k, size)] = piece[first : first + rank, :]


def masked(low_piece, offset, start, end):
    tokens = offset + lax.broadcasted_iota(jnp.int32, low_piece.shape, 1)
    return jnp.where((tokens >= start) & (tokens < end), low_piece.astype(F32), 0.0).astype(BF16)


def tails_kernel(size, bounds, rows_in, rows_grad, *rest):
    pieces = rest[:size]
    out, low_scratch, acc = rest[size:]
    tokens, width = rows_in.shape
    rows = tokens // size
    low, _, last = example_scalars(bounds, tokens)
    start = bounds[0, 0, last]
    for m, source in enumerate((rows_in, rows_grad)):
        place_pieces(pieces, m, low_scratch)

        def chunk(c):
            left = masked(low_scratch[c], low + c * rows, start, low + tokens)
            return jnp.dot(left, source[c * rows : (c + 1) * rows, :], preferred_element_type=F32)

        acc[...] = chunk(size - 1)
        for c in range(size - 1):

            @pl.when(start < low + (c + 1) * rows)
            def _():
                acc[...] += chunk(c)

        out[m] = (ADAPTER_SCALE * acc[...]).astype(BF16)


def tail_parts(bounds, rows_in, rows_grad, low):
    size = len(low)
    rank, rows = low[0].shape[0] // 2, low[0].shape[1]
    tokens, width = rows_in.shape
    return call(
        functools.partial(tails_kernel, size),
        jax.ShapeDtypeStruct((2, rank, width), BF16),
        [SMEM] + [VMEM] * (2 + size),
        VMEM,
        [pltpu.VMEM((size, rank, rows), BF16), pltpu.VMEM((rank, width), F32)],
        4 * tokens * width * rank,
        4 * tokens * width,
        "tail_parts",
    )(bounds, rows_in, rows_grad, *low)


def normalize(grads, first_moment, second_moment):
    first = first_moment + (1.0 - BETA_ONE) * grads
    second = second_moment + ((1.0 - BETA_TWO) * grads) * grads
    guess = lax.rsqrt(second)
    below = second * guess + EPSILON
    return first * (guess * (2.0 - below * guess))


def split_two(value):
    high = value.astype(BF16)
    return high, (value - high.astype(F32)).astype(BF16)


def project_rank(rank_side, normed):
    both = jnp.dot(
        jnp.concatenate(split_two(rank_side[...]), axis=0), normed, preferred_element_type=F32
    )
    half = both.shape[0] // 2
    return both[:half] + both[half:]


def project_width(value, right):
    high, low = split_two(value)
    return jnp.dot(high, right, preferred_element_type=F32) + jnp.dot(
        low, right, preferred_element_type=F32
    )


def right_rows_copy(width_side, right, sem):
    rows = right.shape[0]
    first = pl.multiple_of(lax.axis_index("tensor") * rows, rows)
    return pltpu.make_async_copy(width_side.at[pl.ds(first, rows)], right, sem)


def slots_kernel(m, size, bounds, owner, source, moments, rank_side, width_side, *rest):
    pieces = rest[:size]
    out, head, low_scratch, acc, normed, ranked, wide, right, sem = rest[size:]
    right_copy = right_rows_copy(width_side, right, sem)
    right_copy.start()
    tokens, width = source.shape
    rank = head.shape[0]
    rows = tokens // size
    low, first, last = example_scalars(bounds, tokens)
    count = bounds.shape[2]
    place_pieces(pieces, m, low_scratch)
    step = 16

    def slot(j):
        return jnp.minimum(first + j, count - 1)

    def ends_here(j):
        return (first + j <= last) & (bounds[0, 1, slot(j)] <= low + tokens)

    @pl.loop(0, TOUCH)
    def _(j):
        start, end = bounds[0, 0, slot(j)], bounds[0, 1, slot(j)]

        @pl.when(ends_here(j) | (j == 0))
        def _():
            for c in range(size):
                begin = low + c * rows

                @pl.when((start < begin + rows) & (end > begin))
                def _():
                    left = masked(low_scratch[c], begin, start, end)
                    term = jnp.dot(
                        left, source[c * rows : (c + 1) * rows, :], preferred_element_type=F32
                    )
                    fresh = (start >= begin) | (c == 0)
                    acc[...] = jnp.where(fresh, 0.0, acc[...]) + term

            @pl.when(j == 0)
            def _():
                head[...] = (ADAPTER_SCALE * acc[...]).astype(BF16)

            @pl.when(j > 0)
            def _():
                for r in range(0, rank, step):
                    normed[r : r + step, :] = normalize(
                        ADAPTER_SCALE * acc[r : r + step, :],
                        moments[0, m, r : r + step, :],
                        moments[1, m, r : r + step, :],
                    ).astype(BF16)
                ranked[j] = project_rank(rank_side, normed[...])

    right_copy.wait()
    wide[...] = project_width(ranked[...].reshape(-1, width), right[...]).reshape(wide.shape)
    out[...] = jnp.zeros_like(out)
    for j in range(1, TOUCH):

        @pl.when(ends_here(j))
        def _():
            out[owner[0, slot(j)]] = wide[j].astype(BF16)


def slot_features(
    m, bounds, owner, source, moments, rank_side, width_side, pieces, name
):
    size = len(pieces)
    rank, rows = pieces[0].shape[0] // 2, pieces[0].shape[1]
    tokens, width = source.shape
    lines = rank_side.shape[0]
    columns = width_side.shape[1]
    return call(
        functools.partial(slots_kernel, m, size),
        [
            jax.ShapeDtypeStruct((owner.shape[1], lines, columns), BF16),
            jax.ShapeDtypeStruct((rank, width), BF16),
        ],
        [SMEM, SMEM, VMEM, VMEM, VMEM, HBM] + [VMEM] * size,
        [VMEM, VMEM],
        [
            pltpu.VMEM((size, rank, rows), BF16),
            pltpu.VMEM((rank, width), F32),
            pltpu.VMEM((rank, width), BF16),
            pltpu.VMEM((TOUCH, lines, width), F32),
            pltpu.VMEM((TOUCH, lines, columns), F32),
            pltpu.VMEM((width, columns), BF16),
            pltpu.SemaphoreType.DMA,
        ],
        2 * tokens * width * rank * TOUCH,
        4 * tokens * width,
        name,
    )(bounds, owner, source, moments, rank_side, width_side, *pieces)


def head_kernel(
    hops, block, bounds, owner, filled_grad, filled_in, head_grad, head_in, moments, rank_side, width_side, *rest
):
    arrived = rest[:hops]
    out, normed, ranked, right, sem = rest[hops:]
    right_copy = right_rows_copy(width_side, right, sem)
    right_copy.start()
    low, first, last = example_scalars(bounds, block)
    rank = head_in.shape[0]
    lines = rank_side.shape[0]
    continued = (bounds[0, 0, first] < low).astype(F32)
    step = 16
    out[:, :lines] = filled_grad[...]
    out[:, lines:] = filled_in[...]
    ends = bounds[0, 1, first] <= low + block

    @pl.when(ends)
    def _():
        for m, head in enumerate((head_grad, head_in)):
            for r in range(0, rank, step):
                here = slice(r, r + step)
                incoming = arrived[0][m, here, :].astype(F32)
                for k in range(1, hops):
                    incoming = incoming + arrived[k][m, here, :].astype(F32)
                normed[here, :] = normalize(
                    head[here, :].astype(F32) + continued * incoming,
                    moments[0, m, here, :],
                    moments[1, m, here, :],
                ).astype(BF16)
            ranked[m * lines : (m + 1) * lines, :] = project_rank(rank_side, normed[...])

    right_copy.wait()

    @pl.when(ends)
    def _():
        out[owner[0, first]] = project_width(ranked[...], right[...]).astype(BF16)


def head_features(
    bounds, owner, filled_grad, filled_in, head_grad, head_in, moments, rank_side, width_side, arrived, block
):
    hops = len(arrived)
    rank, width = head_in.shape
    slots, lines, columns = filled_in.shape
    return call(
        functools.partial(head_kernel, hops, block),
        jax.ShapeDtypeStruct((slots, 2 * lines, columns), BF16),
        [SMEM, SMEM] + [VMEM] * 6 + [HBM] + [VMEM] * hops,
        VMEM,
        [
            pltpu.VMEM((rank, width), BF16),
            pltpu.VMEM((2 * lines, width), F32),
            pltpu.VMEM((width, columns), BF16),
            pltpu.SemaphoreType.DMA,
        ],
        2 * width * 2 * rank * 4 * lines,
        8 * rank * width,
        "head_features",
    )(
        bounds,
        owner,
        filled_grad,
        filled_in,
        head_grad,
        head_in,
        moments,
        rank_side,
        width_side,
        *arrived,
    )


def depth_chunks(depth):
    return [0, depth // 8, depth // 2, depth]


def operand_copies(source, weight, held, weight_buf, sem, column):
    edges = depth_chunks(held.shape[1])
    pairs = []
    for c, (begin, end) in enumerate(zip(edges, edges[1:])):
        depth = pl.ds(begin, end - begin)
        columns = pl.ds(column, weight_buf.shape[0])
        pair = (
            pltpu.make_async_copy(source.at[:, depth], held.at[:, depth], sem.at[0, c]),
            pltpu.make_async_copy(weight.at[columns, depth], weight_buf.at[:, depth], sem.at[1, c]),
        )
        for copy in pair:
            copy.start()
        pairs.append((slice(begin, end), pair))
    return pairs


def chunked_product(pairs, held, weight_buf, out):
    for c, (depth, pair) in enumerate(pairs):
        for copy in pair:
            copy.wait()
        term = dot_trailing(held[:, depth], weight_buf[:, depth])
        out[...] = term if c == 0 else out[...] + term


def first_kernel(source, weight, out, held, weight_buf, sem):
    chunked_product(
        operand_copies(source, weight, held, weight_buf, sem, 0), held, weight_buf, out
    )


def second_kernel(size, source, weight, down, done, *rest):
    pieces = rest[:size]
    out, result, acc, low_rows, held, weight_buf, sem, out_sem = rest[size:]
    tokens, width = result.shape
    split = done.shape[1]
    pairs = operand_copies(source, weight, held, weight_buf, sem, split)
    place = lax.axis_index("tensor")
    rows = tokens // size
    rank = low_rows.shape[1]
    for k, piece in enumerate(pieces):
        block = lax.rem(place + size - k, size)
        low_rows[pl.ds(pl.multiple_of(block * rows, rows), rows), :] = (
            piece[rank:, :].astype(F32).T.astype(BF16)
        )

    def out_copy(begin, end, k):
        here = pl.ds(begin, end - begin)
        return pltpu.make_async_copy(result.at[:, here], out.at[:, here], out_sem.at[k])

    def finish(base, begin, end, k):
        extra = dot_trailing(low_rows[...], down[begin:end, :])
        result[:, begin:end] = (base[...] + ADAPTER_SCALE * extra).astype(BF16)
        out_copy(begin, end, k).start()

    finish(done, 0, split, 0)
    chunked_product(pairs, held, weight_buf, acc)
    finish(acc, split, width, 1)
    out_copy(0, split, 0).wait()
    out_copy(split, width, 1).wait()


def first_product(source, weight, split):
    tokens, depth = source.shape
    return call(
        first_kernel,
        jax.ShapeDtypeStruct((tokens, split), F32),
        [HBM, HBM],
        VMEM,
        [
            pltpu.VMEM((tokens, depth), BF16),
            pltpu.VMEM((split, depth), BF16),
            pltpu.SemaphoreType.DMA((2, len(depth_chunks(depth)) - 1)),
        ],
        2 * tokens * depth * split,
        2 * depth * (tokens + split),
        "first_product",
        56,
    )(source, weight)


def second_product(source, weight, down, done, pieces):
    tokens, depth = source.shape
    width, rank = down.shape
    rest = width - done.shape[1]
    size = len(pieces)
    return call(
        functools.partial(second_kernel, size),
        jax.ShapeDtypeStruct((tokens, width), BF16),
        [HBM, HBM] + [VMEM] * (2 + size),
        HBM,
        [
            pltpu.VMEM((tokens, width), BF16),
            pltpu.VMEM((tokens, rest), F32),
            pltpu.VMEM((tokens, rank), BF16),
            pltpu.VMEM((tokens, depth), BF16),
            pltpu.VMEM((rest, depth), BF16),
            pltpu.SemaphoreType.DMA((2, len(depth_chunks(depth)) - 1)),
            pltpu.SemaphoreType.DMA((2,)),
        ],
        2 * tokens * depth * rest,
        2 * depth * (tokens + rest),
        "second_product",
        56,
    )(source, weight, down, done, *pieces)


def gather_rows(value, axis, dim):
    size = lax.axis_size(axis)
    if size != 2:
        return lax.all_gather(value, axis, axis=dim, tiled=True)
    other = shifted(value, axis, 1)
    low = lax.axis_index(axis) == 0
    return jnp.concatenate([jnp.where(low, value, other), jnp.where(low, other, value)], axis=dim)


def per_device(
    attention_output_rows,
    projection_result_gradient,
    adapter_down_weight,
    adapter_up_weight,
    output_projection_weight,
    adam_first_moments,
    adam_second_moments,
    rank_side_projection,
    width_side_projection,
    bounds,
    example_owner_slot,
):
    packs, blk, width_local = attention_output_rows.shape
    assert packs == 1
    width = projection_result_gradient.shape[2]
    size = lax.axis_size("tensor")
    rows_in = attention_output_rows.reshape(blk, width_local)
    rows_grad = projection_result_gradient.reshape(blk, width)

    pieces = rank_pieces(rows_in, rows_grad, adapter_down_weight, adapter_up_weight, size)
    stacked = jnp.stack([adam_first_moments, adam_second_moments]).astype(BF16)
    betas = jnp.array([BETA_ONE, BETA_TWO], F32).reshape(2, 1, 1, 1)
    moments = betas * gather_rows(stacked, "dp", 2).astype(F32)
    first_token = lax.axis_index("seq") * blk
    starts, ends = bounds[0, 0], bounds[0, 1]
    spans = jnp.any((starts < first_token) & (ends >= first_token + blk)).astype(F32)

    columns_grad = lax.dynamic_slice_in_dim(
        rows_grad, lax.axis_index("tensor") * width_local, width_local, 1
    )
    done = first_product(rows_grad, output_projection_weight, width_local // 2)
    sent, done = lax.optimization_barrier((scatter(pieces), done))
    low, moments, spans, columns_grad = lax.optimization_barrier(
        (gather_pieces(total_of(sent)), moments, spans, columns_grad)
    )
    tails = tail_parts(bounds, rows_in, columns_grad, low)
    shared = (rank_side_projection, width_side_projection)

    def hop(outgoing, k):
        return lax.ppermute(outgoing, "seq", [(k, k + 1)])

    def onward(arrived):
        return (tails.astype(F32) + spans * arrived.astype(F32)).astype(BF16)

    arrived = [hop(tails, 0)]
    outgoing, columns_grad = lax.optimization_barrier((onward(arrived[0]), columns_grad))
    arrived.append(hop(outgoing, 1))
    filled_in, head_in = slot_features(
        1, bounds, example_owner_slot, columns_grad, moments, *shared, low, "slots_in"
    )
    arrived[1], rows_in, head_in = lax.optimization_barrier((arrived[1], rows_in, head_in))
    for k in range(2, lax.axis_size("seq") - 1):
        arrived.append(hop(onward(arrived[-1]), k))
    filled_grad, head_grad = slot_features(
        0, bounds, example_owner_slot, rows_in, moments, *shared, low, "slots_grad"
    )
    arrived, head_grad = lax.optimization_barrier((arrived, head_grad))
    buffer = head_features(
        bounds,
        example_owner_slot,
        filled_grad,
        filled_in,
        head_grad,
        head_in,
        moments,
        *shared,
        arrived,
        blk,
    )
    arrived = lax.all_to_all(buffer, ("seq", "tensor"), split_axis=0, concat_axis=0, tiled=True)
    features = jnp.sum(arrived.astype(F32), axis=0).reshape(1, 1, -1)
    out = second_product(
        rows_grad,
        output_projection_weight,
        adapter_down_weight,
        done,
        low,
    )
    return (out.reshape(attention_output_rows.shape), features)


def solution(mesh):
    return jax.shard_map(
        per_device,
        mesh=mesh,
        in_specs=(
            P("dp", "seq", "tensor"),
            P("dp", "seq", None),
            P("tensor", None),
            P(None, "tensor"),
            P("tensor", None),
            P(None, "dp", "tensor"),
            P(None, "dp", "tensor"),
            P(),
            P(),
            P("dp", None, None),
            P("dp", None),
        ),
        out_specs=(P("dp", "seq", "tensor"), P("dp", ("seq", "tensor"), None)),
        check_vma=False,
    )
```

time: 101 us -> 79.7 us (0.79)
  local copies, waits for them, and re-layouts: 21.4 us -> 2.52 us
  starting transfers between devices: 33.3 us -> 26.2 us
  waiting for transfers between devices: 6.03 us -> 8.94 us
  Pallas kernels: 35.1 us -> 37.3 us
    unnamed x34 -> x26, local copies, waits for them, and re-layouts: 20.7 us -> 0.07 us
    ppermute x13 -> x7, starting transfers between devices: 19.9 us -> 12.4 us  [shifted(): lax.ppermute(value, axis, [(i, (i + shift) % size) for i in range(size)])]
    pallas_call x1, Pallas kernels: 7.68 us -> 10.6 us  [second_product(): call(functools.partial(second_kernel, size), jax.ShapeDtypeStruct((tokens...]
    dynamic_slice x0 -> x1, local copies, waits for them, and re-layouts: none -> 1.8 us  [per_device(): lax.dynamic_slice_in_dim(rows_grad, lax.axis_index('tensor') * width_loca...]
    ppermute x3, waiting for transfers between devices: 0.01 us -> 1.49 us  [hop(): return lax.ppermute(outgoing, 'seq', [(k, k + 1)])]
    ppermute x13 -> x7, waiting for transfers between devices: 6.02 us -> 7.44 us  [shifted(): lax.ppermute(value, axis, [(i, (i + shift) % size) for i in range(size)])]
    another operation x2, other arithmetic: 1.32 us -> 0.12 us  [per_device(): stacked = jnp.stack([adam_first_moments, adam_second_moments]).astype(BF16)]
    pallas_call x3 -> x2, Pallas kernels: 15.6 us -> 15.2 us  [the longest x1 8.45 us: first_product(): call(first_kernel, jax.ShapeDtypeStruct((tokens, split), F32), [HBM, HBM]...]
  transfers between devices with their start and end apart: 17 -> 11, of which waited for: 4 -> 3; matrix products, arithmetic and copies ran while one was open for 2% -> 4% of each run, Pallas kernels for 30% -> 34%
where the time goes in v4:
time: 79.7 us; the launch traced here: 78.3 us
  Pallas kernels  37.3 us (47%)
  starting transfers between devices  26.2 us (33%)
  waiting for transfers between devices  8.94 us (11%)
  local copies, waits for them, and re-layouts  2.52 us (3%)
  other arithmetic  1.68 us (2%)
  between operations  1.66 us (2%)
    ppermute x7, starting transfers between devices, shifted(): lax.ppermute(value, axis, [(i, (i + shift) % size) for i in range(size)])  12.4 us
    pallas_call x1, Pallas kernels, second_product(): call(functools.partial(second_kernel, size), jax.ShapeDtypeStruct((tokens...  10.6 us
    all_to_all x1, starting transfers between devices, per_device(): lax.all_to_all(buffer, ('seq', 'tensor'), split_axis=0, concat_axis=0, ti...  10.3 us
    pallas_call x1, Pallas kernels, first_product(): call(first_kernel, jax.ShapeDtypeStruct((tokens, split), F32), [HBM, HBM]...  8.45 us
    pallas_call x2, Pallas kernels, slot_features(): call(functools.partial(slots_kernel, m, size), [jax.ShapeDtypeStruct((own...  7.83 us
    ppermute x7, waiting for transfers between devices, shifted(): lax.ppermute(value, axis, [(i, (i + shift) % size) for i in range(size)])  7.44 us
    pallas_call x1, Pallas kernels, rank_pieces(): call(pieces_kernel, [jax.ShapeDtypeStruct((2 * rank, rows), BF16)] * size...  6.74 us
    ppermute x3, starting transfers between devices, hop(): return lax.ppermute(outgoing, 'seq', [(k, k + 1)])  3.51 us
  transfers between devices with their start and end apart: 11, of which 3 were waited for; matrix products, arithmetic and copies ran while one was open for 4% of the time, Pallas kernels for 34%

profile of v4, /device:TPU:0, one launch (start us, length us, event | category | flops | bytes accessed | tf_op | source)
XLA Modules:
  0.0 78.3 jit_solution(16603204461766951780)
XLA Ops:
  0.7 6.7 %rank_pieces.1 = (bf16[256,256]{1,0:T(8,128)(2,1)}, bf16[256,256]{1,0:T(8,128)(2,1)}, bf16[256,256]{1,0:T(8,128)(2,1)}, bf16[256,256]{1,0:T(8,128)(2,1)}) custom-call(bf16[1024,1024]{1,0:T(8,128)(2,1)} %bitcast.9, bf16[1024,4096]{1,0:T(8,128)(2,1)} %bitcast.12, bf16[1024,128]{1,0:T(8,128)(2,1)} %down.3, bf16[128,1024]{1,0:T(8,128)(2,1)} %up.1), custom_call_target="tpu_custom_call" | custom-call | flops 536870912 | bytes 4194304 | tf_op jit(solution)/shard_map/rank_pieces/pallas_call | solution.py:82
  7.4 3.1 %collective-permute-start = (bf16[256,256]{1,0:T(8,128)(2,1)}, bf16[256,256]{1,0:T(8,128)(2,1)S(1)}, u32[]{:S(2)}, u32[]{:S(2)}) collective-permute-start(bf16[256,256]{1,0:T(8,128)(2,1)} %get-tuple-element.32), channel_id=1, source_target_pairs={{0,1},{1,2},{2,3},{3,0},{4,5},{5,6},{6,7},{7,4},{8,9},{9,10},{10,1... | collective-permute-start | bytes 393224 | tf_op jit(solution)/shard_map/ppermute | solution.py:104
  10.5 2.6 %collective-permute-start.1 = (bf16[256,256]{1,0:T(8,128)(2,1)}, bf16[256,256]{1,0:T(8,128)(2,1)S(1)}, u32[]{:S(2)}, u32[]{:S(2)}) collective-permute-start(bf16[256,256]{1,0:T(8,128)(2,1)} %get-tuple-element.33), channel_id=1, source_target_pairs={{0,2},{1,3},{2,0},{3,1},{4,6},{5,7},{6,4},{7,5},{8,10},{9,11},{10,... | collective-permute-start | bytes 393224 | tf_op jit(solution)/shard_map/ppermute | solution.py:104
  13.1 1.3 %collective-permute-start.2 = (bf16[256,256]{1,0:T(8,128)(2,1)}, bf16[256,256]{1,0:T(8,128)(2,1)S(1)}, u32[]{:S(2)}, u32[]{:S(2)}) collective-permute-start(bf16[256,256]{1,0:T(8,128)(2,1)} %get-tuple-element.34), channel_id=1, source_target_pairs={{0,3},{1,0},{2,1},{3,2},{4,7},{5,4},{6,5},{7,6},{8,11},{9,8},{10,9... | collective-permute-start | bytes 393224 | tf_op jit(solution)/shard_map/ppermute | solution.py:104
  14.4 0.1 convert_bitcast_fusion
  14.5 0.1 pad_maximum_fusion
  14.6 1.6 %collective-permute-start.6 = (bf16[2,2,64,1024]{3,2,1,0:T(8,128)(2,1)S(1)}, bf16[2,2,64,1024]{3,2,1,0:T(8,128)(2,1)S(1)}, u32[]{:S(2)}, u32[]{:S(2)}) collective-permute-start(bf16[2,2,64,1024]{3,2,1,0:T(8,128)(2,1)S(1)} %pad_maximum_fusion), channel_id=1, source_target_pairs={{0,16},{16,0},{1,17},{17,1},{2,18},{18,2},{3,19},{19,3},{4,20},{20... | collective-permute-start | bytes 1572872 | tf_op jit(solution)/shard_map/ppermute | solution.py:104
  16.1 8.5 %first_product.1.done = f32[1024,512]{1,0:T(8,128)} custom-call(bf16[1024,4096]{1,0:T(8,128)(2,1)} %bitcast.13, bf16[1024,4096]{1,0:T(8,128)(2,1)} %weight.3), custom_call_target="tpu_custom_call" | custom-call | flops 4294967296 | bytes 12582912 | tf_op jit(solution)/shard_map/first_product/pallas_call | solution.py:454
  24.6 0.6 and_reduce_fusion
  25.9 1.8 %dynamic-slice_bitcast_fusion.rows_grad.source = bf16[1024,1024]{1,0:T(8,128)(2,1)S(1)} fusion(bf16[1,1024,4096]{2,1,0:T(8,128)(2,1)} %param.13, s32[]{:T(128)S(6)} %select_n.18), kind=kLoop, calls=%fused_computation | loop fusion | bytes 4194308 | tf_op jit(solution)/shard_map/dynamic_slice | solution.py:534
  27.7 0.0 copy-start.12
  27.8 0.1 add_convert_fusion.rest_0_
  27.9 0.7 collective-permute-start.3
  28.6 0.3 collective-permute-start.4
  28.9 2.8 %collective-permute-start.5 = (bf16[256,256]{1,0:T(8,128)(2,1)S(1)}, bf16[256,256]{1,0:T(8,128)(2,1)S(1)}, u32[]{:S(2)}, u32[]{:S(2)}) collective-permute-start(bf16[256,256]{1,0:T(8,128)(2,1)S(1)} %add_convert_fusion.rest_0_), channel_id=1, source_target_pairs={{0,3},{1,0},{2,1},{3,2},{4,7},{5,4},{6,5},{7,6},{8,11},{9,8},{10,9... | collective-permute-start | bytes 393224 | tf_op jit(solution)/shard_map/ppermute | solution.py:104
  31.7 0.1 broadcast_select_fusion.1
  31.8 0.3 convert_multiply_fusion.moments
  32.2 4.0 %collective-permute-done.3.rest_1_ = bf16[256,256]{1,0:T(8,128)(2,1)S(1)} collective-permute-done((bf16[256,256]{1,0:T(8,128)(2,1)S(1)}, bf16[256,256]{1,0:T(8,128)(2,1)S(1)}, u32[]{:S(2)}, u32[]{:S(2)}) %collective-permute-start.3) | collective-permute-done | bytes 131104 | tf_op jit(solution)/shard_map/ppermute | solution.py:104
  36.2 3.4 %collective-permute-done.4.rest_2_ = bf16[256,256]{1,0:T(8,128)(2,1)S(1)} collective-permute-done((bf16[256,256]{1,0:T(8,128)(2,1)S(1)}, bf16[256,256]{1,0:T(8,128)(2,1)S(1)}, u32[]{:S(2)}, u32[]{:S(2)}) %collective-permute-start.4) | collective-permute-done | bytes 131104 | tf_op jit(solution)/shard_map/ppermute | solution.py:104
  39.7 1.1 %tail_parts.1 = bf16[2,128,1024]{2,1,0:T(8,128)(2,1)S(1)} custom-call(s32[1,2,16]{2,1,0:T(2,128)S(1)} %copy-done.6, bf16[1024,1024]{1,0:T(8,128)(2,1)S(1)} %bitcast.10, bf16[1024,1024]{1,0:T(8,128)(2,1)S(1)} %dynamic-slice_bitcast_fusion.rows_grad.source, bf16[256,256]{1,0:T(8,128)(2,1)S(1)} %add_convert_fusion.rest_0_, ...), custom_call_target="tpu_custom_call" | custom-call | flops 536870912 | bytes 4194304 | tf_op jit(solution)/shard_map/tail_parts/pallas_call | solution.py:177
  40.8 2.1 %collective-permute-start.7 = (bf16[2,128,1024]{2,1,0:T(8,128)(2,1)S(1)}, bf16[2,128,1024]{2,1,0:T(8,128)(2,1)S(1)}, u32[]{:S(2)}, u32[]{:S(2)}) collective-permute-start(bf16[2,128,1024]{2,1,0:T(8,128)(2,1)S(1)} %tail_parts.1), channel_id=1, source_target_pairs={{0,4},{1,5},{2,6},{3,7},{16,20},{17,21},{18,22},{19,23}} | collective-permute-start | bytes 1572872 | tf_op jit(solution)/shard_map/ppermute | solution.py:546
  42.9 1.5 %collective-permute-done.7.rest_0_ = bf16[2,128,1024]{2,1,0:T(8,128)(2,1)S(1)} collective-permute-done((bf16[2,128,1024]{2,1,0:T(8,128)(2,1)S(1)}, bf16[2,128,1024]{2,1,0:T(8,128)(2,1)S(1)}, u32[]{:S(2)}, u32[]{:S(2)}) %collective-permute-start.7) | collective-permute-done | bytes 524320 | tf_op jit(solution)/shard_map/ppermute | solution.py:546
  44.4 0.2 fusion
  44.6 0.7 collective-permute-start.8
  45.3 3.9 %slots_in.1 = (bf16[16,16,256]{2,1,0:T(8,128)(2,1)S(1)}, bf16[128,1024]{1,0:T(8,128)(2,1)S(1)}) custom-call(s32[1,2,16]{2,1,0:T(2,128)S(1)} %copy-done.6, s32[1,16]{1,0:T(1,128)S(1)} %copy-done.8, bf16[1024,1024]{1,0:T(8,128)(2,1)S(1)} %dynamic-slice_bitcast_fusion.rows_grad.source, f32[2,2,128,1024]{3,2,1,0:T(8,128)S(1)} %convert_multiply_fusion.moments, ...), custom_call_target="tpu_custom_call" | custom-call | flops 2147483648 | bytes 4194304 | tf_op jit(solution)/shard_map/slots_in/pallas_call | solution.py:292
  49.2 0.2 fusion.1
  49.5 0.7 collective-permute-start.9
  50.2 3.9 %slots_grad.1 = (bf16[16,16,256]{2,1,0:T(8,128)(2,1)S(1)}, bf16[128,1024]{1,0:T(8,128)(2,1)S(1)}) custom-call(s32[1,2,16]{2,1,0:T(2,128)S(1)} %copy-done.6, s32[1,16]{1,0:T(1,128)S(1)} %copy-done.8, bf16[1024,1024]{1,0:T(8,128)(2,1)S(1)} %bitcast.11, f32[2,2,128,1024]{3,2,1,0:T(8,128)S(1)} %convert_multiply_fusion.moments, f32[16,128]{1,0:T(8,128)S(1)} %copy-done.7, ...), custom_call_target="tpu_custom_call" | custom-call | flops 2147483648 | bytes 4194304 | tf_op jit(solution)/shard_map/slots_grad/pallas_call | solution.py:292
  54.1 2.7 %head_features.1 = bf16[16,32,256]{2,1,0:T(8,128)(2,1)} custom-call(s32[1,2,16]{2,1,0:T(2,128)S(1)} %copy-done.6, s32[1,16]{1,0:T(1,128)S(1)} %copy-done.8, bf16[16,16,256]{2,1,0:T(8,128)(2,1)S(1)} %get-tuple-element.51.filled_grad, bf16[16,16,256]{2,1,0:T(8,128)(2,1)S(1)} %get-tuple-element.52.filled_in, bf16[128,1024]{1,0:T(8,128)(2,1)S(1)} %get-tuple-element.55.head_grad, ...), custom_call_target="tpu_custom_call" | custom-call | flops 33554432 | bytes 1048576 | tf_op jit(solution)/shard_map/head_features/pallas_call | solution.py:359
  56.8 10.3 %all-to-all-start = ((bf16[16,32,256]{2,1,0:T(8,128)(2,1)}), bf16[16,32,256]{2,1,0:T(8,128)(2,1)S(1)}, u32[]{:S(2)}, u32[]{:S(2)}) async-start(bf16[16,32,256]{2,1,0:T(8,128)(2,1)} %head_features.1), calls=%async_computation | async-start | bytes 524288 | tf_op jit(solution)/shard_map/all_to_all | solution.py:576
  67.1 10.6 %second_product.1 = bf16[1024,1024]{1,0:T(8,128)(2,1)} custom-call(bf16[1024,4096]{1,0:T(8,128)(2,1)} %bitcast.14, bf16[1024,4096]{1,0:T(8,128)(2,1)} %weight.3, bf16[1024,128]{1,0:T(8,128)(2,1)} %down.3, f32[1024,512]{1,0:T(8,128)} %first_product.1.done, bf16[256,256]{1,0:T(8,128)(2,1)} %copy-done.2, bf16[256,256]{1,0:T(8,128)(2,1)} %copy-done.3, ...), custom_call_target="tpu_custom_call" | custom-call | flops 4294967296 | bytes 12582912 | tf_op jit(solution)/shard_map/second_product/pallas_call | solution.py:476
  77.7 0.6 reshape.27
  (34 shorter events, 0.1 us)
Async XLA Ops:
  0.6 13.8 %copy-start.9 = (f32[2,64,1024]{2,1,0:T(8,128)S(1)}, f32[2,64,1024]{2,1,0:T(8,128)}, u32[]{:S(2)}) copy-start(f32[2,64,1024]{2,1,0:T(8,128)} %param.18) | copy-start | bytes 1572868
  0.6 13.8 %copy-start.10 = (f32[2,64,1024]{2,1,0:T(8,128)S(1)}, f32[2,64,1024]{2,1,0:T(8,128)}, u32[]{:S(2)}) copy-start(f32[2,64,1024]{2,1,0:T(8,128)} %param.17) | copy-start | bytes 1572868
  7.4 20.3 %collective-permute-start = (bf16[256,256]{1,0:T(8,128)(2,1)}, bf16[256,256]{1,0:T(8,128)(2,1)S(1)}, u32[]{:S(2)}, u32[]{:S(2)}) collective-permute-start(bf16[256,256]{1,0:T(8,128)(2,1)} %get-tuple-element.32), channel_id=1, source_target_pairs={{0,1},{1,2},{2,3},{3,0},{4,5},{5,6},{6,7},{7,4},{8,9},{9,10},{10,1... | collective-permute-start | bytes 393224 | tf_op jit(solution)/shard_map/ppermute | solution.py:104
  10.5 17.3 %collective-permute-start.1 = (bf16[256,256]{1,0:T(8,128)(2,1)}, bf16[256,256]{1,0:T(8,128)(2,1)S(1)}, u32[]{:S(2)}, u32[]{:S(2)}) collective-permute-start(bf16[256,256]{1,0:T(8,128)(2,1)} %get-tuple-element.33), channel_id=1, source_target_pairs={{0,2},{1,3},{2,0},{3,1},{4,6},{5,7},{6,4},{7,5},{8,10},{9,11},{10,... | collective-permute-start | bytes 393224 | tf_op jit(solution)/shard_map/ppermute | solution.py:104
  13.1 14.7 %collective-permute-start.2 = (bf16[256,256]{1,0:T(8,128)(2,1)}, bf16[256,256]{1,0:T(8,128)(2,1)S(1)}, u32[]{:S(2)}, u32[]{:S(2)}) collective-permute-start(bf16[256,256]{1,0:T(8,128)(2,1)} %get-tuple-element.34), channel_id=1, source_target_pairs={{0,3},{1,0},{2,1},{3,2},{4,7},{5,4},{6,5},{7,6},{8,11},{9,8},{10,9... | collective-permute-start | bytes 393224 | tf_op jit(solution)/shard_map/ppermute | solution.py:104
  14.6 10.0 %copy-start.6 = (s32[1,2,16]{2,1,0:T(2,128)S(1)}, s32[1,2,16]{2,1,0:T(2,128)}, u32[]{:S(2)}) copy-start(s32[1,2,16]{2,1,0:T(2,128)} %bounds.7) | copy-start | bytes 388
  14.6 17.2 %collective-permute-start.6 = (bf16[2,2,64,1024]{3,2,1,0:T(8,128)(2,1)S(1)}, bf16[2,2,64,1024]{3,2,1,0:T(8,128)(2,1)S(1)}, u32[]{:S(2)}, u32[]{:S(2)}) collective-permute-start(bf16[2,2,64,1024]{3,2,1,0:T(8,128)(2,1)S(1)} %pad_maximum_fusion), channel_id=1, source_target_pairs={{0,16},{16,0},{1,17},{17,1},{2,18},{18,2},{3,19},{19,3},{4,20},{20... | collective-permute-start | bytes 1572872 | tf_op jit(solution)/shard_map/ppermute | solution.py:104
  25.9 1.9 %copy-start.11 = (bf16[256,256]{1,0:T(8,128)(2,1)S(1)}, bf16[256,256]{1,0:T(8,128)(2,1)}, u32[]{:S(2)}) copy-start(bf16[256,256]{1,0:T(8,128)(2,1)} %get-tuple-element.36) | copy-start | bytes 393220
  27.7 4.1 %copy-start.12 = (f32[2]{0:T(128)S(1)}, f32[2]{0:T(128)}, u32[]{:S(2)}) copy-start(f32[2]{0:T(128)} %constant.26.clone) | copy-start | bytes 28
  27.9 22.3 %copy-start.2 = (bf16[256,256]{1,0:T(8,128)(2,1)}, bf16[256,256]{1,0:T(8,128)(2,1)S(1)}, u32[]{:S(2)}) copy-start(bf16[256,256]{1,0:T(8,128)(2,1)S(1)} %add_convert_fusion.rest_0_) | copy-start | bytes 393220
  27.9 8.3 %collective-permute-start.3 = (bf16[256,256]{1,0:T(8,128)(2,1)S(1)}, bf16[256,256]{1,0:T(8,128)(2,1)S(1)}, u32[]{:S(2)}, u32[]{:S(2)}) collective-permute-start(bf16[256,256]{1,0:T(8,128)(2,1)S(1)} %add_convert_fusion.rest_0_), channel_id=1, source_target_pairs={{0,1},{1,2},{2,3},{3,0},{4,5},{5,6},{6,7},{7,4},{8,9},{9,10},{10,1... | collective-permute-start | bytes 393224 | tf_op jit(solution)/shard_map/ppermute | solution.py:104
  28.6 11.1 %collective-permute-start.4 = (bf16[256,256]{1,0:T(8,128)(2,1)S(1)}, bf16[256,256]{1,0:T(8,128)(2,1)S(1)}, u32[]{:S(2)}, u32[]{:S(2)}) collective-permute-start(bf16[256,256]{1,0:T(8,128)(2,1)S(1)} %add_convert_fusion.rest_0_), channel_id=1, source_target_pairs={{0,2},{1,3},{2,0},{3,1},{4,6},{5,7},{6,4},{7,5},{8,10},{9,11},{10,... | collective-permute-start | bytes 393224 | tf_op jit(solution)/shard_map/ppermute | solution.py:104
  28.9 10.7 %collective-permute-start.5 = (bf16[256,256]{1,0:T(8,128)(2,1)S(1)}, bf16[256,256]{1,0:T(8,128)(2,1)S(1)}, u32[]{:S(2)}, u32[]{:S(2)}) collective-permute-start(bf16[256,256]{1,0:T(8,128)(2,1)S(1)} %add_convert_fusion.rest_0_), channel_id=1, source_target_pairs={{0,3},{1,0},{2,1},{3,2},{4,7},{5,4},{6,5},{7,6},{8,11},{9,8},{10,9... | collective-permute-start | bytes 393224 | tf_op jit(solution)/shard_map/ppermute | solution.py:104
  31.8 7.8 %copy-start = (bf16[1,1024,1024]{2,1,0:T(8,128)(2,1)S(1)}, bf16[1,1024,1024]{2,1,0:T(8,128)(2,1)}, u32[]{:S(2)}) copy-start(bf16[1,1024,1024]{2,1,0:T(8,128)(2,1)} %param.12) | copy-start | bytes 6291460
  32.2 13.1 %copy-start.1 = (bf16[4096,256]{1,0:T(8,128)(2,1)S(1)}, bf16[4096,256]{1,0:T(8,128)(2,1)}, u32[]{:S(2)}) copy-start(bf16[4096,256]{1,0:T(8,128)(2,1)} %width_side.5) | copy-start | bytes 6291460
  32.2 13.1 %copy-start.7 = (f32[16,128]{1,0:T(8,128)S(1)}, f32[16,128]{1,0:T(8,128)}, u32[]{:S(2)}) copy-start(f32[16,128]{1,0:T(8,128)} %rank_side.5) | copy-start | bytes 24580
  32.2 13.1 %copy-start.8 = (s32[1,16]{1,0:T(1,128)S(1)}, s32[1,16]{1,0:T(1,128)}, u32[]{:S(2)}) copy-start(s32[1,16]{1,0:T(1,128)} %owner.5) | copy-start | bytes 196
  36.2 14.0 %copy-start.3 = (bf16[256,256]{1,0:T(8,128)(2,1)}, bf16[256,256]{1,0:T(8,128)(2,1)S(1)}, u32[]{:S(2)}) copy-start(bf16[256,256]{1,0:T(8,128)(2,1)S(1)} %collective-permute-done.3.rest_1_) | copy-start | bytes 393220
  39.7 10.5 %copy-start.4 = (bf16[256,256]{1,0:T(8,128)(2,1)}, bf16[256,256]{1,0:T(8,128)(2,1)S(1)}, u32[]{:S(2)}) copy-start(bf16[256,256]{1,0:T(8,128)(2,1)S(1)} %collective-permute-done.4.rest_2_) | copy-start | bytes 393220
  39.7 10.5 %copy-start.5 = (bf16[256,256]{1,0:T(8,128)(2,1)}, bf16[256,256]{1,0:T(8,128)(2,1)S(1)}, u32[]{:S(2)}) copy-start(bf16[256,256]{1,0:T(8,128)(2,1)S(1)} %collective-permute-done.5.rest_3_) | copy-start | bytes 393220
  40.8 3.6 %collective-permute-start.7 = (bf16[2,128,1024]{2,1,0:T(8,128)(2,1)S(1)}, bf16[2,128,1024]{2,1,0:T(8,128)(2,1)S(1)}, u32[]{:S(2)}, u32[]{:S(2)}) collective-permute-start(bf16[2,128,1024]{2,1,0:T(8,128)(2,1)S(1)} %tail_parts.1), channel_id=1, source_target_pairs={{0,4},{1,5},{2,6},{3,7},{16,20},{17,21},{18,22},{19,23}} | collective-permute-start | bytes 1572872 | tf_op jit(solution)/shard_map/ppermute | solution.py:546
  44.6 4.7 %collective-permute-start.8 = (bf16[2,128,1024]{2,1,0:T(8,128)(2,1)S(1)}, bf16[2,128,1024]{2,1,0:T(8,128)(2,1)S(1)}, u32[]{:S(2)}, u32[]{:S(2)}) collective-permute-start(bf16[2,128,1024]{2,1,0:T(8,128)(2,1)S(1)} %fusion), channel_id=1, source_target_pairs={{4,8},{5,9},{6,10},{7,11},{20,24},{21,25},{22,26},{23,27}} | collective-permute-start | bytes 1572872 | tf_op jit(solution)/shard_map/ppermute | solution.py:546
  49.5 4.7 %collective-permute-start.9 = (bf16[2,128,1024]{2,1,0:T(8,128)(2,1)S(1)}, bf16[2,128,1024]{2,1,0:T(8,128)(2,1)S(1)}, u32[]{:S(2)}, u32[]{:S(2)}) collective-permute-start(bf16[2,128,1024]{2,1,0:T(8,128)(2,1)S(1)} %fusion.1), channel_id=1, source_target_pairs={{8,12},{9,13},{10,14},{11,15},{24,28},{25,29},{26,30},{27,31}} | collective-permute-start | bytes 1572872 | tf_op jit(solution)/shard_map/ppermute | solution.py:546
  56.8 20.8 %all-to-all-start = ((bf16[16,32,256]{2,1,0:T(8,128)(2,1)}), bf16[16,32,256]{2,1,0:T(8,128)(2,1)S(1)}, u32[]{:S(2)}, u32[]{:S(2)}) async-start(bf16[16,32,256]{2,1,0:T(8,128)(2,1)} %head_features.1), calls=%async_computation | async-start | bytes 524288 | tf_op jit(solution)/shard_map/all_to_all | solution.py:576

commit v5 on v4

v5 whole, which is shorter than its diff:
```python
import functools

import jax
import jax.numpy as jnp
from jax import lax
from jax.experimental import pallas as pl
from jax.experimental.pallas import tpu as pltpu
from jax.sharding import PartitionSpec as P

TOUCH = 8
ADAPTER_SCALE = 4.0
BETA_ONE = 0.9
BETA_TWO = 0.999
EPSILON = 1e-08
MIB = 2**20
PIECES_VMEM, FIRST_VMEM, PREPARE_VMEM, SECOND_VMEM = 53.4, 48, 45, 54
BF16 = jnp.bfloat16
F32 = jnp.float32

HBM = pl.BlockSpec(memory_space=pltpu.HBM)
VMEM = pl.BlockSpec(memory_space=pltpu.VMEM)
SMEM = pl.BlockSpec(memory_space=pltpu.SMEM)


def dot_trailing(left, right):
    return lax.dot_general(left, right, (((1,), (1,)), ((), ())), preferred_element_type=F32)


def call(kernel, out_shape, in_specs, out_specs, scratch, flops, nbytes, name, vmem=32):
    return pl.pallas_call(
        kernel,
        out_shape=out_shape,
        in_specs=in_specs,
        out_specs=out_specs,
        scratch_shapes=scratch,
        compiler_params=pltpu.CompilerParams(vmem_limit_bytes=int(vmem * MIB)),
        cost_estimate=pl.CostEstimate(flops=flops, bytes_accessed=nbytes, transcendentals=0),
        name=name,
    )


def pieces_kernel(source_in, source_grad, down, up, *rest):
    *outs, rows_in, rows_grad, down_buf, up_buf, sem = rest
    size = len(outs)
    place = lax.axis_index("tensor")
    tokens, width = rows_in.shape
    rows = tokens // size
    rank = up_buf.shape[0]
    there = pl.ds(pl.multiple_of(place * width, width), width)
    copies = []
    for i in range(size):
        here = pl.ds(i * rows, rows)
        copies.append(pltpu.make_async_copy(source_in.at[here], rows_in.at[here], sem.at[0, i]))
    for i in range(size):
        here = pl.ds(i * rows, rows)
        copies.append(
            pltpu.make_async_copy(source_grad.at[here, there], rows_grad.at[here], sem.at[1, i])
        )
    copies.insert(0, pltpu.make_async_copy(down, down_buf, sem.at[0, size]))
    copies.insert(size + 1, pltpu.make_async_copy(up, up_buf, sem.at[1, size]))
    for copy in copies:
        copy.start()

    def keep(product, first):
        for i in range(size):
            part = product[i * rows : (i + 1) * rows, :].astype(BF16)
            for k, out in enumerate(outs):

                @pl.when(lax.rem(place + k, size) == i)
                def _():
                    out[:, first : first + rank] = part

    for copy in copies[: size + 1]:
        copy.wait()
    keep(jnp.dot(rows_in[...], down_buf[...], preferred_element_type=F32), 0)
    for copy in copies[size + 1 :]:
        copy.wait()
    keep(dot_trailing(rows_grad[...], up_buf[...]), rank)


def rank_pieces(rows_in, rows_grad, down, up, size):
    tokens, width = rows_in.shape
    rank = up.shape[0]
    rows = tokens // size
    return call(
        pieces_kernel,
        [jax.ShapeDtypeStruct((rows, 2 * rank), BF16)] * size,
        [HBM] * 4,
        [VMEM] * size,
        [
            pltpu.VMEM((tokens, width), BF16),
            pltpu.VMEM((tokens, width), BF16),
            pltpu.VMEM(down.shape, BF16),
            pltpu.VMEM(up.shape, BF16),
            pltpu.SemaphoreType.DMA((2, size + 1)),
        ],
        4 * tokens * width * rank,
        4 * tokens * width,
        "rank_pieces",
        PIECES_VMEM,
    )(rows_in, rows_grad, down, up)


def shifted(value, axis, shift):
    size = lax.axis_size(axis)
    return lax.ppermute(value, axis, [(i, (i + shift) % size) for i in range(size)])


def scatter(pieces):
    return [shifted(piece, "tensor", k) if k else piece for k, piece in enumerate(pieces)]


def total_kernel(*refs):
    *terms, out = refs
    total = terms[0][...].astype(F32)
    for term in terms[1:]:
        total = total + term[...].astype(F32)
    out[...] = total.T.astype(BF16)


def total_of(terms):
    rows, ranks = terms[0].shape
    return call(
        total_kernel,
        jax.ShapeDtypeStruct((ranks, rows), BF16),
        [VMEM] * len(terms),
        VMEM,
        [],
        len(terms) * rows * ranks,
        2 * (len(terms) + 1) * rows * ranks,
        "total_low",
    )(*terms)


def gather_pieces(total):
    size = lax.axis_size("tensor")
    return [total] + [shifted(total, "tensor", k) for k in range(1, size)]


def example_scalars(bounds, block):
    low = lax.axis_index("seq") * block
    count = bounds.shape[2]
    first = jnp.int32(-1)
    last = jnp.int32(-1)
    for e in range(count):
        start = bounds[0, 0, e]
        first = first + (start <= low).astype(jnp.int32)
        last = last + (start <= low + block - 1).astype(jnp.int32)
    return low, first, last


def place_pieces(pieces, m, low_scratch):
    size = len(pieces)
    place = lax.axis_index("tensor")
    rank = low_scratch.shape[1]
    first = (1 - m) * rank
    for k, piece in enumerate(pieces):
        low_scratch[lax.rem(place + size - k, size)] = piece[first : first + rank, :]


def masked(low_piece, offset, start, end):
    tokens = offset + lax.broadcasted_iota(jnp.int32, low_piece.shape, 1)
    return jnp.where((tokens >= start) & (tokens < end), low_piece.astype(F32), 0.0).astype(BF16)


def left_side():
    return lax.axis_index("seq") < lax.axis_size("seq") // 2


def fits(bounds, example, low, tokens):
    return bounds[0, 0, example] >= low, bounds[0, 1, example] <= low + tokens


def edges(bounds, low, first, last, tokens):
    left = left_side()
    inner = jnp.where(left, last, first)
    outer = jnp.where(left, first, last)
    inner_starts, inner_ends = fits(bounds, inner, low, tokens)
    outer_starts, outer_ends = fits(bounds, outer, low, tokens)
    inner_on = (left & ~inner_ends) | (~left & ~inner_starts)
    outer_on = (left & ~outer_starts) | (~left & ~outer_ends)
    outer_inside = (left & outer_ends) | (~left & outer_starts)
    return inner, outer, inner_on, outer_on, outer_on & outer_inside


def sum_part(acc, source, low_scratch, low, start, end):
    size, _, rows = low_scratch.shape
    for c in range(size):
        begin = low + c * rows

        @pl.when((start < begin + rows) & (end > begin))
        def _():
            left = masked(low_scratch[c], begin, start, end)
            term = jnp.dot(
                left, source[c * rows : (c + 1) * rows, :], preferred_element_type=F32
            )
            fresh = (start >= begin) | (c == 0)
            acc[...] = jnp.where(fresh, 0.0, acc[...]) + term


def inner_kernel(size, bounds, rows_in, rows_grad, *rest):
    pieces = rest[:size]
    out, low_scratch, acc = rest[size:]
    tokens = rows_in.shape[0]
    low, first, last = example_scalars(bounds, tokens)
    inner = edges(bounds, low, first, last, tokens)[0]
    for m, source in enumerate((rows_in, rows_grad)):
        place_pieces(pieces, m, low_scratch)
        sum_part(acc, source, low_scratch, low, bounds[0, 0, inner], bounds[0, 1, inner])
        out[m] = (ADAPTER_SCALE * acc[...]).astype(BF16)


def inner_parts(bounds, rows_in, rows_grad, low):
    size = len(low)
    rank, rows = low[0].shape[0] // 2, low[0].shape[1]
    tokens, width = rows_in.shape
    return call(
        functools.partial(inner_kernel, size),
        jax.ShapeDtypeStruct((2, rank, width), BF16),
        [SMEM] + [VMEM] * (2 + size),
        VMEM,
        [pltpu.VMEM((size, rank, rows), BF16), pltpu.VMEM((rank, width), F32)],
        4 * tokens * width * rank,
        4 * tokens * width,
        "inner_parts",
    )(bounds, rows_in, rows_grad, *low)


def normalize(grads, first_moment, second_moment):
    first = first_moment + (1.0 - BETA_ONE) * grads
    second = second_moment + ((1.0 - BETA_TWO) * grads) * grads
    guess = lax.rsqrt(second)
    below = second * guess + EPSILON
    return first * (guess * (2.0 - below * guess))


def split_two(value):
    high = value.astype(BF16)
    return high, (value - high.astype(F32)).astype(BF16)


def rank_side_pair(rank_side, blocks):
    lines, rank = rank_side.shape
    blocks[...] = jnp.zeros_like(blocks)
    for i, term in enumerate(split_two(rank_side[...])):
        for j in range(2):
            at = (2 * i + j) * lines
            blocks[at : at + lines, j * rank : (j + 1) * rank] = term


def project_rank(blocks, normed):
    both = jnp.dot(blocks[...], normed, preferred_element_type=F32)
    half = both.shape[0] // 2
    return both[:half] + both[half:]


def project_width(value, right):
    high, low = split_two(value)
    return jnp.dot(high, right, preferred_element_type=F32) + jnp.dot(
        low, right, preferred_element_type=F32
    )


STEP = 16


def slots_kernel(m, size, bounds, owner, source, moments, rank_side, width_side, *rest):
    pieces = rest[:size]
    out, outer_part, low_scratch, acc, normed, blocks, ranked, wide = rest[size:]
    tokens = source.shape[0]
    rank, width = outer_part.shape
    lines = rank_side.shape[0]
    low, first, last = example_scalars(bounds, tokens)
    count = bounds.shape[2]
    _, outer, _, outer_on, _ = edges(bounds, low, first, last, tokens)
    place_pieces(pieces, m, low_scratch)
    rank_side_pair(rank_side, blocks)

    def slot(j):
        return jnp.minimum(first + j, count - 1)

    def inside(j):
        starts, ends = fits(bounds, slot(j), low, tokens)
        return (first + j <= last) & starts & ends

    @pl.loop(0, TOUCH)
    def _(j):
        here = inside(j)
        is_outer = (first + j == outer) & outer_on

        @pl.when(here | is_outer)
        def _():
            start, end = bounds[0, 0, slot(j)], bounds[0, 1, slot(j)]
            sum_part(acc, source, low_scratch, low, start, end)

        @pl.when(is_outer)
        def _():
            outer_part[...] = (ADAPTER_SCALE * acc[...]).astype(BF16)

        @pl.when(here)
        def _():
            for r in range(0, rank, STEP):
                normed[j, r : r + STEP, :] = normalize(
                    ADAPTER_SCALE * acc[r : r + STEP, :],
                    moments[0, m, r : r + STEP, :],
                    moments[1, m, r : r + STEP, :],
                ).astype(BF16)

        @pl.when(~here)
        def _():
            normed[j] = jnp.zeros((rank, width), BF16)

    for j in range(0, TOUCH, 2):
        ranked[j * lines : (j + 2) * lines, :] = project_rank(
            blocks, normed[j : j + 2].reshape(2 * rank, width)
        )
    wide[...] = project_width(ranked[...], width_side[...]).reshape(wide.shape)
    out[...] = jnp.zeros_like(out)
    for j in range(TOUCH):

        @pl.when(inside(j))
        def _():
            out[owner[0, slot(j)]] = wide[j].astype(BF16)


def slot_features(m, bounds, owner, source, moments, rank_side, width_side, pieces, name):
    size = len(pieces)
    rank, rows = pieces[0].shape[0] // 2, pieces[0].shape[1]
    tokens, width = source.shape
    lines = rank_side.shape[0]
    columns = width_side.shape[1]
    return call(
        functools.partial(slots_kernel, m, size),
        [
            jax.ShapeDtypeStruct((owner.shape[1], lines, columns), BF16),
            jax.ShapeDtypeStruct((rank, width), BF16),
        ],
        [SMEM, SMEM] + [VMEM] * (4 + size),
        [VMEM, VMEM],
        [
            pltpu.VMEM((size, rank, rows), BF16),
            pltpu.VMEM((rank, width), F32),
            pltpu.VMEM((TOUCH, rank, width), BF16),
            pltpu.VMEM((4 * lines, 2 * rank), BF16),
            pltpu.VMEM((TOUCH * lines, width), F32),
            pltpu.VMEM((TOUCH, lines, columns), F32),
        ],
        2 * tokens * width * rank * TOUCH,
        4 * tokens * width,
        name,
    )(bounds, owner, source, moments, rank_side, width_side, *pieces)


def crossing_kernel(
    tokens,
    hops,
    bounds,
    owner,
    filled_grad,
    filled_in,
    outer_grad,
    outer_in,
    kept,
    received,
    moments,
    rank_side,
    width_side,
    *rest
):
    arrived = rest[:hops]
    out, normed, blocks, ranked = rest[hops:]
    low, first, last = example_scalars(bounds, tokens)
    rank = outer_in.shape[0]
    lines = rank_side.shape[0]
    half = kept.shape[1]
    inner, outer, inner_on, _, outer_done = edges(bounds, low, first, last, tokens)
    place, middle = lax.axis_index("seq"), lax.axis_size("seq") // 2
    inner_done = inner_on & ((place == middle - 1) | (place == middle))
    out[:, :lines] = filled_grad[...]
    out[:, lines:] = filled_in[...]
    rank_side_pair(rank_side, blocks)

    @pl.when(outer_done)
    def _():
        for m, part in enumerate((outer_grad, outer_in)):
            for r in range(0, rank, STEP):
                here = slice(r, r + STEP)
                grads = part[here, :].astype(F32)
                for k in range(hops):
                    grads = grads + arrived[k][m, here, :].astype(F32)
                normed[m * rank + r : m * rank + r + STEP, :] = normalize(
                    grads, moments[0, m, here, :], moments[1, m, here, :]
                ).astype(BF16)
        ranked[: 2 * lines, :] = project_rank(blocks, normed[...])

    @pl.when(inner_done)
    def _():
        offset = jnp.where(left_side(), 0, half)
        normed[...] = jnp.zeros_like(normed)
        for m in range(2):
            for r in range(0, half, STEP):
                here = pl.ds(pl.multiple_of(offset + r, STEP), STEP)
                there = pl.ds(pl.multiple_of(m * rank + offset + r, STEP), STEP)
                grads = kept[m, r : r + STEP, :].astype(F32)
                grads = grads + received[m, r : r + STEP, :].astype(F32)
                normed[there, :] = normalize(
                    grads, moments[0, m, here, :], moments[1, m, here, :]
                ).astype(BF16)
        ranked[2 * lines :, :] = project_rank(blocks, normed[...])

    @pl.when(outer_done | inner_done)
    def _():
        wide = project_width(ranked[...], width_side[...]).astype(BF16)

        @pl.when(outer_done)
        def _():
            out[owner[0, outer]] = wide[: 2 * lines]

        @pl.when(inner_done)
        def _():
            out[owner[0, inner]] = wide[2 * lines :]


def crossing_features(
    tokens, bounds, owner, filled, outer, kept, received, moments, rank_side, width_side, arrived
):
    hops = len(arrived)
    rank, width = outer[0].shape
    slots, lines, columns = filled[0].shape
    return call(
        functools.partial(crossing_kernel, tokens, hops),
        jax.ShapeDtypeStruct((slots, 2 * lines, columns), BF16),
        [SMEM, SMEM] + [VMEM] * (9 + hops),
        VMEM,
        [
            pltpu.VMEM((2 * rank, width), BF16),
            pltpu.VMEM((4 * lines, 2 * rank), BF16),
            pltpu.VMEM((4 * lines, width), F32),
        ],
        8 * width * 2 * rank * 4 * lines,
        12 * rank * width,
        "crossing_features",
    )(
        bounds,
        owner,
        *filled,
        *outer,
        kept,
        received,
        moments,
        rank_side,
        width_side,
        *arrived,
    )


def owned_kernel(arrived, out):
    total = arrived[0].astype(F32)
    for k in range(1, arrived.shape[0]):
        total = total + arrived[k].astype(F32)
    columns = total.shape[1]
    for line in range(total.shape[0]):
        out[:, line * columns : (line + 1) * columns] = total[line : line + 1, :]


def owned_features(arrived):
    _, lines, columns = arrived.shape
    return call(
        owned_kernel,
        jax.ShapeDtypeStruct((1, lines * columns), F32),
        [VMEM],
        VMEM,
        [],
        arrived.size,
        2 * arrived.size,
        "owned_features",
    )(arrived)


TILE = 256


def depth_chunks(depth):
    return [0, depth // 8, 3 * depth // 8, 5 * depth // 8, 7 * depth // 8, depth]


def operand_copies(source, weight, held, weight_buf, sem, column):
    edges = depth_chunks(held.shape[1])
    pairs = []
    for c, (begin, end) in enumerate(zip(edges, edges[1:])):
        depth = pl.ds(begin, end - begin)
        columns = pl.ds(column, weight_buf.shape[0])
        pair = (
            pltpu.make_async_copy(source.at[:, depth], held.at[:, depth], sem.at[0, c]),
            pltpu.make_async_copy(weight.at[columns, depth], weight_buf.at[:, depth], sem.at[1, c]),
        )
        pairs.append((slice(begin, end), pair))
    return pairs


def start_all(pairs):
    for _, pair in pairs:
        for copy in pair:
            copy.start()


def add_chunk(pairs, c, held, weight_buf, out):
    depth, pair = pairs[c]
    for copy in pair:
        copy.wait()
    for n in range(0, weight_buf.shape[0], TILE):
        there = slice(n, n + TILE)
        term = dot_trailing(held[:, depth], weight_buf[there, depth])
        out[:, there] = term if c == 0 else out[:, there] + term


def first_kernel(column, source, weight, out, acc, held, weight_buf, sem):
    pairs = operand_copies(source, weight, held, weight_buf, sem, column)
    start_all(pairs)
    for c in range(len(pairs)):
        add_chunk(pairs, c, held, weight_buf, acc)
    out[...] = acc[...].astype(BF16)


def second_kernel(size, count, source, weight, down, *rest):
    done, pieces = rest[:count], rest[count : count + size]
    out, result, acc, low_rows, held, weight_buf, *bufs = rest[count + size :]
    down_buf, *bufs = bufs
    done_bufs, (pieces_buf, sem, extra_sem, out_sem) = bufs[:count], bufs[count:]
    tokens, width = result.shape
    split = sum(part.shape[1] for part in done)
    place = lax.axis_index("tensor")
    rows = tokens // size
    rank = low_rows.shape[1]
    extras = [pltpu.make_async_copy(down, down_buf, extra_sem.at[0])]
    for k, piece in enumerate(pieces):
        extras.append(pltpu.make_async_copy(piece, pieces_buf.at[k], extra_sem.at[1 + k]))
    for k, part in enumerate(done):
        extras.append(pltpu.make_async_copy(part, done_bufs[k], extra_sem.at[1 + size + k]))
    pairs = operand_copies(source, weight, held, weight_buf, sem, split)
    early = 2
    start_all(pairs[:early])
    for copy in extras:
        copy.start()
    start_all(pairs[early:])
    for c in range(early):
        add_chunk(pairs, c, held, weight_buf, acc)
    for copy in extras:
        copy.wait()
    for k in range(size):
        block = lax.rem(place + size - k, size)
        low_rows[pl.ds(pl.multiple_of(block * rows, rows), rows), :] = (
            pieces_buf[k, rank:, :].astype(F32).T.astype(BF16)
        )

    def out_copy(begin, end, k):
        here = pl.ds(begin, end - begin)
        return pltpu.make_async_copy(result.at[:, here], out.at[:, here], out_sem.at[k])

    def finish(base, begin, end, k):
        extra = dot_trailing(low_rows[...], down_buf[begin:end, :])
        result[:, begin:end] = (base[...].astype(F32) + ADAPTER_SCALE * extra).astype(BF16)
        out_copy(begin, end, k).start()

    cuts = [0]
    for k, part in enumerate(done_bufs):
        cuts.append(cuts[-1] + part.shape[1])
        finish(part, cuts[-2], cuts[-1], k)
    cuts.append(width)
    for c in range(early, len(pairs)):
        add_chunk(pairs, c, held, weight_buf, acc)
    finish(acc, split, width, count)
    for k in range(count + 1):
        out_copy(cuts[k], cuts[k + 1], k).wait()


def first_product(source, weight, column, split):
    tokens, depth = source.shape
    return call(
        functools.partial(first_kernel, column),
        jax.ShapeDtypeStruct((tokens, split), BF16),
        [HBM, HBM],
        VMEM,
        [
            pltpu.VMEM((tokens, split), F32),
            pltpu.VMEM((tokens, depth), BF16),
            pltpu.VMEM((split, depth), BF16),
            pltpu.SemaphoreType.DMA((2, len(depth_chunks(depth)) - 1)),
        ],
        2 * tokens * depth * split,
        2 * depth * (tokens + split),
        "first_product",
        FIRST_VMEM,
    )(source, weight)


def second_product(source, weight, down, done, pieces):
    tokens, depth = source.shape
    width, rank = down.shape
    rest = width - sum(part.shape[1] for part in done)
    size, count = len(pieces), len(done)
    return call(
        functools.partial(second_kernel, size, count),
        jax.ShapeDtypeStruct((tokens, width), BF16),
        [HBM] * (3 + count + size),
        HBM,
        [
            pltpu.VMEM((tokens, width), BF16),
            pltpu.VMEM((tokens, rest), F32),
            pltpu.VMEM((tokens, rank), BF16),
            pltpu.VMEM((tokens, depth), BF16),
            pltpu.VMEM((rest, depth), BF16),
            pltpu.VMEM(down.shape, BF16),
        ]
        + [pltpu.VMEM(part.shape, BF16) for part in done]
        + [
            pltpu.VMEM((size,) + pieces[0].shape, BF16),
            pltpu.SemaphoreType.DMA((2, len(depth_chunks(depth)) - 1)),
            pltpu.SemaphoreType.DMA((1 + size + count,)),
            pltpu.SemaphoreType.DMA((count + 1,)),
        ],
        2 * tokens * depth * rest,
        2 * depth * (tokens + rest),
        "second_product",
        SECOND_VMEM,
    )(source, weight, down, *done, *pieces)


def prepare_kernel(source_in, source_grad, width_side, first, second, other, *rest):
    rows_in, columns_grad, right, moments, own, arrived, sem = rest
    place = lax.axis_index("tensor")
    width, rows = right.shape[0], own.shape[2]
    here = pl.ds(pl.multiple_of(place * width, width), width)
    copies = [
        pltpu.make_async_copy(first, own.at[0], sem.at[0]),
        pltpu.make_async_copy(second, own.at[1], sem.at[1]),
        pltpu.make_async_copy(other, arrived, sem.at[2]),
        pltpu.make_async_copy(source_grad.at[:, here], columns_grad, sem.at[3]),
        pltpu.make_async_copy(source_in, rows_in, sem.at[4]),
        pltpu.make_async_copy(width_side.at[here], right, sem.at[5]),
    ]
    for copy in copies:
        copy.start()
    for copy in copies[:3]:
        copy.wait()
    mine = lax.axis_index("dp")
    for i, beta in enumerate((BETA_ONE, BETA_TWO)):
        for m in range(2):
            if arrived.shape[2] == rows:
                at = pl.ds(pl.multiple_of(mine * rows, rows), rows)
                moments[i, m, at, :] = beta * own[i, m]
                at = pl.ds(pl.multiple_of((1 - mine) * rows, rows), rows)
                moments[i, m, at, :] = beta * arrived[i, m].astype(F32)
            else:
                moments[i, m] = beta * arrived[i, m].astype(F32)
    for copy in copies[3:]:
        copy.wait()


def other_moments(first, second):
    sent = jnp.stack([first, second]).astype(BF16)
    if lax.axis_size("dp") != 2:
        return lax.all_gather(sent, "dp", axis=2, tiled=True)
    return shifted(sent, "dp", 1)


def prepare(rows_in, rows_grad, width_side, first, second, other):
    tokens, width = rows_in.shape
    columns = width_side.shape[1]
    rank = first.shape[1] * lax.axis_size("dp")
    return call(
        prepare_kernel,
        [
            jax.ShapeDtypeStruct((tokens, width), BF16),
            jax.ShapeDtypeStruct((tokens, width), BF16),
            jax.ShapeDtypeStruct((width, columns), BF16),
            jax.ShapeDtypeStruct((2, 2, rank, width), F32),
        ],
        [HBM] * 6,
        [VMEM] * 4,
        [
            pltpu.VMEM((2,) + first.shape, F32),
            pltpu.VMEM(other.shape, BF16),
            pltpu.SemaphoreType.DMA((6,)),
        ],
        8 * rank * width,
        4 * tokens * width + 8 * rank * width,
        "prepare",
        PREPARE_VMEM,
    )(rows_in, rows_grad, width_side, first, second, other)


def per_device(
    attention_output_rows,
    projection_result_gradient,
    adapter_down_weight,
    adapter_up_weight,
    output_projection_weight,
    adam_first_moments,
    adam_second_moments,
    rank_side_projection,
    width_side_projection,
    bounds,
    example_owner_slot,
):
    packs, blk, width_local = attention_output_rows.shape
    assert packs == 1
    width = projection_result_gradient.shape[2]
    size = lax.axis_size("tensor")
    rows_in = attention_output_rows.reshape(blk, width_local)
    rows_grad = projection_result_gradient.reshape(blk, width)

    pieces = rank_pieces(rows_in, rows_grad, adapter_down_weight, adapter_up_weight, size)
    pieces, own_moments = lax.optimization_barrier(
        (pieces, (adam_first_moments, adam_second_moments))
    )
    other = other_moments(*own_moments)

    cuts = [0, width_local // 4, 3 * width_local // 4]

    def product(rows, k):
        return first_product(rows, output_projection_weight, cuts[k], cuts[k + 1] - cuts[k])

    done = [product(rows_grad, 0)]
    sent, done = lax.optimization_barrier((scatter(pieces), done))
    total, rows_late, bounds_late = lax.optimization_barrier((total_of(sent), rows_grad, bounds))
    done.append(product(rows_late, 1))
    done, rows_late, other = lax.optimization_barrier((done, rows_late, other))
    prepared = prepare(rows_in, rows_late, width_side_projection, *own_moments, other)
    first_token = lax.axis_index("seq") * blk
    end_token = first_token + blk
    starts, ends = bounds_late[0, 0], bounds_late[0, 1]
    left = left_side()
    spans = jnp.any(
        jnp.where(
            left,
            (starts < first_token) & (ends >= end_token),
            (starts <= first_token) & (ends > end_token),
        )
    ).astype(F32)
    low, prepared, done, spans = lax.optimization_barrier(
        (gather_pieces(total), prepared, done, spans)
    )
    rows_in, columns_grad, right, moments = prepared
    inner = inner_parts(bounds, rows_in, columns_grad, low)
    shared = (rank_side_projection, right)
    seq = lax.axis_size("seq")
    middle = seq // 2

    def onward(arrived):
        return inner.astype(F32) + spans * arrived.astype(F32)

    arrived = []
    outgoing = inner
    for k in range(middle - 1):
        pairs = [(k, k + 1), (k + 1, k), (seq - 1 - k, seq - 2 - k), (seq - 2 - k, seq - 1 - k)]
        moved = lax.ppermute(outgoing, "seq", pairs)
        if middle > 2:
            place = lax.axis_index("seq")
            moved = jnp.where((place == k + 1) | (place == seq - 2 - k), moved, 0)
        arrived.append(moved)
        outgoing = onward(arrived[-1]).astype(BF16)
    filled_in, outer_in = slot_features(
        1, bounds, example_owner_slot, columns_grad, moments, *shared, low, "slots_in"
    )
    arrived, rows_in, outer_in = lax.optimization_barrier((arrived, rows_in, outer_in))
    summed = onward(arrived[-1]).astype(BF16)
    half = summed.shape[1] // 2
    kept = jnp.where(left, summed[:, :half], summed[:, half:])
    sent = jnp.where(left, summed[:, half:], summed[:, :half])
    received = lax.ppermute(sent, "seq", [(middle - 1, middle), (middle, middle - 1)])
    filled_grad, outer_grad = slot_features(
        0, bounds, example_owner_slot, rows_in, moments, *shared, low, "slots_grad"
    )
    received, outer_grad = lax.optimization_barrier((received, outer_grad))
    buffer = crossing_features(
        blk,
        bounds,
        example_owner_slot,
        (filled_grad, filled_in),
        (outer_grad, outer_in),
        kept,
        received,
        moments,
        *shared,
        arrived,
    )
    arrived = lax.all_to_all(buffer, ("seq", "tensor"), split_axis=0, concat_axis=0, tiled=True)
    features = owned_features(arrived)[None]
    out = second_product(
        rows_grad,
        output_projection_weight,
        adapter_down_weight,
        done,
        low,
    )
    return (out.reshape(attention_output_rows.shape), features)


def solution(mesh):
    return jax.shard_map(
        per_device,
        mesh=mesh,
        in_specs=(
            P("dp", "seq", "tensor"),
            P("dp", "seq", None),
            P("tensor", None),
            P(None, "tensor"),
            P("tensor", None),
            P(None, "dp", "tensor"),
            P(None, "dp", "tensor"),
            P(),
            P(),
            P("dp", None, None),
            P("dp", None),
        ),
        out_specs=(P("dp", "seq", "tensor"), P("dp", ("seq", "tensor"), None)),
        check_vma=False,
    )
```

time: 79.7 us -> 69.6 us (0.87); the launches traced: 78.3 us -> 69.4 us
  waiting for transfers between devices: 8.94 us -> 0.46 us
  Pallas kernels: 37.3 us -> 41.6 us
  starting transfers between devices: 26.2 us -> 23 us
    ppermute x7, waiting for transfers between devices: 7.44 us -> 0.09 us  [shifted(): lax.ppermute(value, axis, [(i, (i + shift) % size) for i in range(size)])]
    pallas_call x5 -> x9, Pallas kernels: 29.5 us -> 33 us  [the longest x2 12.6 us: first_product(): call(functools.partial(first_kernel, column), jax.ShapeDtypeStruct((token...]
    ppermute x3 -> x2, starting transfers between devices: 3.51 us -> 1.04 us  [the longest x1 0.86 us: per_device(): lax.ppermute(sent, 'seq', [(middle - 1, middle), (middle, middle - 1)])]
    dynamic_slice x1 -> x0, local copies, waits for them, and re-layouts: 1.8 us -> none  [per_device(): lax.dynamic_slice_in_dim(rows_grad, lax.axis_index('tensor') * width_loca...]
    unnamed x26 -> x22, local copies, waits for them, and re-layouts: 0.07 us -> 1.83 us
    ppermute x3 -> x2, waiting for transfers between devices: 1.49 us -> 0.01 us  [the longest x1 0.01 us: per_device(): moved = lax.ppermute(outgoing, 'seq', pairs)]
  transfers between devices with their start and end apart: 11 -> 10, of which waited for: 3 -> 2; matrix products, arithmetic and copies ran while one was open for 4% -> 1% of each run, Pallas kernels for 34% -> 48%
where the time goes in v5:
time: 69.6 us; the launch traced here: 69.4 us
  Pallas kernels  41.6 us (60%)
  starting transfers between devices  23 us (33%)
  local copies, waits for them, and re-layouts  1.83 us (3%)
  between operations  1.54 us (2%)
  other arithmetic  0.99 us (1%)
    pallas_call x2, Pallas kernels, first_product(): call(functools.partial(first_kernel, column), jax.ShapeDtypeStruct((token...  12.6 us
    ppermute x7, starting transfers between devices, shifted(): lax.ppermute(value, axis, [(i, (i + shift) % size) for i in range(size)])  12.4 us
    pallas_call x1, Pallas kernels, second_product(): call(functools.partial(second_kernel, size, count), jax.ShapeDtypeStruct(...  9.69 us
    all_to_all x1, starting transfers between devices, per_device(): lax.all_to_all(buffer, ('seq', 'tensor'), split_axis=0, concat_axis=0, ti...  9.5 us
    pallas_call x2, Pallas kernels, slot_features(): call(functools.partial(slots_kernel, m, size), [jax.ShapeDtypeStruct((own...  8.62 us
    pallas_call x1, Pallas kernels, rank_pieces(): call(pieces_kernel, [jax.ShapeDtypeStruct((rows, 2 * rank), BF16)] * size...  4.41 us
    pallas_call x1, Pallas kernels, prepare(): call(prepare_kernel, [jax.ShapeDtypeStruct((tokens, width), BF16), jax.Sh...  2.48 us
    unnamed x22, local copies, waits for them, and re-layouts  1.83 us
  transfers between devices with their start and end apart: 10, of which 2 were waited for; matrix products, arithmetic and copies ran while one was open for 1% of the time, Pallas kernels for 48%

profile of v5, /device:TPU:0, one launch (start us, length us, event | category | flops | bytes accessed | tf_op | source)
XLA Modules:
  0.0 69.4 jit_solution(6457456029829628147)
XLA Ops:
  0.7 4.4 %rank_pieces.1 = (bf16[256,256]{1,0:T(8,128)(2,1)S(1)}, bf16[256,256]{1,0:T(8,128)(2,1)S(1)}, bf16[256,256]{1,0:T(8,128)(2,1)S(1)}, bf16[256,256]{1,0:T(8,128)(2,1)S(1)}) custom-call(bf16[1024,1024]{1,0:T(8,128)(2,1)} %bitcast.13, bf16[1024,4096]{1,0:T(8,128)(2,1)} %bitcast.8, bf16[1024,128]{1,0:T(8,128)(2,1)} %down.3, bf16[128,1024]{1,0:T(8,128)(2,1)} %up.1), custom_call_target="tpu_custom_call" | custom-call | flops 536870912 | bytes 4194304 | tf_op jit(solution)/shard_map/rank_pieces/pallas_call | solution.py:85
  5.1 3.1 %collective-permute-start = (bf16[256,256]{1,0:T(8,128)(2,1)S(1)}, bf16[256,256]{1,0:T(8,128)(2,1)S(1)}, u32[]{:S(2)}, u32[]{:S(2)}) collective-permute-start(bf16[256,256]{1,0:T(8,128)(2,1)S(1)} %get-tuple-element.53), channel_id=1, source_target_pairs={{0,1},{1,2},{2,3},{3,0},{4,5},{5,6},{6,7},{7,4},{8,9},{9,10},{10,1... | collective-permute-start | bytes 393224 | tf_op jit(solution)/shard_map/ppermute | solution.py:106
  8.1 2.6 %collective-permute-start.1 = (bf16[256,256]{1,0:T(8,128)(2,1)S(1)}, bf16[256,256]{1,0:T(8,128)(2,1)S(1)}, u32[]{:S(2)}, u32[]{:S(2)}) collective-permute-start(bf16[256,256]{1,0:T(8,128)(2,1)S(1)} %get-tuple-element.54), channel_id=1, source_target_pairs={{0,2},{1,3},{2,0},{3,1},{4,6},{5,7},{6,4},{7,5},{8,10},{9,11},{10,... | collective-permute-start | bytes 393224 | tf_op jit(solution)/shard_map/ppermute | solution.py:106
  10.7 1.3 %collective-permute-start.2 = (bf16[256,256]{1,0:T(8,128)(2,1)S(1)}, bf16[256,256]{1,0:T(8,128)(2,1)S(1)}, u32[]{:S(2)}, u32[]{:S(2)}) collective-permute-start(bf16[256,256]{1,0:T(8,128)(2,1)S(1)} %get-tuple-element.55), channel_id=1, source_target_pairs={{0,3},{1,0},{2,1},{3,2},{4,7},{5,4},{6,5},{7,6},{8,11},{9,8},{10,9... | collective-permute-start | bytes 393224 | tf_op jit(solution)/shard_map/ppermute | solution.py:106
  12.1 0.1 convert_bitcast_fusion
  12.2 0.1 pad_maximum_fusion
  12.2 1.6 %collective-permute-start.6 = (bf16[2,2,64,1024]{3,2,1,0:T(8,128)(2,1)S(1)}, bf16[2,2,64,1024]{3,2,1,0:T(8,128)(2,1)S(1)}, u32[]{:S(2)}, u32[]{:S(2)}) collective-permute-start(bf16[2,2,64,1024]{3,2,1,0:T(8,128)(2,1)S(1)} %pad_maximum_fusion), channel_id=1, source_target_pairs={{0,16},{16,0},{1,17},{17,1},{2,18},{18,2},{3,19},{19,3},{4,20},{20... | collective-permute-start | bytes 1572872 | tf_op jit(solution)/shard_map/ppermute | solution.py:106
  13.8 5.9 %first_product.2.rest_0_ = bf16[1024,256]{1,0:T(8,128)(2,1)S(1)} custom-call(bf16[1024,4096]{1,0:T(8,128)(2,1)} %bitcast.9, bf16[1024,4096]{1,0:T(8,128)(2,1)} %weight.5), custom_call_target="tpu_custom_call" | custom-call | flops 2147483648 | bytes 10485760 | tf_op jit(solution)/shard_map/first_product/pallas_call | solution.py:579
  19.7 0.8 %copy-done.3 = bf16[1024,256]{1,0:T(8,128)(2,1)} copy-done((bf16[1024,256]{1,0:T(8,128)(2,1)}, bf16[1024,256]{1,0:T(8,128)(2,1)S(1)}, u32[]{:S(2)}) %copy-start.3) | copy-done | bytes 524312
  20.5 0.0 collective-permute-done.refs_1_
  20.5 0.1 total_low.1.rest_2_.rest_0_
  20.7 0.0 copy-start.8
  20.7 3.2 %collective-permute-start.5 = (bf16[256,256]{1,0:T(8,128)(2,1)S(1)}, bf16[256,256]{1,0:T(8,128)(2,1)S(1)}, u32[]{:S(2)}, u32[]{:S(2)}) collective-permute-start(bf16[256,256]{1,0:T(8,128)(2,1)S(1)} %total_low.1.rest_2_.rest_0_), channel_id=1, source_target_pairs={{0,3},{1,0},{2,1},{3,2},{4,7},{5,4},{6,5},{7,6},{8,11},{9,8},{10,9... | collective-permute-start | bytes 393224 | tf_op jit(solution)/shard_map/ppermute | solution.py:106
  23.9 0.4 collective-permute-start.4
  24.3 0.2 collective-permute-start.3
  24.6 6.7 %first_product.3.rest_1_ = bf16[1024,512]{1,0:T(8,128)(2,1)S(1)} custom-call(bf16[1024,4096]{1,0:T(8,128)(2,1)} %bitcast.10, bf16[1024,4096]{1,0:T(8,128)(2,1)} %weight.5), custom_call_target="tpu_custom_call" | custom-call | flops 4294967296 | bytes 12582912 | tf_op jit(solution)/shard_map/first_product/pallas_call | solution.py:579
  31.3 1.0 %copy-done = bf16[1024,512]{1,0:T(8,128)(2,1)} copy-done((bf16[1024,512]{1,0:T(8,128)(2,1)}, bf16[1024,512]{1,0:T(8,128)(2,1)S(1)}, u32[]{:S(2)}) %copy-start) | copy-done | bytes 1048600
  32.3 0.6 select_reduce_fusion
  33.6 2.5 %prepare.1 = (bf16[1024,1024]{1,0:T(8,128)(2,1)S(1)}, bf16[1024,1024]{1,0:T(8,128)(2,1)S(1)}, bf16[1024,256]{1,0:T(8,128)(2,1)S(1)}, f32[2,2,128,1024]{3,2,1,0:T(8,128)S(1)}) custom-call(bf16[1024,1024]{1,0:T(8,128)(2,1)} %bitcast.14, bf16[1024,4096]{1,0:T(8,128)(2,1)} %bitcast.11, bf16[4096,256]{1,0:T(8,128)(2,1)} %width_side.1, ...), custom_call_target="tpu_custom_call" | custom-call | flops 1048576 | bytes 5242880 | tf_op jit(solution)/shard_map/prepare/pallas_call | solution.py:671
  36.1 0.1 collective-permute-done.4.rest_4_.rest_2_
  36.2 0.0 copy-start.10
  36.2 1.7 %inner_parts.1 = bf16[2,128,1024]{2,1,0:T(8,128)(2,1)S(1)} custom-call(s32[1,2,16]{2,1,0:T(2,128)S(1)} %copy-done.8, bf16[1024,1024]{1,0:T(8,128)(2,1)S(1)} %get-tuple-element.85.rows_in.source, bf16[1024,1024]{1,0:T(8,128)(2,1)S(1)} %get-tuple-element.81.rows_grad.source, bf16[256,256]{1,0:T(8,128)(2,1)S(1)} %total_low.1.rest_2_.rest_0_, ...), custom_call_target="tpu_custom_call" | custom-call | flops 536870912 | bytes 4194304 | tf_op jit(solution)/shard_map/inner_parts/pallas_call | solution.py:217
  37.8 0.2 collective-permute-start.7
  38.0 4.3 %slots_in.1 = (bf16[16,16,256]{2,1,0:T(8,128)(2,1)S(1)}, bf16[128,1024]{1,0:T(8,128)(2,1)S(1)}) custom-call(s32[1,2,16]{2,1,0:T(2,128)S(1)} %copy-done.8, s32[1,16]{1,0:T(1,128)S(1)} %copy-done.10, bf16[1024,1024]{1,0:T(8,128)(2,1)S(1)} %get-tuple-element.81.rows_grad.source, f32[2,2,128,1024]{3,2,1,0:T(8,128)S(1)} %get-tuple-element.82.moments, ...), custom_call_target="tpu_custom_call" | custom-call | flops 2147483648 | bytes 4194304 | tf_op jit(solution)/shard_map/slots_in/pallas_call | solution.py:332
  42.4 0.2 add_convert_fusion
  42.6 0.9 %collective-permute-start.8 = (bf16[2,64,1024]{2,1,0:T(8,128)(2,1)S(1)}, bf16[2,64,1024]{2,1,0:T(8,128)(2,1)S(1)}, u32[]{:S(2)}, u32[]{:S(2)}) collective-permute-start(bf16[2,64,1024]{2,1,0:T(8,128)(2,1)S(1)} %get-tuple-element.95), channel_id=1, source_target_pairs={{4,8},{8,4},{5,9},{9,5},{6,10},{10,6},{7,11},{11,7},{20,24},{24,20... | collective-permute-start | bytes 786440 | tf_op jit(solution)/shard_map/ppermute | solution.py:771
  43.5 4.3 %slots_grad.1 = (bf16[16,16,256]{2,1,0:T(8,128)(2,1)S(1)}, bf16[128,1024]{1,0:T(8,128)(2,1)S(1)}) custom-call(s32[1,2,16]{2,1,0:T(2,128)S(1)} %copy-done.8, s32[1,16]{1,0:T(1,128)S(1)} %copy-done.10, bf16[1024,1024]{1,0:T(8,128)(2,1)S(1)} %get-tuple-element.85.rows_in.source, f32[2,2,128,1024]{3,2,1,0:T(8,128)S(1)} %get-tuple-element.82.moments, ...), custom_call_target="tpu_custom_call" | custom-call | flops 2147483648 | bytes 4194304 | tf_op jit(solution)/shard_map/slots_grad/pallas_call | solution.py:332
  47.9 1.3 %crossing_features.1 = bf16[16,32,256]{2,1,0:T(8,128)(2,1)} custom-call(s32[1,2,16]{2,1,0:T(2,128)S(1)} %copy-done.8, s32[1,16]{1,0:T(1,128)S(1)} %copy-done.10, bf16[16,16,256]{2,1,0:T(8,128)(2,1)S(1)} %get-tuple-element.86.filled_grad, bf16[16,16,256]{2,1,0:T(8,128)(2,1)S(1)} %get-tuple-element.87.filled_in, ...), custom_call_target="tpu_custom_call" | custom-call | flops 134217728 | bytes 1572864 | tf_op jit(solution)/shard_map/crossing_features/pallas_call | solution.py:430
  49.2 9.5 %all-to-all-start = ((bf16[16,32,256]{2,1,0:T(8,128)(2,1)}), bf16[16,32,256]{2,1,0:T(8,128)(2,1)S(1)}, u32[]{:S(2)}, u32[]{:S(2)}) async-start(bf16[16,32,256]{2,1,0:T(8,128)(2,1)} %crossing_features.1), calls=%async_computation | async-start | bytes 524288 | tf_op jit(solution)/shard_map/all_to_all | solution.py:788
  58.7 9.7 %second_product.1 = bf16[1024,1024]{1,0:T(8,128)(2,1)} custom-call(bf16[1024,4096]{1,0:T(8,128)(2,1)} %bitcast.12, bf16[1024,4096]{1,0:T(8,128)(2,1)} %weight.5, bf16[1024,128]{1,0:T(8,128)(2,1)} %down.3, bf16[1024,256]{1,0:T(8,128)(2,1)} %copy-done.3, bf16[1024,512]{1,0:T(8,128)(2,1)} %copy-done, bf16[256,256]{1,0:T(8,128)(2,1)} %copy-done.4, ...), custom_call_target="tpu_custom_call" | custom-call | flops 2147483648 | bytes 10485760 | tf_op jit(solution)/shard_map/second_product/pallas_call | solution.py:602
  68.4 0.4 all-to-all-done.arrived
  68.8 0.7 owned_features.1
  (26 shorter events, 0.1 us)
Async XLA Ops:
  0.6 11.4 %copy-start.1 = (f32[2,64,1024]{2,1,0:T(8,128)S(1)}, f32[2,64,1024]{2,1,0:T(8,128)}, u32[]{:S(2)}) copy-start(f32[2,64,1024]{2,1,0:T(8,128)} %first) | copy-start | bytes 1572868
  0.6 11.4 %copy-start.2 = (f32[2,64,1024]{2,1,0:T(8,128)S(1)}, f32[2,64,1024]{2,1,0:T(8,128)}, u32[]{:S(2)}) copy-start(f32[2,64,1024]{2,1,0:T(8,128)} %second) | copy-start | bytes 1572868
  5.1 15.4 %collective-permute-start = (bf16[256,256]{1,0:T(8,128)(2,1)S(1)}, bf16[256,256]{1,0:T(8,128)(2,1)S(1)}, u32[]{:S(2)}, u32[]{:S(2)}) collective-permute-start(bf16[256,256]{1,0:T(8,128)(2,1)S(1)} %get-tuple-element.53), channel_id=1, source_target_pairs={{0,1},{1,2},{2,3},{3,0},{4,5},{5,6},{6,7},{7,4},{8,9},{9,10},{10,1... | collective-permute-start | bytes 393224 | tf_op jit(solution)/shard_map/ppermute | solution.py:106
  8.1 12.4 %collective-permute-start.1 = (bf16[256,256]{1,0:T(8,128)(2,1)S(1)}, bf16[256,256]{1,0:T(8,128)(2,1)S(1)}, u32[]{:S(2)}, u32[]{:S(2)}) collective-permute-start(bf16[256,256]{1,0:T(8,128)(2,1)S(1)} %get-tuple-element.54), channel_id=1, source_target_pairs={{0,2},{1,3},{2,0},{3,1},{4,6},{5,7},{6,4},{7,5},{8,10},{9,11},{10,... | collective-permute-start | bytes 393224 | tf_op jit(solution)/shard_map/ppermute | solution.py:106
  10.7 9.8 %collective-permute-start.2 = (bf16[256,256]{1,0:T(8,128)(2,1)S(1)}, bf16[256,256]{1,0:T(8,128)(2,1)S(1)}, u32[]{:S(2)}, u32[]{:S(2)}) collective-permute-start(bf16[256,256]{1,0:T(8,128)(2,1)S(1)} %get-tuple-element.55), channel_id=1, source_target_pairs={{0,3},{1,0},{2,1},{3,2},{4,7},{5,4},{6,5},{7,6},{8,11},{9,8},{10,9... | collective-permute-start | bytes 393224 | tf_op jit(solution)/shard_map/ppermute | solution.py:106
  12.2 21.3 %collective-permute-start.6 = (bf16[2,2,64,1024]{3,2,1,0:T(8,128)(2,1)S(1)}, bf16[2,2,64,1024]{3,2,1,0:T(8,128)(2,1)S(1)}, u32[]{:S(2)}, u32[]{:S(2)}) collective-permute-start(bf16[2,2,64,1024]{3,2,1,0:T(8,128)(2,1)S(1)} %pad_maximum_fusion), channel_id=1, source_target_pairs={{0,16},{16,0},{1,17},{17,1},{2,18},{18,2},{3,19},{19,3},{4,20},{20... | collective-permute-start | bytes 1572872 | tf_op jit(solution)/shard_map/ppermute | solution.py:106
  19.7 0.8 %copy-start.3 = (bf16[1024,256]{1,0:T(8,128)(2,1)}, bf16[1024,256]{1,0:T(8,128)(2,1)S(1)}, u32[]{:S(2)}) copy-start(bf16[1024,256]{1,0:T(8,128)(2,1)S(1)} %first_product.2.rest_0_) | copy-start | bytes 1572868
  20.7 22.8 %copy-start.4 = (bf16[256,256]{1,0:T(8,128)(2,1)}, bf16[256,256]{1,0:T(8,128)(2,1)S(1)}, u32[]{:S(2)}) copy-start(bf16[256,256]{1,0:T(8,128)(2,1)S(1)} %total_low.1.rest_2_.rest_0_) | copy-start | bytes 393220
  20.7 11.6 %copy-start.8 = (s32[1,2,16]{2,1,0:T(2,128)S(1)}, s32[1,2,16]{2,1,0:T(2,128)}, u32[]{:S(2)}) copy-start(s32[1,2,16]{2,1,0:T(2,128)} %bounds.7) | copy-start | bytes 388
  20.7 15.4 %collective-permute-start.5 = (bf16[256,256]{1,0:T(8,128)(2,1)S(1)}, bf16[256,256]{1,0:T(8,128)(2,1)S(1)}, u32[]{:S(2)}, u32[]{:S(2)}) collective-permute-start(bf16[256,256]{1,0:T(8,128)(2,1)S(1)} %total_low.1.rest_2_.rest_0_), channel_id=1, source_target_pairs={{0,3},{1,0},{2,1},{3,2},{4,7},{5,4},{6,5},{7,6},{8,11},{9,8},{10,9... | collective-permute-start | bytes 393224 | tf_op jit(solution)/shard_map/ppermute | solution.py:106
  23.9 12.2 %collective-permute-start.4 = (bf16[256,256]{1,0:T(8,128)(2,1)S(1)}, bf16[256,256]{1,0:T(8,128)(2,1)S(1)}, u32[]{:S(2)}, u32[]{:S(2)}) collective-permute-start(bf16[256,256]{1,0:T(8,128)(2,1)S(1)} %total_low.1.rest_2_.rest_0_), channel_id=1, source_target_pairs={{0,2},{1,3},{2,0},{3,1},{4,6},{5,7},{6,4},{7,5},{8,10},{9,11},{10,... | collective-permute-start | bytes 393224 | tf_op jit(solution)/shard_map/ppermute | solution.py:106
  24.3 11.8 %collective-permute-start.3 = (bf16[256,256]{1,0:T(8,128)(2,1)S(1)}, bf16[256,256]{1,0:T(8,128)(2,1)S(1)}, u32[]{:S(2)}, u32[]{:S(2)}) collective-permute-start(bf16[256,256]{1,0:T(8,128)(2,1)S(1)} %total_low.1.rest_2_.rest_0_), channel_id=1, source_target_pairs={{0,1},{1,2},{2,3},{3,0},{4,5},{5,6},{6,7},{7,4},{8,9},{9,10},{10,1... | collective-permute-start | bytes 393224 | tf_op jit(solution)/shard_map/ppermute | solution.py:106
  31.3 1.0 %copy-start = (bf16[1024,512]{1,0:T(8,128)(2,1)}, bf16[1024,512]{1,0:T(8,128)(2,1)S(1)}, u32[]{:S(2)}) copy-start(bf16[1024,512]{1,0:T(8,128)(2,1)S(1)} %first_product.3.rest_1_) | copy-start | bytes 3145732
  36.1 7.4 %copy-start.5 = (bf16[256,256]{1,0:T(8,128)(2,1)}, bf16[256,256]{1,0:T(8,128)(2,1)S(1)}, u32[]{:S(2)}) copy-start(bf16[256,256]{1,0:T(8,128)(2,1)S(1)} %collective-permute-done.5.rest_5_.rest_3_) | copy-start | bytes 393220
  36.1 7.4 %copy-start.6 = (bf16[256,256]{1,0:T(8,128)(2,1)}, bf16[256,256]{1,0:T(8,128)(2,1)S(1)}, u32[]{:S(2)}) copy-start(bf16[256,256]{1,0:T(8,128)(2,1)S(1)} %collective-permute-done.4.rest_4_.rest_2_) | copy-start | bytes 393220
  36.2 7.4 %copy-start.7 = (bf16[256,256]{1,0:T(8,128)(2,1)}, bf16[256,256]{1,0:T(8,128)(2,1)S(1)}, u32[]{:S(2)}) copy-start(bf16[256,256]{1,0:T(8,128)(2,1)S(1)} %collective-permute-done.3.rest_3_.rest_1_) | copy-start | bytes 393220
  36.2 1.9 %copy-start.9 = (f32[16,128]{1,0:T(8,128)S(1)}, f32[16,128]{1,0:T(8,128)}, u32[]{:S(2)}) copy-start(f32[16,128]{1,0:T(8,128)} %rank_side.5) | copy-start | bytes 24580
  36.2 1.9 %copy-start.10 = (s32[1,16]{1,0:T(1,128)S(1)}, s32[1,16]{1,0:T(1,128)}, u32[]{:S(2)}) copy-start(s32[1,16]{1,0:T(1,128)} %owner.5) | copy-start | bytes 196
  37.8 4.5 %collective-permute-start.7 = (bf16[2,128,1024]{2,1,0:T(8,128)(2,1)S(1)}, bf16[2,128,1024]{2,1,0:T(8,128)(2,1)S(1)}, u32[]{:S(2)}, u32[]{:S(2)}) collective-permute-start(bf16[2,128,1024]{2,1,0:T(8,128)(2,1)S(1)} %inner_parts.1), channel_id=1, source_target_pairs={{0,4},{4,0},{12,8},{8,12},{1,5},{5,1},{13,9},{9,13},{2,6},{6,2},{1... | collective-permute-start | bytes 1572872 | tf_op jit(solution)/shard_map/ppermute | solution.py:757
  42.6 5.2 %collective-permute-start.8 = (bf16[2,64,1024]{2,1,0:T(8,128)(2,1)S(1)}, bf16[2,64,1024]{2,1,0:T(8,128)(2,1)S(1)}, u32[]{:S(2)}, u32[]{:S(2)}) collective-permute-start(bf16[2,64,1024]{2,1,0:T(8,128)(2,1)S(1)} %get-tuple-element.95), channel_id=1, source_target_pairs={{4,8},{8,4},{5,9},{9,5},{6,10},{10,6},{7,11},{11,7},{20,24},{24,20... | collective-permute-start | bytes 786440 | tf_op jit(solution)/shard_map/ppermute | solution.py:771
  49.2 19.6 %all-to-all-start = ((bf16[16,32,256]{2,1,0:T(8,128)(2,1)}), bf16[16,32,256]{2,1,0:T(8,128)(2,1)S(1)}, u32[]{:S(2)}, u32[]{:S(2)}) async-start(bf16[16,32,256]{2,1,0:T(8,128)(2,1)} %crossing_features.1), calls=%async_computation | async-start | bytes 524288 | tf_op jit(solution)/shard_map/all_to_all | solution.py:788

commit v6 on v5

--- a/solution.py
+++ b/solution.py
@@ -13,7 +13,7 @@
 BETA_TWO = 0.999
 EPSILON = 1e-08
 MIB = 2**20
-PIECES_VMEM, FIRST_VMEM, PREPARE_VMEM, SECOND_VMEM = 53.4, 48, 45, 54
+PIECES_VMEM, FIRST_VMEM, PREPARE_VMEM, SECOND_VMEM = 53.4, 48, 45, 46
 BF16 = jnp.bfloat16
 F32 = jnp.float32
 
@@ -39,9 +39,13 @@
     )
 
 
-def pieces_kernel(source_in, source_grad, down, up, *rest):
-    *outs, rows_in, rows_grad, down_buf, up_buf, sem = rest
+def pieces_kernel(source_in, source_grad, down, up, first, second, *rest):
+    *outs, moments, rows_in, rows_grad, partial, own, cast, down_buf, up_buf, sem, own_sem = rest
     size = len(outs)
+    own_copies = [
+        pltpu.make_async_copy(moment, own.at[i], own_sem.at[i])
+        for i, moment in enumerate((first, second))
+    ]
     place = lax.axis_index("tensor")
     tokens, width = rows_in.shape
     rows = tokens // size
@@ -58,47 +62,52 @@
         )
     copies.insert(0, pltpu.make_async_copy(down, down_buf, sem.at[0, size]))
     copies.insert(size + 1, pltpu.make_async_copy(up, up_buf, sem.at[1, size]))
-    for copy in copies:
+    for copy in copies[: size + 1] + own_copies + copies[size + 1 :]:
         copy.start()
-
-    def keep(product, first):
-        for i in range(size):
-            part = product[i * rows : (i + 1) * rows, :].astype(BF16)
-            for k, out in enumerate(outs):
-
-                @pl.when(lax.rem(place + k, size) == i)
-                def _():
-                    out[:, first : first + rank] = part
-
     for copy in copies[: size + 1]:
         copy.wait()
-    keep(jnp.dot(rows_in[...], down_buf[...], preferred_element_type=F32), 0)
+    product = jnp.dot(rows_in[...], down_buf[...], preferred_element_type=F32)
+    partial[:, :rank] = product.astype(BF16)
+    for i, copy in enumerate(own_copies):
+        copy.wait()
+        cast[i] = own[i].astype(BF16)
+    cast_copy = pltpu.make_async_copy(cast, moments, own_sem.at[2])
+    cast_copy.start()
     for copy in copies[size + 1 :]:
         copy.wait()
-    keep(dot_trailing(rows_grad[...], up_buf[...]), rank)
-
-
-def rank_pieces(rows_in, rows_grad, down, up, size):
+    partial[:, rank:] = dot_trailing(rows_grad[...], up_buf[...]).astype(BF16)
+    for k, out in enumerate(outs):
+        block = pl.multiple_of(lax.rem(place + k, size) * rows, rows)
+        out[...] = partial[pl.ds(block, rows), :]
+    cast_copy.wait()
+
+
+def rank_pieces(rows_in, rows_grad, down, up, first, second, size):
     tokens, width = rows_in.shape
     rank = up.shape[0]
     rows = tokens // size
     return call(
         pieces_kernel,
-        [jax.ShapeDtypeStruct((rows, 2 * rank), BF16)] * size,
-        [HBM] * 4,
-        [VMEM] * size,
+        [jax.ShapeDtypeStruct((rows, 2 * rank), BF16)] * size
+        + [jax.ShapeDtypeStruct((2,) + first.shape, BF16)],
+        [HBM] * 6,
+        [VMEM] * size + [HBM],
         [
             pltpu.VMEM((tokens, width), BF16),
             pltpu.VMEM((tokens, width), BF16),
+            pltpu.VMEM((tokens, 2 * rank), BF16),
+            pltpu.VMEM((2,) + first.shape, F32),
+            pltpu.VMEM((2,) + first.shape, BF16),
             pltpu.VMEM(down.shape, BF16),
             pltpu.VMEM(up.shape, BF16),
             pltpu.SemaphoreType.DMA((2, size + 1)),
+            pltpu.SemaphoreType.DMA((3,)),
         ],
         4 * tokens * width * rank,
         4 * tokens * width,
         "rank_pieces",
         PIECES_VMEM,
-    )(rows_in, rows_grad, down, up)
+    )(rows_in, rows_grad, down, up, first, second)
 
 
 def shifted(value, axis, shift):
@@ -200,13 +209,13 @@
 
 def inner_kernel(size, bounds, rows_in, rows_grad, *rest):
     pieces = rest[:size]
-    out, low_scratch, acc = rest[size:]
+    out, ordered, acc = rest[size:]
     tokens = rows_in.shape[0]
     low, first, last = example_scalars(bounds, tokens)
     inner = edges(bounds, low, first, last, tokens)[0]
     for m, source in enumerate((rows_in, rows_grad)):
-        place_pieces(pieces, m, low_scratch)
-        sum_part(acc, source, low_scratch, low, bounds[0, 0, inner], bounds[0, 1, inner])
+        place_pieces(pieces, m, ordered.at[m])
+        sum_part(acc, source, ordered.at[m], low, bounds[0, 0, inner], bounds[0, 1, inner])
         out[m] = (ADAPTER_SCALE * acc[...]).astype(BF16)
 
 
@@ -216,10 +225,13 @@
     tokens, width = rows_in.shape
     return call(
         functools.partial(inner_kernel, size),
-        jax.ShapeDtypeStruct((2, rank, width), BF16),
+        [
+            jax.ShapeDtypeStruct((2, rank, width), BF16),
+            jax.ShapeDtypeStruct((2, size, rank, rows), BF16),
+        ],
         [SMEM] + [VMEM] * (2 + size),
-        VMEM,
-        [pltpu.VMEM((size, rank, rows), BF16), pltpu.VMEM((rank, width), F32)],
+        [VMEM, VMEM],
+        [pltpu.VMEM((rank, width), F32)],
         4 * tokens * width * rank,
         4 * tokens * width,
         "inner_parts",
@@ -264,16 +276,16 @@
 STEP = 16
 
 
-def slots_kernel(m, size, bounds, owner, source, moments, rank_side, width_side, *rest):
-    pieces = rest[:size]
-    out, outer_part, low_scratch, acc, normed, blocks, ranked, wide = rest[size:]
+def slots_kernel(m, bounds, owner, source, moments, rank_side, width_side, ordered, *rest):
+    out, outer_part, acc, normed, blocks, ranked, wide = rest
+    size = ordered.shape[1]
     tokens = source.shape[0]
+    rows = tokens // size
     rank, width = outer_part.shape
     lines = rank_side.shape[0]
     low, first, last = example_scalars(bounds, tokens)
     count = bounds.shape[2]
     _, outer, _, outer_on, _ = edges(bounds, low, first, last, tokens)
-    place_pieces(pieces, m, low_scratch)
     rank_side_pair(rank_side, blocks)
 
     def slot(j):
@@ -283,32 +295,49 @@
         starts, ends = fits(bounds, slot(j), low, tokens)
         return (first + j <= last) & starts & ends
 
-    @pl.loop(0, TOUCH)
-    def _(j):
-        here = inside(j)
-        is_outer = (first + j == outer) & outer_on
-
-        @pl.when(here | is_outer)
-        def _():
-            start, end = bounds[0, 0, slot(j)], bounds[0, 1, slot(j)]
-            sum_part(acc, source, low_scratch, low, start, end)
-
-        @pl.when(is_outer)
-        def _():
-            outer_part[...] = (ADAPTER_SCALE * acc[...]).astype(BF16)
-
-        @pl.when(here)
-        def _():
-            for r in range(0, rank, STEP):
-                normed[j, r : r + STEP, :] = normalize(
-                    ADAPTER_SCALE * acc[r : r + STEP, :],
-                    moments[0, m, r : r + STEP, :],
-                    moments[1, m, r : r + STEP, :],
-                ).astype(BF16)
-
-        @pl.when(~here)
-        def _():
-            normed[j] = jnp.zeros((rank, width), BF16)
+    @pl.loop(0, TOUCH // 2)
+    def _(pair):
+        slots = (2 * pair, 2 * pair + 1)
+        here = [inside(j) for j in slots]
+        is_outer = [(first + j == outer) & outer_on for j in slots]
+        wanted = [h | o for h, o in zip(here, is_outer)]
+        starts = [jnp.where(w, bounds[0, 0, slot(j)], 0) for w, j in zip(wanted, slots)]
+        ends = [jnp.where(w, bounds[0, 1, slot(j)], 0) for w, j in zip(wanted, slots)]
+        begin_pair = jnp.where(wanted[0], starts[0], starts[1])
+        end_pair = jnp.where(wanted[1], ends[1], ends[0])
+        for c in range(size):
+            begin = low + c * rows
+
+            @pl.when((begin_pair < begin + rows) & (end_pair > begin))
+            def _():
+                left = jnp.concatenate(
+                    [masked(ordered[m, c], begin, s, e) for s, e in zip(starts, ends)], axis=0
+                )
+                term = jnp.dot(
+                    left, source[c * rows : (c + 1) * rows, :], preferred_element_type=F32
+                )
+                fresh = (begin_pair >= begin) | (c == 0)
+                acc[...] = jnp.where(fresh, 0.0, acc[...]) + term
+
+        for k, j in enumerate(slots):
+
+            @pl.when(is_outer[k])
+            def _():
+                part = ADAPTER_SCALE * acc[k * rank : (k + 1) * rank, :]
+                outer_part[...] = part.astype(BF16)
+
+            @pl.when(here[k])
+            def _():
+                for r in range(0, rank, STEP):
+                    normed[j, r : r + STEP, :] = normalize(
+                        ADAPTER_SCALE * acc[k * rank + r : k * rank + r + STEP, :],
+                        moments[0, m, r : r + STEP, :],
+                        moments[1, m, r : r + STEP, :],
+                    ).astype(BF16)
+
+            @pl.when(~here[k])
+            def _():
+                normed[j] = jnp.zeros((rank, width), BF16)
 
     for j in range(0, TOUCH, 2):
         ranked[j * lines : (j + 2) * lines, :] = project_rank(
@@ -323,23 +352,21 @@
             out[owner[0, slot(j)]] = wide[j].astype(BF16)
 
 
-def slot_features(m, bounds, owner, source, moments, rank_side, width_side, pieces, name):
-    size = len(pieces)
-    rank, rows = pieces[0].shape[0] // 2, pieces[0].shape[1]
+def slot_features(m, bounds, owner, source, moments, rank_side, width_side, ordered, name):
+    rank = ordered.shape[2]
     tokens, width = source.shape
     lines = rank_side.shape[0]
     columns = width_side.shape[1]
     return call(
-        functools.partial(slots_kernel, m, size),
+        functools.partial(slots_kernel, m),
         [
             jax.ShapeDtypeStruct((owner.shape[1], lines, columns), BF16),
             jax.ShapeDtypeStruct((rank, width), BF16),
         ],
-        [SMEM, SMEM] + [VMEM] * (4 + size),
+        [SMEM, SMEM] + [VMEM] * 5,
         [VMEM, VMEM],
         [
-            pltpu.VMEM((size, rank, rows), BF16),
-            pltpu.VMEM((rank, width), F32),
+            pltpu.VMEM((2 * rank, width), F32),
             pltpu.VMEM((TOUCH, rank, width), BF16),
             pltpu.VMEM((4 * lines, 2 * rank), BF16),
             pltpu.VMEM((TOUCH * lines, width), F32),
@@ -348,7 +375,7 @@
         2 * tokens * width * rank * TOUCH,
         4 * tokens * width,
         name,
-    )(bounds, owner, source, moments, rank_side, width_side, *pieces)
+    )(bounds, owner, source, moments, rank_side, width_side, ordered)
 
 
 def crossing_kernel(
@@ -657,11 +684,10 @@
         copy.wait()
 
 
-def other_moments(first, second):
-    sent = jnp.stack([first, second]).astype(BF16)
+def other_moments(own):
     if lax.axis_size("dp") != 2:
-        return lax.all_gather(sent, "dp", axis=2, tiled=True)
-    return shifted(sent, "dp", 1)
+        return lax.all_gather(own, "dp", axis=2, tiled=True)
+    return shifted(own, "dp", 1)
 
 
 def prepare(rows_in, rows_grad, width_side, first, second, other):
@@ -710,12 +736,11 @@
     rows_in = attention_output_rows.reshape(blk, width_local)
     rows_grad = projection_result_gradient.reshape(blk, width)
 
-    pieces = rank_pieces(rows_in, rows_grad, adapter_down_weight, adapter_up_weight, size)
-    pieces, own_moments = lax.optimization_barrier(
-        (pieces, (adam_first_moments, adam_second_moments))
-    )
-    other = other_moments(*own_moments)
-
+    own_moments = (adam_first_moments, adam_second_moments)
+    *pieces, sent_moments = rank_pieces(
+        rows_in, rows_grad, adapter_down_weight, adapter_up_weight, *own_moments, size
+    )
+    other = other_moments(sent_moments)
     cuts = [0, width_local // 4, 3 * width_local // 4]
 
     def product(rows, k):
@@ -742,7 +767,7 @@
         (gather_pieces(total), prepared, done, spans)
     )
     rows_in, columns_grad, right, moments = prepared
-    inner = inner_parts(bounds, rows_in, columns_grad, low)
+    inner, ordered = inner_parts(bounds, rows_in, columns_grad, low)
     shared = (rank_side_projection, right)
     seq = lax.axis_size("seq")
     middle = seq // 2
@@ -761,7 +786,7 @@
         arrived.append(moved)
         outgoing = onward(arrived[-1]).astype(BF16)
     filled_in, outer_in = slot_features(
-        1, bounds, example_owner_slot, columns_grad, moments, *shared, low, "slots_in"
+        1, bounds, example_owner_slot, columns_grad, moments, *shared, ordered, "slots_in"
     )
     arrived, rows_in, outer_in = lax.optimization_barrier((arrived, rows_in, outer_in))
     summed = onward(arrived[-1]).astype(BF16)
@@ -770,7 +795,7 @@
     sent = jnp.where(left, summed[:, half:], summed[:, :half])
     received = lax.ppermute(sent, "seq", [(middle - 1, middle), (middle, middle - 1)])
     filled_grad, outer_grad = slot_features(
-        0, bounds, example_owner_slot, rows_in, moments, *shared, low, "slots_grad"
+        0, bounds, example_owner_slot, rows_in, moments, *shared, ordered, "slots_grad"
     )
     received, outer_grad = lax.optimization_barrier((received, outer_grad))
     buffer = crossing_features(

time: 69.6 us -> 68.1 us (0.978)
  local copies, waits for them, and re-layouts: 1.83 us -> 0.04 us
  Pallas kernels: 41.6 us -> 40.1 us
  starting transfers between devices: 23 us -> 24.4 us
  waiting for transfers between devices: 0.46 us -> 1.67 us
    unnamed x22 -> x12, local copies, waits for them, and re-layouts: 1.83 us -> 0.04 us
    ppermute x7, starting transfers between devices: 12.4 us -> 14.1 us  [shifted(): lax.ppermute(value, axis, [(i, (i + shift) % size) for i in range(size)])]
    pallas_call x1, Pallas kernels: 9.69 us -> 8.41 us  [second_product(): call(functools.partial(second_kernel, size, count), jax.ShapeDtypeStruct(...]
    all_to_all x1, waiting for transfers between devices: 0.37 us -> 1.64 us  [per_device(): lax.all_to_all(buffer, ('seq', 'tensor'), split_axis=0, concat_axis=0, ti...]
  transfers between devices with their start and end apart: 10 -> 10, of which waited for: 2 -> 1; matrix products, arithmetic and copies ran while one was open for 1% -> 1% of each run, Pallas kernels for 48% -> 46%
where the time goes in v6:
time: 68.1 us; the launch traced here: 68.6 us
  Pallas kernels  40.1 us (59%)
  starting transfers between devices  24.4 us (36%)
  waiting for transfers between devices  1.67 us (2%)
  between operations  1.54 us (2%)
  other arithmetic  0.88 us (1%)
    ppermute x7, starting transfers between devices, shifted(): lax.ppermute(value, axis, [(i, (i + shift) % size) for i in range(size)])  14.1 us
    pallas_call x2, Pallas kernels, first_product(): call(functools.partial(first_kernel, column), jax.ShapeDtypeStruct((token...  12.6 us
    all_to_all x1, starting transfers between devices, per_device(): lax.all_to_all(buffer, ('seq', 'tensor'), split_axis=0, concat_axis=0, ti...  8.99 us
    pallas_call x1, Pallas kernels, second_product(): call(functools.partial(second_kernel, size, count), jax.ShapeDtypeStruct(...  8.41 us
    pallas_call x2, Pallas kernels, slot_features(): call(functools.partial(slots_kernel, m), [jax.ShapeDtypeStruct((owner.sha...  8.08 us
    pallas_call x1, Pallas kernels, rank_pieces(): call(pieces_kernel, [jax.ShapeDtypeStruct((rows, 2 * rank), BF16)] * size...  4.3 us
    pallas_call x1, Pallas kernels, prepare(): call(prepare_kernel, [jax.ShapeDtypeStruct((tokens, width), BF16), jax.Sh...  2.48 us
    pallas_call x1, Pallas kernels, inner_parts(): call(functools.partial(inner_kernel, size), [jax.ShapeDtypeStruct((2, ran...  2.03 us
  transfers between devices with their start and end apart: 10, of which 1 were waited for; matrix products, arithmetic and copies ran while one was open for 1% of the time, Pallas kernels for 46%

profile of v6, /device:TPU:0, one launch (start us, length us, event | category | flops | bytes accessed | tf_op | source)
XLA Modules:
  0.0 68.6 jit_solution(8687238897026496745)
XLA Ops:
  0.6 4.3 %rank_pieces.1 = (bf16[256,256]{1,0:T(8,128)(2,1)S(1)}, bf16[256,256]{1,0:T(8,128)(2,1)S(1)}, bf16[256,256]{1,0:T(8,128)(2,1)S(1)}, bf16[256,256]{1,0:T(8,128)(2,1)S(1)}, bf16[2,2,64,1024]{3,2,1,0:T(8,128)(2,1)}) custom-call(bf16[1024,1024]{1,0:T(8,128)(2,1)} %bitcast.9, bf16[1024,4096]{1,0:T(8,128)(2,1)} %bitcast.4, bf16[1024,128]{1,0:T(8,128)(2,1)} %down.3, ...), custom_call_target="tpu_custom_call" | custom-call | flops 536870912 | bytes 4194304 | tf_op jit(solution)/shard_map/rank_pieces/pallas_call | solution.py:89
  4.9 3.1 %collective-permute-start = (bf16[256,256]{1,0:T(8,128)(2,1)S(1)}, bf16[256,256]{1,0:T(8,128)(2,1)S(1)}, u32[]{:S(2)}, u32[]{:S(2)}) collective-permute-start(bf16[256,256]{1,0:T(8,128)(2,1)S(1)} %get-tuple-element.46), channel_id=1, source_target_pairs={{0,1},{1,2},{2,3},{3,0},{4,5},{5,6},{6,7},{7,4},{8,9},{9,10},{10,1... | collective-permute-start | bytes 393224 | tf_op jit(solution)/shard_map/ppermute | solution.py:115
  8.0 2.6 %collective-permute-start.1 = (bf16[256,256]{1,0:T(8,128)(2,1)S(1)}, bf16[256,256]{1,0:T(8,128)(2,1)S(1)}, u32[]{:S(2)}, u32[]{:S(2)}) collective-permute-start(bf16[256,256]{1,0:T(8,128)(2,1)S(1)} %get-tuple-element.47), channel_id=1, source_target_pairs={{0,2},{1,3},{2,0},{3,1},{4,6},{5,7},{6,4},{7,5},{8,10},{9,11},{10,... | collective-permute-start | bytes 393224 | tf_op jit(solution)/shard_map/ppermute | solution.py:115
  10.6 1.3 %collective-permute-start.2 = (bf16[256,256]{1,0:T(8,128)(2,1)S(1)}, bf16[256,256]{1,0:T(8,128)(2,1)S(1)}, u32[]{:S(2)}, u32[]{:S(2)}) collective-permute-start(bf16[256,256]{1,0:T(8,128)(2,1)S(1)} %get-tuple-element.48), channel_id=1, source_target_pairs={{0,3},{1,0},{2,1},{3,2},{4,7},{5,4},{6,5},{7,6},{8,11},{9,8},{10,9... | collective-permute-start | bytes 393224 | tf_op jit(solution)/shard_map/ppermute | solution.py:115
  12.0 1.5 %collective-permute-start.6 = (bf16[2,2,64,1024]{3,2,1,0:T(8,128)(2,1)}, bf16[2,2,64,1024]{3,2,1,0:T(8,128)(2,1)S(1)}, u32[]{:S(2)}, u32[]{:S(2)}) collective-permute-start(bf16[2,2,64,1024]{3,2,1,0:T(8,128)(2,1)} %get-tuple-element.56), channel_id=1, source_target_pairs={{0,16},{16,0},{1,17},{17,1},{2,18},{18,2},{3,19},{19,3},{4,20},{20... | collective-permute-start | bytes 1572872 | tf_op jit(solution)/shard_map/ppermute | solution.py:115
  13.4 5.9 %first_product.2.rest_0_ = bf16[1024,256]{1,0:T(8,128)(2,1)S(1)} custom-call(bf16[1024,4096]{1,0:T(8,128)(2,1)} %bitcast.5, bf16[1024,4096]{1,0:T(8,128)(2,1)} %weight.5), custom_call_target="tpu_custom_call" | custom-call | flops 2147483648 | bytes 10485760 | tf_op jit(solution)/shard_map/first_product/pallas_call | solution.py:606
  19.4 0.0 collective-permute-done.1.refs_2_
  19.4 0.0 collective-permute-done.2.refs_3_
  19.4 0.1 total_low.1.rest_2_.rest_0_
  19.6 0.0 copy-start.3
  19.6 0.0 copy-start
  19.6 0.0 copy-start.1
  19.6 3.2 %collective-permute-start.3 = (bf16[256,256]{1,0:T(8,128)(2,1)S(1)}, bf16[256,256]{1,0:T(8,128)(2,1)S(1)}, u32[]{:S(2)}, u32[]{:S(2)}) collective-permute-start(bf16[256,256]{1,0:T(8,128)(2,1)S(1)} %total_low.1.rest_2_.rest_0_), channel_id=1, source_target_pairs={{0,1},{1,2},{2,3},{3,0},{4,5},{5,6},{6,7},{7,4},{8,9},{9,10},{10,1... | collective-permute-start | bytes 393224 | tf_op jit(solution)/shard_map/ppermute | solution.py:115
  22.8 1.6 %collective-permute-start.4 = (bf16[256,256]{1,0:T(8,128)(2,1)S(1)}, bf16[256,256]{1,0:T(8,128)(2,1)S(1)}, u32[]{:S(2)}, u32[]{:S(2)}) collective-permute-start(bf16[256,256]{1,0:T(8,128)(2,1)S(1)} %total_low.1.rest_2_.rest_0_), channel_id=1, source_target_pairs={{0,2},{1,3},{2,0},{3,1},{4,6},{5,7},{6,4},{7,5},{8,10},{9,11},{10,... | collective-permute-start | bytes 393224 | tf_op jit(solution)/shard_map/ppermute | solution.py:115
  24.4 0.8 %collective-permute-start.5 = (bf16[256,256]{1,0:T(8,128)(2,1)S(1)}, bf16[256,256]{1,0:T(8,128)(2,1)}, u32[]{:S(2)}, u32[]{:S(2)}) collective-permute-start(bf16[256,256]{1,0:T(8,128)(2,1)S(1)} %total_low.1.rest_2_.rest_0_), channel_id=1, source_target_pairs={{0,3},{1,0},{2,1},{3,2},{4,7},{5,4},{6,5},{7,6},{8,11},{9,8},{10,9... | collective-permute-start | bytes 393224 | tf_op jit(solution)/shard_map/ppermute | solution.py:115
  25.2 6.7 %first_product.3.rest_1_ = bf16[1024,512]{1,0:T(8,128)(2,1)S(1)} custom-call(bf16[1024,4096]{1,0:T(8,128)(2,1)} %bitcast.6, bf16[1024,4096]{1,0:T(8,128)(2,1)} %weight.5), custom_call_target="tpu_custom_call" | custom-call | flops 4294967296 | bytes 12582912 | tf_op jit(solution)/shard_map/first_product/pallas_call | solution.py:606
  31.9 0.6 select_reduce_fusion
  33.2 2.5 %prepare.1 = (bf16[1024,1024]{1,0:T(8,128)(2,1)S(1)}, bf16[1024,1024]{1,0:T(8,128)(2,1)S(1)}, bf16[1024,256]{1,0:T(8,128)(2,1)S(1)}, f32[2,2,128,1024]{3,2,1,0:T(8,128)S(1)}) custom-call(bf16[1024,1024]{1,0:T(8,128)(2,1)} %bitcast.10, bf16[1024,4096]{1,0:T(8,128)(2,1)} %bitcast.7, bf16[4096,256]{1,0:T(8,128)(2,1)} %width_side.1, f32[2,64,1024]{2,1,0:T(8,128)S(1)} %copy-done, ...), custom_call_target="tpu_custom_call" | custom-call | flops 1048576 | bytes 5242880 | tf_op jit(solution)/shard_map/prepare/pallas_call | solution.py:697
  35.7 0.0 copy-start.4
  35.8 0.0 copy-start.5
  35.8 2.0 %inner_parts.1 = (bf16[2,128,1024]{2,1,0:T(8,128)(2,1)S(1)}, bf16[2,4,128,256]{3,2,1,0:T(8,128)(2,1)S(1)}) custom-call(s32[1,2,16]{2,1,0:T(2,128)S(1)} %copy-done.3, bf16[1024,1024]{1,0:T(8,128)(2,1)S(1)} %get-tuple-element.79.rows_in.source, bf16[1024,1024]{1,0:T(8,128)(2,1)S(1)} %get-tuple-element.73.rows_grad.source, ...), custom_call_target="tpu_custom_call" | custom-call | flops 536870912 | bytes 4194304 | tf_op jit(solution)/shard_map/inner_parts/pallas_call | solution.py:226
  37.8 0.4 collective-permute-start.7
  38.3 4.0 %slots_in.1 = (bf16[16,16,256]{2,1,0:T(8,128)(2,1)S(1)}, bf16[128,1024]{1,0:T(8,128)(2,1)S(1)}) custom-call(s32[1,2,16]{2,1,0:T(2,128)S(1)} %copy-done.3, s32[1,16]{1,0:T(1,128)S(1)} %copy-done.5, bf16[1024,1024]{1,0:T(8,128)(2,1)S(1)} %get-tuple-element.73.rows_grad.source, f32[2,2,128,1024]{3,2,1,0:T(8,128)S(1)} %get-tuple-element.75.moments, ...), custom_call_target="tpu_custom_call" | custom-call | flops 2147483648 | bytes 4194304 | tf_op jit(solution)/shard_map/slots_in/pallas_call | solution.py:360
  42.3 0.2 add_convert_fusion
  42.6 0.9 %collective-permute-start.8 = (bf16[2,64,1024]{2,1,0:T(8,128)(2,1)S(1)}, bf16[2,64,1024]{2,1,0:T(8,128)(2,1)S(1)}, u32[]{:S(2)}, u32[]{:S(2)}) collective-permute-start(bf16[2,64,1024]{2,1,0:T(8,128)(2,1)S(1)} %get-tuple-element.89), channel_id=1, source_target_pairs={{4,8},{8,4},{5,9},{9,5},{6,10},{10,6},{7,11},{11,7},{20,24},{24,20... | collective-permute-start | bytes 786440 | tf_op jit(solution)/shard_map/ppermute | solution.py:796
  43.4 4.0 %slots_grad.1 = (bf16[16,16,256]{2,1,0:T(8,128)(2,1)S(1)}, bf16[128,1024]{1,0:T(8,128)(2,1)S(1)}) custom-call(s32[1,2,16]{2,1,0:T(2,128)S(1)} %copy-done.3, s32[1,16]{1,0:T(1,128)S(1)} %copy-done.5, bf16[1024,1024]{1,0:T(8,128)(2,1)S(1)} %get-tuple-element.79.rows_in.source, f32[2,2,128,1024]{3,2,1,0:T(8,128)S(1)} %get-tuple-element.75.moments, ...), custom_call_target="tpu_custom_call" | custom-call | flops 2147483648 | bytes 4194304 | tf_op jit(solution)/shard_map/slots_grad/pallas_call | solution.py:360
  47.5 0.0 copy-start.2
  47.5 1.3 %crossing_features.1 = bf16[16,32,256]{2,1,0:T(8,128)(2,1)} custom-call(s32[1,2,16]{2,1,0:T(2,128)S(1)} %copy-done.3, s32[1,16]{1,0:T(1,128)S(1)} %copy-done.5, bf16[16,16,256]{2,1,0:T(8,128)(2,1)S(1)} %get-tuple-element.80.filled_grad, bf16[16,16,256]{2,1,0:T(8,128)(2,1)S(1)} %get-tuple-element.81.filled_in, ...), custom_call_target="tpu_custom_call" | custom-call | flops 134217728 | bytes 1572864 | tf_op jit(solution)/shard_map/crossing_features/pallas_call | solution.py:457
  48.9 9.0 %all-to-all-start = ((bf16[16,32,256]{2,1,0:T(8,128)(2,1)}), bf16[16,32,256]{2,1,0:T(8,128)(2,1)S(1)}, u32[]{:S(2)}, u32[]{:S(2)}) async-start(bf16[16,32,256]{2,1,0:T(8,128)(2,1)} %crossing_features.1), calls=%async_computation | async-start | bytes 524288 | tf_op jit(solution)/shard_map/all_to_all | solution.py:813
  57.9 8.4 %second_product.1 = bf16[1024,1024]{1,0:T(8,128)(2,1)} custom-call(bf16[1024,4096]{1,0:T(8,128)(2,1)} %bitcast.8, bf16[1024,4096]{1,0:T(8,128)(2,1)} %weight.5, bf16[1024,128]{1,0:T(8,128)(2,1)S(1)} %copy-done.2, bf16[1024,256]{1,0:T(8,128)(2,1)S(1)} %first_product.2.rest_0_, bf16[1024,512]{1,0:T(8,128)(2,1)S(1)} %first_product.3.rest_1_, ...), custom_call_target="tpu_custom_call" | custom-call | flops 2147483648 | bytes 10485760 | tf_op jit(solution)/shard_map/second_product/pallas_call | solution.py:629
  66.3 1.6 %all-to-all-done.arrived = bf16[16,32,256]{2,1,0:T(8,128)(2,1)S(1)} async-done(((bf16[16,32,256]{2,1,0:T(8,128)(2,1)}), bf16[16,32,256]{2,1,0:T(8,128)(2,1)S(1)}, u32[]{:S(2)}, u32[]{:S(2)}) %all-to-all-start) | async-done | bytes 262176 | tf_op jit(solution)/shard_map/all_to_all | solution.py:813
  67.9 0.7 owned_features.1
  (14 shorter events, 0.1 us)
Async XLA Ops:
  4.9 14.5 %collective-permute-start = (bf16[256,256]{1,0:T(8,128)(2,1)S(1)}, bf16[256,256]{1,0:T(8,128)(2,1)S(1)}, u32[]{:S(2)}, u32[]{:S(2)}) collective-permute-start(bf16[256,256]{1,0:T(8,128)(2,1)S(1)} %get-tuple-element.46), channel_id=1, source_target_pairs={{0,1},{1,2},{2,3},{3,0},{4,5},{5,6},{6,7},{7,4},{8,9},{9,10},{10,1... | collective-permute-start | bytes 393224 | tf_op jit(solution)/shard_map/ppermute | solution.py:115
  8.0 11.4 %collective-permute-start.1 = (bf16[256,256]{1,0:T(8,128)(2,1)S(1)}, bf16[256,256]{1,0:T(8,128)(2,1)S(1)}, u32[]{:S(2)}, u32[]{:S(2)}) collective-permute-start(bf16[256,256]{1,0:T(8,128)(2,1)S(1)} %get-tuple-element.47), channel_id=1, source_target_pairs={{0,2},{1,3},{2,0},{3,1},{4,6},{5,7},{6,4},{7,5},{8,10},{9,11},{10,... | collective-permute-start | bytes 393224 | tf_op jit(solution)/shard_map/ppermute | solution.py:115
  10.6 8.8 %collective-permute-start.2 = (bf16[256,256]{1,0:T(8,128)(2,1)S(1)}, bf16[256,256]{1,0:T(8,128)(2,1)S(1)}, u32[]{:S(2)}, u32[]{:S(2)}) collective-permute-start(bf16[256,256]{1,0:T(8,128)(2,1)S(1)} %get-tuple-element.48), channel_id=1, source_target_pairs={{0,3},{1,0},{2,1},{3,2},{4,7},{5,4},{6,5},{7,6},{8,11},{9,8},{10,9... | collective-permute-start | bytes 393224 | tf_op jit(solution)/shard_map/ppermute | solution.py:115
  12.0 21.2 %collective-permute-start.6 = (bf16[2,2,64,1024]{3,2,1,0:T(8,128)(2,1)}, bf16[2,2,64,1024]{3,2,1,0:T(8,128)(2,1)S(1)}, u32[]{:S(2)}, u32[]{:S(2)}) collective-permute-start(bf16[2,2,64,1024]{3,2,1,0:T(8,128)(2,1)} %get-tuple-element.56), channel_id=1, source_target_pairs={{0,16},{16,0},{1,17},{17,1},{2,18},{18,2},{3,19},{19,3},{4,20},{20... | collective-permute-start | bytes 1572872 | tf_op jit(solution)/shard_map/ppermute | solution.py:115
  19.6 12.3 %copy-start.3 = (s32[1,2,16]{2,1,0:T(2,128)S(1)}, s32[1,2,16]{2,1,0:T(2,128)}, u32[]{:S(2)}) copy-start(s32[1,2,16]{2,1,0:T(2,128)} %bounds.7) | copy-start | bytes 388
  19.6 13.6 %copy-start = (f32[2,64,1024]{2,1,0:T(8,128)S(1)}, f32[2,64,1024]{2,1,0:T(8,128)}, u32[]{:S(2)}) copy-start(f32[2,64,1024]{2,1,0:T(8,128)} %first.3) | copy-start | bytes 1572868
  19.6 13.6 %copy-start.1 = (f32[2,64,1024]{2,1,0:T(8,128)S(1)}, f32[2,64,1024]{2,1,0:T(8,128)}, u32[]{:S(2)}) copy-start(f32[2,64,1024]{2,1,0:T(8,128)} %second.3) | copy-start | bytes 1572868
  19.6 16.1 %collective-permute-start.3 = (bf16[256,256]{1,0:T(8,128)(2,1)S(1)}, bf16[256,256]{1,0:T(8,128)(2,1)S(1)}, u32[]{:S(2)}, u32[]{:S(2)}) collective-permute-start(bf16[256,256]{1,0:T(8,128)(2,1)S(1)} %total_low.1.rest_2_.rest_0_), channel_id=1, source_target_pairs={{0,1},{1,2},{2,3},{3,0},{4,5},{5,6},{6,7},{7,4},{8,9},{9,10},{10,1... | collective-permute-start | bytes 393224 | tf_op jit(solution)/shard_map/ppermute | solution.py:115
  22.8 13.0 %collective-permute-start.4 = (bf16[256,256]{1,0:T(8,128)(2,1)S(1)}, bf16[256,256]{1,0:T(8,128)(2,1)S(1)}, u32[]{:S(2)}, u32[]{:S(2)}) collective-permute-start(bf16[256,256]{1,0:T(8,128)(2,1)S(1)} %total_low.1.rest_2_.rest_0_), channel_id=1, source_target_pairs={{0,2},{1,3},{2,0},{3,1},{4,6},{5,7},{6,4},{7,5},{8,10},{9,11},{10,... | collective-permute-start | bytes 393224 | tf_op jit(solution)/shard_map/ppermute | solution.py:115
  24.4 11.3 %collective-permute-start.5 = (bf16[256,256]{1,0:T(8,128)(2,1)S(1)}, bf16[256,256]{1,0:T(8,128)(2,1)}, u32[]{:S(2)}, u32[]{:S(2)}) collective-permute-start(bf16[256,256]{1,0:T(8,128)(2,1)S(1)} %total_low.1.rest_2_.rest_0_), channel_id=1, source_target_pairs={{0,3},{1,0},{2,1},{3,2},{4,7},{5,4},{6,5},{7,6},{8,11},{9,8},{10,9... | collective-permute-start | bytes 393224 | tf_op jit(solution)/shard_map/ppermute | solution.py:115
  35.7 2.5 %copy-start.4 = (f32[16,128]{1,0:T(8,128)S(1)}, f32[16,128]{1,0:T(8,128)}, u32[]{:S(2)}) copy-start(f32[16,128]{1,0:T(8,128)} %rank_side.5) | copy-start | bytes 24580
  35.8 2.5 %copy-start.5 = (s32[1,16]{1,0:T(1,128)S(1)}, s32[1,16]{1,0:T(1,128)}, u32[]{:S(2)}) copy-start(s32[1,16]{1,0:T(1,128)} %owner.5) | copy-start | bytes 196
  37.8 4.5 %collective-permute-start.7 = (bf16[2,128,1024]{2,1,0:T(8,128)(2,1)S(1)}, bf16[2,128,1024]{2,1,0:T(8,128)(2,1)S(1)}, u32[]{:S(2)}, u32[]{:S(2)}) collective-permute-start(bf16[2,128,1024]{2,1,0:T(8,128)(2,1)S(1)} %get-tuple-element.74), channel_id=1, source_target_pairs={{0,4},{4,0},{12,8},{8,12},{1,5},{5,1},{13,9},{9,13},{2,6},{6,2},{1... | collective-permute-start | bytes 1572872 | tf_op jit(solution)/shard_map/ppermute | solution.py:782
  42.6 4.9 %collective-permute-start.8 = (bf16[2,64,1024]{2,1,0:T(8,128)(2,1)S(1)}, bf16[2,64,1024]{2,1,0:T(8,128)(2,1)S(1)}, u32[]{:S(2)}, u32[]{:S(2)}) collective-permute-start(bf16[2,64,1024]{2,1,0:T(8,128)(2,1)S(1)} %get-tuple-element.89), channel_id=1, source_target_pairs={{4,8},{8,4},{5,9},{9,5},{6,10},{10,6},{7,11},{11,7},{20,24},{24,20... | collective-permute-start | bytes 786440 | tf_op jit(solution)/shard_map/ppermute | solution.py:796
  47.5 10.3 %copy-start.2 = (bf16[1024,128]{1,0:T(8,128)(2,1)S(1)}, bf16[1024,128]{1,0:T(8,128)(2,1)}, u32[]{:S(2)}) copy-start(bf16[1024,128]{1,0:T(8,128)(2,1)} %down.3) | copy-start | bytes 786436
  48.9 19.1 %all-to-all-start = ((bf16[16,32,256]{2,1,0:T(8,128)(2,1)}), bf16[16,32,256]{2,1,0:T(8,128)(2,1)S(1)}, u32[]{:S(2)}, u32[]{:S(2)}) async-start(bf16[16,32,256]{2,1,0:T(8,128)(2,1)} %crossing_features.1), calls=%async_computation | async-start | bytes 524288 | tf_op jit(solution)/shard_map/all_to_all | solution.py:813

commit v7 on v6

--- a/solution.py
+++ b/solution.py
@@ -536,7 +536,7 @@
     for copy in pair:
         copy.wait()
     for n in range(0, weight_buf.shape[0], TILE):
-        there = slice(n, n + TILE)
+        there = slice(n, min(n + TILE, weight_buf.shape[0]))
         term = dot_trailing(held[:, depth], weight_buf[there, depth])
         out[:, there] = term if c == 0 else out[:, there] + term
 
@@ -741,7 +741,7 @@
         rows_in, rows_grad, adapter_down_weight, adapter_up_weight, *own_moments, size
     )
     other = other_moments(sent_moments)
-    cuts = [0, width_local // 4, 3 * width_local // 4]
+    cuts = [0, 3 * width_local // 8, 5 * width_local // 8]
 
     def product(rows, k):
         return first_product(rows, output_projection_weight, cuts[k], cuts[k + 1] - cuts[k])

time: 68.1 us -> 67.5 us (level)
  transfers between devices with their start and end apart: 10 -> 10, of which waited for: 1 -> 1; matrix products, arithmetic and copies ran while one was open for 1% -> 1% of each run, Pallas kernels for 46% -> 47%
where the time goes in v7:
time: 67.5 us; the launch traced here: 67.7 us
  Pallas kernels  40 us (59%)
  starting transfers between devices  24 us (36%)
  between operations  1.53 us (2%)
  waiting for transfers between devices  1.31 us (2%)
  other arithmetic  0.87 us (1%)
    ppermute x7, starting transfers between devices, shifted(): lax.ppermute(value, axis, [(i, (i + shift) % size) for i in range(size)])  13.5 us
    pallas_call x2, Pallas kernels, first_product(): call(functools.partial(first_kernel, column), jax.ShapeDtypeStruct((token...  12.5 us
    all_to_all x1, starting transfers between devices, per_device(): lax.all_to_all(buffer, ('seq', 'tensor'), split_axis=0, concat_axis=0, ti...  9.12 us
    pallas_call x1, Pallas kernels, second_product(): call(functools.partial(second_kernel, size, count), jax.ShapeDtypeStruct(...  8.77 us
    pallas_call x2, Pallas kernels, slot_features(): call(functools.partial(slots_kernel, m), [jax.ShapeDtypeStruct((owner.sha...  8.09 us
    pallas_call x1, Pallas kernels, rank_pieces(): call(pieces_kernel, [jax.ShapeDtypeStruct((rows, 2 * rank), BF16)] * size...  4.3 us
    pallas_call x1, Pallas kernels, prepare(): call(prepare_kernel, [jax.ShapeDtypeStruct((tokens, width), BF16), jax.Sh...  2.48 us
    pallas_call x1, Pallas kernels, inner_parts(): call(functools.partial(inner_kernel, size), [jax.ShapeDtypeStruct((2, ran...  1.67 us
  transfers between devices with their start and end apart: 10, of which 1 were waited for; matrix products, arithmetic and copies ran while one was open for 1% of the time, Pallas kernels for 47%

profile of v7, /device:TPU:0, one launch (start us, length us, event | category | flops | bytes accessed | tf_op | source)
XLA Modules:
  0.0 67.7 jit_solution(7992733484892459330)
XLA Ops:
  0.6 4.3 %rank_pieces.1 = (bf16[256,256]{1,0:T(8,128)(2,1)S(1)}, bf16[256,256]{1,0:T(8,128)(2,1)S(1)}, bf16[256,256]{1,0:T(8,128)(2,1)S(1)}, bf16[256,256]{1,0:T(8,128)(2,1)S(1)}, bf16[2,2,64,1024]{3,2,1,0:T(8,128)(2,1)}) custom-call(bf16[1024,1024]{1,0:T(8,128)(2,1)} %bitcast.9, bf16[1024,4096]{1,0:T(8,128)(2,1)} %bitcast.4, bf16[1024,128]{1,0:T(8,128)(2,1)} %down.3, ...), custom_call_target="tpu_custom_call" | custom-call | flops 536870912 | bytes 4194304 | tf_op jit(solution)/shard_map/rank_pieces/pallas_call | solution.py:89
  4.9 3.1 %collective-permute-start = (bf16[256,256]{1,0:T(8,128)(2,1)S(1)}, bf16[256,256]{1,0:T(8,128)(2,1)S(1)}, u32[]{:S(2)}, u32[]{:S(2)}) collective-permute-start(bf16[256,256]{1,0:T(8,128)(2,1)S(1)} %get-tuple-element.46), channel_id=1, source_target_pairs={{0,1},{1,2},{2,3},{3,0},{4,5},{5,6},{6,7},{7,4},{8,9},{9,10},{10,1... | collective-permute-start | bytes 393224 | tf_op jit(solution)/shard_map/ppermute | solution.py:115
  8.0 2.6 %collective-permute-start.1 = (bf16[256,256]{1,0:T(8,128)(2,1)S(1)}, bf16[256,256]{1,0:T(8,128)(2,1)S(1)}, u32[]{:S(2)}, u32[]{:S(2)}) collective-permute-start(bf16[256,256]{1,0:T(8,128)(2,1)S(1)} %get-tuple-element.47), channel_id=1, source_target_pairs={{0,2},{1,3},{2,0},{3,1},{4,6},{5,7},{6,4},{7,5},{8,10},{9,11},{10,... | collective-permute-start | bytes 393224 | tf_op jit(solution)/shard_map/ppermute | solution.py:115
  10.6 1.3 %collective-permute-start.2 = (bf16[256,256]{1,0:T(8,128)(2,1)S(1)}, bf16[256,256]{1,0:T(8,128)(2,1)S(1)}, u32[]{:S(2)}, u32[]{:S(2)}) collective-permute-start(bf16[256,256]{1,0:T(8,128)(2,1)S(1)} %get-tuple-element.48), channel_id=1, source_target_pairs={{0,3},{1,0},{2,1},{3,2},{4,7},{5,4},{6,5},{7,6},{8,11},{9,8},{10,9... | collective-permute-start | bytes 393224 | tf_op jit(solution)/shard_map/ppermute | solution.py:115
  12.0 1.5 %collective-permute-start.6 = (bf16[2,2,64,1024]{3,2,1,0:T(8,128)(2,1)}, bf16[2,2,64,1024]{3,2,1,0:T(8,128)(2,1)S(1)}, u32[]{:S(2)}, u32[]{:S(2)}) collective-permute-start(bf16[2,2,64,1024]{3,2,1,0:T(8,128)(2,1)} %get-tuple-element.56), channel_id=1, source_target_pairs={{0,16},{16,0},{1,17},{17,1},{2,18},{18,2},{3,19},{19,3},{4,20},{20... | collective-permute-start | bytes 1572872 | tf_op jit(solution)/shard_map/ppermute | solution.py:115
  13.5 6.5 %first_product.2.rest_0_ = bf16[1024,384]{1,0:T(8,128)(2,1)S(1)} custom-call(bf16[1024,4096]{1,0:T(8,128)(2,1)} %bitcast.5, bf16[1024,4096]{1,0:T(8,128)(2,1)} %weight.5), custom_call_target="tpu_custom_call" | custom-call | flops 3221225472 | bytes 11534336 | tf_op jit(solution)/shard_map/first_product/pallas_call | solution.py:606
  20.0 0.0 collective-permute-done.refs_1_
  20.0 0.1 total_low.1.rest_2_.rest_0_
  20.1 2.6 %collective-permute-start.3 = (bf16[256,256]{1,0:T(8,128)(2,1)S(1)}, bf16[256,256]{1,0:T(8,128)(2,1)S(1)}, u32[]{:S(2)}, u32[]{:S(2)}) collective-permute-start(bf16[256,256]{1,0:T(8,128)(2,1)S(1)} %total_low.1.rest_2_.rest_0_), channel_id=1, source_target_pairs={{0,1},{1,2},{2,3},{3,0},{4,5},{5,6},{6,7},{7,4},{8,9},{9,10},{10,1... | collective-permute-start | bytes 393224 | tf_op jit(solution)/shard_map/ppermute | solution.py:115
  22.7 1.6 %collective-permute-start.4 = (bf16[256,256]{1,0:T(8,128)(2,1)S(1)}, bf16[256,256]{1,0:T(8,128)(2,1)S(1)}, u32[]{:S(2)}, u32[]{:S(2)}) collective-permute-start(bf16[256,256]{1,0:T(8,128)(2,1)S(1)} %total_low.1.rest_2_.rest_0_), channel_id=1, source_target_pairs={{0,2},{1,3},{2,0},{3,1},{4,6},{5,7},{6,4},{7,5},{8,10},{9,11},{10,... | collective-permute-start | bytes 393224 | tf_op jit(solution)/shard_map/ppermute | solution.py:115
  24.4 0.8 %collective-permute-start.5 = (bf16[256,256]{1,0:T(8,128)(2,1)S(1)}, bf16[256,256]{1,0:T(8,128)(2,1)S(1)}, u32[]{:S(2)}, u32[]{:S(2)}) collective-permute-start(bf16[256,256]{1,0:T(8,128)(2,1)S(1)} %total_low.1.rest_2_.rest_0_), channel_id=1, source_target_pairs={{0,3},{1,0},{2,1},{3,2},{4,7},{5,4},{6,5},{7,6},{8,11},{9,8},{10,9... | collective-permute-start | bytes 393224 | tf_op jit(solution)/shard_map/ppermute | solution.py:115
  25.2 0.6 select_reduce_fusion
  26.5 0.0 copy-start
  26.5 0.0 copy-start.1
  26.5 6.0 %first_product.3.rest_1_ = bf16[1024,256]{1,0:T(8,128)(2,1)S(1)} custom-call(bf16[1024,4096]{1,0:T(8,128)(2,1)} %bitcast.6, bf16[1024,4096]{1,0:T(8,128)(2,1)} %weight.5), custom_call_target="tpu_custom_call" | custom-call | flops 2147483648 | bytes 10485760 | tf_op jit(solution)/shard_map/first_product/pallas_call | solution.py:606
  32.5 0.0 collective-permute-done.6.other
  32.5 2.5 %prepare.1 = (bf16[1024,1024]{1,0:T(8,128)(2,1)S(1)}, bf16[1024,1024]{1,0:T(8,128)(2,1)S(1)}, bf16[1024,256]{1,0:T(8,128)(2,1)S(1)}, f32[2,2,128,1024]{3,2,1,0:T(8,128)S(1)}) custom-call(bf16[1024,1024]{1,0:T(8,128)(2,1)} %bitcast.10, bf16[1024,4096]{1,0:T(8,128)(2,1)} %bitcast.7, bf16[4096,256]{1,0:T(8,128)(2,1)} %width_side.1, f32[2,64,1024]{2,1,0:T(8,128)S(1)} %copy-done, ...), custom_call_target="tpu_custom_call" | custom-call | flops 1048576 | bytes 5242880 | tf_op jit(solution)/shard_map/prepare/pallas_call | solution.py:697
  35.0 0.0 collective-permute-done.5.rest_5_.rest_3_
  35.1 0.0 copy-start.4
  35.1 0.0 copy-start.5
  35.1 1.7 %inner_parts.1 = (bf16[2,128,1024]{2,1,0:T(8,128)(2,1)S(1)}, bf16[2,4,128,256]{3,2,1,0:T(8,128)(2,1)S(1)}) custom-call(s32[1,2,16]{2,1,0:T(2,128)S(1)} %copy-done.3, bf16[1024,1024]{1,0:T(8,128)(2,1)S(1)} %get-tuple-element.79.rows_in.source, bf16[1024,1024]{1,0:T(8,128)(2,1)S(1)} %get-tuple-element.73.rows_grad.source, ...), custom_call_target="tpu_custom_call" | custom-call | flops 536870912 | bytes 4194304 | tf_op jit(solution)/shard_map/inner_parts/pallas_call | solution.py:226
  36.8 0.5 collective-permute-start.7
  37.2 4.0 %slots_in.1 = (bf16[16,16,256]{2,1,0:T(8,128)(2,1)S(1)}, bf16[128,1024]{1,0:T(8,128)(2,1)S(1)}) custom-call(s32[1,2,16]{2,1,0:T(2,128)S(1)} %copy-done.3, s32[1,16]{1,0:T(1,128)S(1)} %copy-done.5, bf16[1024,1024]{1,0:T(8,128)(2,1)S(1)} %get-tuple-element.73.rows_grad.source, f32[2,2,128,1024]{3,2,1,0:T(8,128)S(1)} %get-tuple-element.75.moments, ...), custom_call_target="tpu_custom_call" | custom-call | flops 2147483648 | bytes 4194304 | tf_op jit(solution)/shard_map/slots_in/pallas_call | solution.py:360
  41.3 0.2 add_convert_fusion
  41.5 0.9 %collective-permute-start.8 = (bf16[2,64,1024]{2,1,0:T(8,128)(2,1)S(1)}, bf16[2,64,1024]{2,1,0:T(8,128)(2,1)S(1)}, u32[]{:S(2)}, u32[]{:S(2)}) collective-permute-start(bf16[2,64,1024]{2,1,0:T(8,128)(2,1)S(1)} %get-tuple-element.89), channel_id=1, source_target_pairs={{4,8},{8,4},{5,9},{9,5},{6,10},{10,6},{7,11},{11,7},{20,24},{24,20... | collective-permute-start | bytes 786440 | tf_op jit(solution)/shard_map/ppermute | solution.py:796
  42.4 4.1 %slots_grad.1 = (bf16[16,16,256]{2,1,0:T(8,128)(2,1)S(1)}, bf16[128,1024]{1,0:T(8,128)(2,1)S(1)}) custom-call(s32[1,2,16]{2,1,0:T(2,128)S(1)} %copy-done.3, s32[1,16]{1,0:T(1,128)S(1)} %copy-done.5, bf16[1024,1024]{1,0:T(8,128)(2,1)S(1)} %get-tuple-element.79.rows_in.source, f32[2,2,128,1024]{3,2,1,0:T(8,128)S(1)} %get-tuple-element.75.moments, ...), custom_call_target="tpu_custom_call" | custom-call | flops 2147483648 | bytes 4194304 | tf_op jit(solution)/shard_map/slots_grad/pallas_call | solution.py:360
  46.5 0.0 copy-start.2
  46.5 1.3 %crossing_features.1 = bf16[16,32,256]{2,1,0:T(8,128)(2,1)} custom-call(s32[1,2,16]{2,1,0:T(2,128)S(1)} %copy-done.3, s32[1,16]{1,0:T(1,128)S(1)} %copy-done.5, bf16[16,16,256]{2,1,0:T(8,128)(2,1)S(1)} %get-tuple-element.80.filled_grad, bf16[16,16,256]{2,1,0:T(8,128)(2,1)S(1)} %get-tuple-element.81.filled_in, ...), custom_call_target="tpu_custom_call" | custom-call | flops 134217728 | bytes 1572864 | tf_op jit(solution)/shard_map/crossing_features/pallas_call | solution.py:457
  47.8 9.1 %all-to-all-start = ((bf16[16,32,256]{2,1,0:T(8,128)(2,1)}), bf16[16,32,256]{2,1,0:T(8,128)(2,1)S(1)}, u32[]{:S(2)}, u32[]{:S(2)}) async-start(bf16[16,32,256]{2,1,0:T(8,128)(2,1)} %crossing_features.1), calls=%async_computation | async-start | bytes 524288 | tf_op jit(solution)/shard_map/all_to_all | solution.py:813
  57.0 8.8 %second_product.1 = bf16[1024,1024]{1,0:T(8,128)(2,1)} custom-call(bf16[1024,4096]{1,0:T(8,128)(2,1)} %bitcast.8, bf16[1024,4096]{1,0:T(8,128)(2,1)} %weight.5, bf16[1024,128]{1,0:T(8,128)(2,1)S(1)} %copy-done.2, bf16[1024,384]{1,0:T(8,128)(2,1)S(1)} %first_product.2.rest_0_, bf16[1024,256]{1,0:T(8,128)(2,1)S(1)} %first_product.3.rest_1_, ...), custom_call_target="tpu_custom_call" | custom-call | flops 3221225472 | bytes 11534336 | tf_op jit(solution)/shard_map/second_product/pallas_call | solution.py:629
  65.7 1.3 %all-to-all-done.arrived = bf16[16,32,256]{2,1,0:T(8,128)(2,1)S(1)} async-done(((bf16[16,32,256]{2,1,0:T(8,128)(2,1)}), bf16[16,32,256]{2,1,0:T(8,128)(2,1)S(1)}, u32[]{:S(2)}, u32[]{:S(2)}) %all-to-all-start) | async-done | bytes 262176 | tf_op jit(solution)/shard_map/all_to_all | solution.py:813
  67.0 0.7 owned_features.1
  (14 shorter events, 0.1 us)
Async XLA Ops:
  4.9 15.0 %collective-permute-start = (bf16[256,256]{1,0:T(8,128)(2,1)S(1)}, bf16[256,256]{1,0:T(8,128)(2,1)S(1)}, u32[]{:S(2)}, u32[]{:S(2)}) collective-permute-start(bf16[256,256]{1,0:T(8,128)(2,1)S(1)} %get-tuple-element.46), channel_id=1, source_target_pairs={{0,1},{1,2},{2,3},{3,0},{4,5},{5,6},{6,7},{7,4},{8,9},{9,10},{10,1... | collective-permute-start | bytes 393224 | tf_op jit(solution)/shard_map/ppermute | solution.py:115
  8.0 12.0 %collective-permute-start.1 = (bf16[256,256]{1,0:T(8,128)(2,1)S(1)}, bf16[256,256]{1,0:T(8,128)(2,1)S(1)}, u32[]{:S(2)}, u32[]{:S(2)}) collective-permute-start(bf16[256,256]{1,0:T(8,128)(2,1)S(1)} %get-tuple-element.47), channel_id=1, source_target_pairs={{0,2},{1,3},{2,0},{3,1},{4,6},{5,7},{6,4},{7,5},{8,10},{9,11},{10,... | collective-permute-start | bytes 393224 | tf_op jit(solution)/shard_map/ppermute | solution.py:115
  10.6 9.4 %collective-permute-start.2 = (bf16[256,256]{1,0:T(8,128)(2,1)S(1)}, bf16[256,256]{1,0:T(8,128)(2,1)S(1)}, u32[]{:S(2)}, u32[]{:S(2)}) collective-permute-start(bf16[256,256]{1,0:T(8,128)(2,1)S(1)} %get-tuple-element.48), channel_id=1, source_target_pairs={{0,3},{1,0},{2,1},{3,2},{4,7},{5,4},{6,5},{7,6},{8,11},{9,8},{10,9... | collective-permute-start | bytes 393224 | tf_op jit(solution)/shard_map/ppermute | solution.py:115
  12.0 13.2 %copy-start.3 = (s32[1,2,16]{2,1,0:T(2,128)S(1)}, s32[1,2,16]{2,1,0:T(2,128)}, u32[]{:S(2)}) copy-start(s32[1,2,16]{2,1,0:T(2,128)} %bounds.7) | copy-start | bytes 388
  12.0 20.6 %collective-permute-start.6 = (bf16[2,2,64,1024]{3,2,1,0:T(8,128)(2,1)}, bf16[2,2,64,1024]{3,2,1,0:T(8,128)(2,1)S(1)}, u32[]{:S(2)}, u32[]{:S(2)}) collective-permute-start(bf16[2,2,64,1024]{3,2,1,0:T(8,128)(2,1)} %get-tuple-element.56), channel_id=1, source_target_pairs={{0,16},{16,0},{1,17},{17,1},{2,18},{18,2},{3,19},{19,3},{4,20},{20... | collective-permute-start | bytes 1572872 | tf_op jit(solution)/shard_map/ppermute | solution.py:115
  20.1 14.9 %collective-permute-start.3 = (bf16[256,256]{1,0:T(8,128)(2,1)S(1)}, bf16[256,256]{1,0:T(8,128)(2,1)S(1)}, u32[]{:S(2)}, u32[]{:S(2)}) collective-permute-start(bf16[256,256]{1,0:T(8,128)(2,1)S(1)} %total_low.1.rest_2_.rest_0_), channel_id=1, source_target_pairs={{0,1},{1,2},{2,3},{3,0},{4,5},{5,6},{6,7},{7,4},{8,9},{9,10},{10,1... | collective-permute-start | bytes 393224 | tf_op jit(solution)/shard_map/ppermute | solution.py:115
  22.7 12.3 %collective-permute-start.4 = (bf16[256,256]{1,0:T(8,128)(2,1)S(1)}, bf16[256,256]{1,0:T(8,128)(2,1)S(1)}, u32[]{:S(2)}, u32[]{:S(2)}) collective-permute-start(bf16[256,256]{1,0:T(8,128)(2,1)S(1)} %total_low.1.rest_2_.rest_0_), channel_id=1, source_target_pairs={{0,2},{1,3},{2,0},{3,1},{4,6},{5,7},{6,4},{7,5},{8,10},{9,11},{10,... | collective-permute-start | bytes 393224 | tf_op jit(solution)/shard_map/ppermute | solution.py:115
  24.4 10.7 %collective-permute-start.5 = (bf16[256,256]{1,0:T(8,128)(2,1)S(1)}, bf16[256,256]{1,0:T(8,128)(2,1)S(1)}, u32[]{:S(2)}, u32[]{:S(2)}) collective-permute-start(bf16[256,256]{1,0:T(8,128)(2,1)S(1)} %total_low.1.rest_2_.rest_0_), channel_id=1, source_target_pairs={{0,3},{1,0},{2,1},{3,2},{4,7},{5,4},{6,5},{7,6},{8,11},{9,8},{10,9... | collective-permute-start | bytes 393224 | tf_op jit(solution)/shard_map/ppermute | solution.py:115
  26.5 6.1 %copy-start = (f32[2,64,1024]{2,1,0:T(8,128)S(1)}, f32[2,64,1024]{2,1,0:T(8,128)}, u32[]{:S(2)}) copy-start(f32[2,64,1024]{2,1,0:T(8,128)} %first.3) | copy-start | bytes 1572868
  26.5 6.1 %copy-start.1 = (f32[2,64,1024]{2,1,0:T(8,128)S(1)}, f32[2,64,1024]{2,1,0:T(8,128)}, u32[]{:S(2)}) copy-start(f32[2,64,1024]{2,1,0:T(8,128)} %second.3) | copy-start | bytes 1572868
  35.1 2.2 %copy-start.4 = (f32[16,128]{1,0:T(8,128)S(1)}, f32[16,128]{1,0:T(8,128)}, u32[]{:S(2)}) copy-start(f32[16,128]{1,0:T(8,128)} %rank_side.5) | copy-start | bytes 24580
  35.1 2.2 %copy-start.5 = (s32[1,16]{1,0:T(1,128)S(1)}, s32[1,16]{1,0:T(1,128)}, u32[]{:S(2)}) copy-start(s32[1,16]{1,0:T(1,128)} %owner.5) | copy-start | bytes 196
  36.8 4.5 %collective-permute-start.7 = (bf16[2,128,1024]{2,1,0:T(8,128)(2,1)S(1)}, bf16[2,128,1024]{2,1,0:T(8,128)(2,1)S(1)}, u32[]{:S(2)}, u32[]{:S(2)}) collective-permute-start(bf16[2,128,1024]{2,1,0:T(8,128)(2,1)S(1)} %get-tuple-element.74), channel_id=1, source_target_pairs={{0,4},{4,0},{12,8},{8,12},{1,5},{5,1},{13,9},{9,13},{2,6},{6,2},{1... | collective-permute-start | bytes 1572872 | tf_op jit(solution)/shard_map/ppermute | solution.py:782
  41.5 4.9 %collective-permute-start.8 = (bf16[2,64,1024]{2,1,0:T(8,128)(2,1)S(1)}, bf16[2,64,1024]{2,1,0:T(8,128)(2,1)S(1)}, u32[]{:S(2)}, u32[]{:S(2)}) collective-permute-start(bf16[2,64,1024]{2,1,0:T(8,128)(2,1)S(1)} %get-tuple-element.89), channel_id=1, source_target_pairs={{4,8},{8,4},{5,9},{9,5},{6,10},{10,6},{7,11},{11,7},{20,24},{24,20... | collective-permute-start | bytes 786440 | tf_op jit(solution)/shard_map/ppermute | solution.py:796
  46.5 10.5 %copy-start.2 = (bf16[1024,128]{1,0:T(8,128)(2,1)S(1)}, bf16[1024,128]{1,0:T(8,128)(2,1)}, u32[]{:S(2)}) copy-start(bf16[1024,128]{1,0:T(8,128)(2,1)} %down.3) | copy-start | bytes 786436
  47.8 19.2 %all-to-all-start = ((bf16[16,32,256]{2,1,0:T(8,128)(2,1)}), bf16[16,32,256]{2,1,0:T(8,128)(2,1)S(1)}, u32[]{:S(2)}, u32[]{:S(2)}) async-start(bf16[16,32,256]{2,1,0:T(8,128)(2,1)} %crossing_features.1), calls=%async_computation | async-start | bytes 524288 | tf_op jit(solution)/shard_map/all_to_all | solution.py:813

commit v8 on v7

--- a/solution.py
+++ b/solution.py
@@ -77,7 +77,7 @@
         copy.wait()
     partial[:, rank:] = dot_trailing(rows_grad[...], up_buf[...]).astype(BF16)
     for k, out in enumerate(outs):
-        block = pl.multiple_of(lax.rem(place + k, size) * rows, rows)
+        block = pl.multiple_of(partner(place, k, size) * rows, rows)
         out[...] = partial[pl.ds(block, rows), :]
     cast_copy.wait()
 
@@ -110,13 +110,24 @@
     )(rows_in, rows_grad, down, up, first, second)
 
 
+def partner(place, k, size):
+    if size & (size - 1) == 0:
+        return place ^ abs(k)
+    return (place + k + size) % size
+
+
+def exchanged(value, axis, k):
+    size = lax.axis_size(axis)
+    return lax.ppermute(value, axis, [(i, partner(i, k, size)) for i in range(size)])
+
+
 def shifted(value, axis, shift):
     size = lax.axis_size(axis)
     return lax.ppermute(value, axis, [(i, (i + shift) % size) for i in range(size)])
 
 
 def scatter(pieces):
-    return [shifted(piece, "tensor", k) if k else piece for k, piece in enumerate(pieces)]
+    return [exchanged(piece, "tensor", k) if k else piece for k, piece in enumerate(pieces)]
 
 
 def total_kernel(*refs):
@@ -143,7 +154,7 @@
 
 def gather_pieces(total):
     size = lax.axis_size("tensor")
-    return [total] + [shifted(total, "tensor", k) for k in range(1, size)]
+    return [total] + [exchanged(total, "tensor", k) for k in range(1, size)]
 
 
 def example_scalars(bounds, block):
@@ -164,7 +175,7 @@
     rank = low_scratch.shape[1]
     first = (1 - m) * rank
     for k, piece in enumerate(pieces):
-        low_scratch[lax.rem(place + size - k, size)] = piece[first : first + rank, :]
+        low_scratch[partner(place, -k, size)] = piece[first : first + rank, :]
 
 
 def masked(low_piece, offset, start, end):
@@ -575,7 +586,7 @@
     for copy in extras:
         copy.wait()
     for k in range(size):
-        block = lax.rem(place + size - k, size)
+        block = partner(place, -k, size)
         low_rows[pl.ds(pl.multiple_of(block * rows, rows), rows), :] = (
             pieces_buf[k, rank:, :].astype(F32).T.astype(BF16)
         )

time: 67.5 us -> 67.8 us (level)
  starting transfers between devices: 24 us -> 19.1 us
  Pallas kernels: 40 us -> 42.6 us
  waiting for transfers between devices: 1.31 us -> 3.38 us
    ppermute x7 -> x1, starting transfers between devices: 13.5 us -> 1.68 us  [shifted(): lax.ppermute(value, axis, [(i, (i + shift) % size) for i in range(size)])]
    ppermute x0 -> x6, starting transfers between devices: none -> 10.2 us  [exchanged(): lax.ppermute(value, axis, [(i, partner(i, k, size)) for i in range(size)])]
    pallas_call x2, Pallas kernels: 8.09 us -> 11.2 us  [slot_features(): call(functools.partial(slots_kernel, m), [jax.ShapeDtypeStruct((owner.sha...]
    all_to_all x1, starting transfers between devices: 9.12 us -> 6.27 us  [per_device(): lax.all_to_all(buffer, ('seq', 'tensor'), split_axis=0, concat_axis=0, ti...]
    ppermute x0 -> x6, waiting for transfers between devices: none -> 2.11 us  [exchanged(): lax.ppermute(value, axis, [(i, partner(i, k, size)) for i in range(size)])]
  transfers between devices with their start and end apart: 10 -> 10, of which waited for: 1 -> 2; matrix products, arithmetic and copies ran while one was open for 1% -> 1% of each run, Pallas kernels for 47% -> 52%
where the time goes in v8:
time: 67.8 us; the launch traced here: 67.5 us
  Pallas kernels  42.6 us (63%)
  starting transfers between devices  19.1 us (28%)
  waiting for transfers between devices  3.38 us (5%)
  between operations  1.54 us (2%)
  other arithmetic  0.87 us (1%)
    pallas_call x2, Pallas kernels, first_product(): call(functools.partial(first_kernel, column), jax.ShapeDtypeStruct((token...  12.5 us
    pallas_call x2, Pallas kernels, slot_features(): call(functools.partial(slots_kernel, m), [jax.ShapeDtypeStruct((owner.sha...  11.2 us
    ppermute x6, starting transfers between devices, exchanged(): lax.ppermute(value, axis, [(i, partner(i, k, size)) for i in range(size)])  10.2 us
    pallas_call x1, Pallas kernels, second_product(): call(functools.partial(second_kernel, size, count), jax.ShapeDtypeStruct(...  8.79 us
    all_to_all x1, starting transfers between devices, per_device(): lax.all_to_all(buffer, ('seq', 'tensor'), split_axis=0, concat_axis=0, ti...  6.27 us
    pallas_call x1, Pallas kernels, rank_pieces(): call(pieces_kernel, [jax.ShapeDtypeStruct((rows, 2 * rank), BF16)] * size...  4.29 us
    pallas_call x1, Pallas kernels, prepare(): call(prepare_kernel, [jax.ShapeDtypeStruct((tokens, width), BF16), jax.Sh...  2.48 us
    ppermute x6, waiting for transfers between devices, exchanged(): lax.ppermute(value, axis, [(i, partner(i, k, size)) for i in range(size)])  2.11 us
  transfers between devices with their start and end apart: 10, of which 2 were waited for; matrix products, arithmetic and copies ran while one was open for 1% of the time, Pallas kernels for 52%

profile of v8, /device:TPU:0, one launch (start us, length us, event | category | flops | bytes accessed | tf_op | source)
XLA Modules:
  0.0 67.5 jit_solution(13660525598471242748)
XLA Ops:
  0.6 4.3 %rank_pieces.1 = (bf16[256,256]{1,0:T(8,128)(2,1)S(1)}, bf16[256,256]{1,0:T(8,128)(2,1)S(1)}, bf16[256,256]{1,0:T(8,128)(2,1)S(1)}, bf16[256,256]{1,0:T(8,128)(2,1)S(1)}, bf16[2,2,64,1024]{3,2,1,0:T(8,128)(2,1)}) custom-call(bf16[1024,1024]{1,0:T(8,128)(2,1)} %bitcast.9, bf16[1024,4096]{1,0:T(8,128)(2,1)} %bitcast.4, bf16[1024,128]{1,0:T(8,128)(2,1)} %down.3, ...), custom_call_target="tpu_custom_call" | custom-call | flops 536870912 | bytes 4194304 | tf_op jit(solution)/shard_map/rank_pieces/pallas_call | solution.py:89
  4.9 3.1 %collective-permute-start = (bf16[256,256]{1,0:T(8,128)(2,1)S(1)}, bf16[256,256]{1,0:T(8,128)(2,1)S(1)}, u32[]{:S(2)}, u32[]{:S(2)}) collective-permute-start(bf16[256,256]{1,0:T(8,128)(2,1)S(1)} %get-tuple-element.46), channel_id=1, source_target_pairs={{0,1},{1,0},{2,3},{3,2},{4,5},{5,4},{6,7},{7,6},{8,9},{9,8},{10,11... | collective-permute-start | bytes 393224 | tf_op jit(solution)/shard_map/ppermute | solution.py:121
  8.0 2.6 %collective-permute-start.1 = (bf16[256,256]{1,0:T(8,128)(2,1)S(1)}, bf16[256,256]{1,0:T(8,128)(2,1)S(1)}, u32[]{:S(2)}, u32[]{:S(2)}) collective-permute-start(bf16[256,256]{1,0:T(8,128)(2,1)S(1)} %get-tuple-element.47), channel_id=1, source_target_pairs={{0,2},{1,3},{2,0},{3,1},{4,6},{5,7},{6,4},{7,5},{8,10},{9,11},{10,... | collective-permute-start | bytes 393224 | tf_op jit(solution)/shard_map/ppermute | solution.py:121
  10.6 0.0 collective-permute-start.2
  10.6 1.7 %collective-permute-start.6 = (bf16[2,2,64,1024]{3,2,1,0:T(8,128)(2,1)}, bf16[2,2,64,1024]{3,2,1,0:T(8,128)(2,1)S(1)}, u32[]{:S(2)}, u32[]{:S(2)}) collective-permute-start(bf16[2,2,64,1024]{3,2,1,0:T(8,128)(2,1)} %get-tuple-element.56), channel_id=1, source_target_pairs={{0,16},{16,0},{1,17},{17,1},{2,18},{18,2},{3,19},{19,3},{4,20},{20... | collective-permute-start | bytes 1572872 | tf_op jit(solution)/shard_map/ppermute | solution.py:126
  12.3 6.5 %first_product.2.rest_0_ = bf16[1024,384]{1,0:T(8,128)(2,1)S(1)} custom-call(bf16[1024,4096]{1,0:T(8,128)(2,1)} %bitcast.5, bf16[1024,4096]{1,0:T(8,128)(2,1)} %weight.5), custom_call_target="tpu_custom_call" | custom-call | flops 3221225472 | bytes 11534336 | tf_op jit(solution)/shard_map/first_product/pallas_call | solution.py:617
  18.8 0.0 collective-permute-done.refs_1_
  18.8 2.1 %collective-permute-done.1.refs_2_ = bf16[256,256]{1,0:T(8,128)(2,1)S(1)} collective-permute-done((bf16[256,256]{1,0:T(8,128)(2,1)S(1)}, bf16[256,256]{1,0:T(8,128)(2,1)S(1)}, u32[]{:S(2)}, u32[]{:S(2)}) %collective-permute-start.1) | collective-permute-done | bytes 131104 | tf_op jit(solution)/shard_map/ppermute | solution.py:121
  20.9 0.1 total_low.1.rest_2_.rest_0_
  21.1 2.0 %collective-permute-start.3 = (bf16[256,256]{1,0:T(8,128)(2,1)S(1)}, bf16[256,256]{1,0:T(8,128)(2,1)S(1)}, u32[]{:S(2)}, u32[]{:S(2)}) collective-permute-start(bf16[256,256]{1,0:T(8,128)(2,1)S(1)} %total_low.1.rest_2_.rest_0_), channel_id=1, source_target_pairs={{0,1},{1,0},{2,3},{3,2},{4,5},{5,4},{6,7},{7,6},{8,9},{9,8},{10,11... | collective-permute-start | bytes 393224 | tf_op jit(solution)/shard_map/ppermute | solution.py:121
  23.1 1.1 %collective-permute-start.4 = (bf16[256,256]{1,0:T(8,128)(2,1)S(1)}, bf16[256,256]{1,0:T(8,128)(2,1)S(1)}, u32[]{:S(2)}, u32[]{:S(2)}) collective-permute-start(bf16[256,256]{1,0:T(8,128)(2,1)S(1)} %total_low.1.rest_2_.rest_0_), channel_id=1, source_target_pairs={{0,2},{1,3},{2,0},{3,1},{4,6},{5,7},{6,4},{7,5},{8,10},{9,11},{10,... | collective-permute-start | bytes 393224 | tf_op jit(solution)/shard_map/ppermute | solution.py:121
  24.2 1.4 %collective-permute-start.5 = (bf16[256,256]{1,0:T(8,128)(2,1)S(1)}, bf16[256,256]{1,0:T(8,128)(2,1)S(1)}, u32[]{:S(2)}, u32[]{:S(2)}) collective-permute-start(bf16[256,256]{1,0:T(8,128)(2,1)S(1)} %total_low.1.rest_2_.rest_0_), channel_id=1, source_target_pairs={{0,3},{1,2},{2,1},{3,0},{4,7},{5,6},{6,5},{7,4},{8,11},{9,10},{10,... | collective-permute-start | bytes 393224 | tf_op jit(solution)/shard_map/ppermute | solution.py:121
  25.6 0.6 select_reduce_fusion
  26.9 0.0 copy-start
  26.9 0.0 copy-start.1
  26.9 6.0 %first_product.3.rest_1_ = bf16[1024,256]{1,0:T(8,128)(2,1)S(1)} custom-call(bf16[1024,4096]{1,0:T(8,128)(2,1)} %bitcast.6, bf16[1024,4096]{1,0:T(8,128)(2,1)} %weight.5), custom_call_target="tpu_custom_call" | custom-call | flops 2147483648 | bytes 10485760 | tf_op jit(solution)/shard_map/first_product/pallas_call | solution.py:617
  33.0 2.5 %prepare.1 = (bf16[1024,1024]{1,0:T(8,128)(2,1)S(1)}, bf16[1024,1024]{1,0:T(8,128)(2,1)S(1)}, bf16[1024,256]{1,0:T(8,128)(2,1)S(1)}, f32[2,2,128,1024]{3,2,1,0:T(8,128)S(1)}) custom-call(bf16[1024,1024]{1,0:T(8,128)(2,1)} %bitcast.10, bf16[1024,4096]{1,0:T(8,128)(2,1)} %bitcast.7, bf16[4096,256]{1,0:T(8,128)(2,1)} %width_side.1, f32[2,64,1024]{2,1,0:T(8,128)S(1)} %copy-done, ...), custom_call_target="tpu_custom_call" | custom-call | flops 1048576 | bytes 5242880 | tf_op jit(solution)/shard_map/prepare/pallas_call | solution.py:708
  35.4 0.0 collective-permute-done.3.rest_3_.rest_1_
  35.5 0.0 copy-start.4
  35.5 0.0 copy-start.5
  35.5 1.2 %inner_parts.1 = (bf16[2,128,1024]{2,1,0:T(8,128)(2,1)S(1)}, bf16[2,4,128,256]{3,2,1,0:T(8,128)(2,1)S(1)}) custom-call(s32[1,2,16]{2,1,0:T(2,128)S(1)} %copy-done.3, bf16[1024,1024]{1,0:T(8,128)(2,1)S(1)} %get-tuple-element.79.rows_in.source, bf16[1024,1024]{1,0:T(8,128)(2,1)S(1)} %get-tuple-element.73.rows_grad.source, ...), custom_call_target="tpu_custom_call" | custom-call | flops 536870912 | bytes 4194304 | tf_op jit(solution)/shard_map/inner_parts/pallas_call | solution.py:237
  36.7 0.1 collective-permute-start.7
  36.8 5.6 %slots_in.1 = (bf16[16,16,256]{2,1,0:T(8,128)(2,1)S(1)}, bf16[128,1024]{1,0:T(8,128)(2,1)S(1)}) custom-call(s32[1,2,16]{2,1,0:T(2,128)S(1)} %copy-done.3, s32[1,16]{1,0:T(1,128)S(1)} %copy-done.5, bf16[1024,1024]{1,0:T(8,128)(2,1)S(1)} %get-tuple-element.73.rows_grad.source, f32[2,2,128,1024]{3,2,1,0:T(8,128)S(1)} %get-tuple-element.75.moments, ...), custom_call_target="tpu_custom_call" | custom-call | flops 2147483648 | bytes 4194304 | tf_op jit(solution)/shard_map/slots_in/pallas_call | solution.py:371
  42.4 0.2 add_convert_fusion
  42.7 0.9 %collective-permute-start.8 = (bf16[2,64,1024]{2,1,0:T(8,128)(2,1)S(1)}, bf16[2,64,1024]{2,1,0:T(8,128)(2,1)S(1)}, u32[]{:S(2)}, u32[]{:S(2)}) collective-permute-start(bf16[2,64,1024]{2,1,0:T(8,128)(2,1)S(1)} %get-tuple-element.89), channel_id=1, source_target_pairs={{4,8},{8,4},{5,9},{9,5},{6,10},{10,6},{7,11},{11,7},{20,24},{24,20... | collective-permute-start | bytes 786440 | tf_op jit(solution)/shard_map/ppermute | solution.py:807
  43.5 5.6 %slots_grad.1 = (bf16[16,16,256]{2,1,0:T(8,128)(2,1)S(1)}, bf16[128,1024]{1,0:T(8,128)(2,1)S(1)}) custom-call(s32[1,2,16]{2,1,0:T(2,128)S(1)} %copy-done.3, s32[1,16]{1,0:T(1,128)S(1)} %copy-done.5, bf16[1024,1024]{1,0:T(8,128)(2,1)S(1)} %get-tuple-element.79.rows_in.source, f32[2,2,128,1024]{3,2,1,0:T(8,128)S(1)} %get-tuple-element.75.moments, ...), custom_call_target="tpu_custom_call" | custom-call | flops 2147483648 | bytes 4194304 | tf_op jit(solution)/shard_map/slots_grad/pallas_call | solution.py:371
  49.1 0.0 copy-start.2
  49.1 1.3 %crossing_features.1 = bf16[16,32,256]{2,1,0:T(8,128)(2,1)} custom-call(s32[1,2,16]{2,1,0:T(2,128)S(1)} %copy-done.3, s32[1,16]{1,0:T(1,128)S(1)} %copy-done.5, bf16[16,16,256]{2,1,0:T(8,128)(2,1)S(1)} %get-tuple-element.80.filled_grad, bf16[16,16,256]{2,1,0:T(8,128)(2,1)S(1)} %get-tuple-element.81.filled_in, ...), custom_call_target="tpu_custom_call" | custom-call | flops 134217728 | bytes 1572864 | tf_op jit(solution)/shard_map/crossing_features/pallas_call | solution.py:468
  50.5 6.3 %all-to-all-start = ((bf16[16,32,256]{2,1,0:T(8,128)(2,1)}), bf16[16,32,256]{2,1,0:T(8,128)(2,1)S(1)}, u32[]{:S(2)}, u32[]{:S(2)}) async-start(bf16[16,32,256]{2,1,0:T(8,128)(2,1)} %crossing_features.1), calls=%async_computation | async-start | bytes 524288 | tf_op jit(solution)/shard_map/all_to_all | solution.py:824
  56.8 8.8 %second_product.1 = bf16[1024,1024]{1,0:T(8,128)(2,1)} custom-call(bf16[1024,4096]{1,0:T(8,128)(2,1)} %bitcast.8, bf16[1024,4096]{1,0:T(8,128)(2,1)} %weight.5, bf16[1024,128]{1,0:T(8,128)(2,1)S(1)} %copy-done.2, bf16[1024,384]{1,0:T(8,128)(2,1)S(1)} %first_product.2.rest_0_, bf16[1024,256]{1,0:T(8,128)(2,1)S(1)} %first_product.3.rest_1_, ...), custom_call_target="tpu_custom_call" | custom-call | flops 3221225472 | bytes 11534336 | tf_op jit(solution)/shard_map/second_product/pallas_call | solution.py:640
  65.5 1.3 %all-to-all-done.arrived = bf16[16,32,256]{2,1,0:T(8,128)(2,1)S(1)} async-done(((bf16[16,32,256]{2,1,0:T(8,128)(2,1)}), bf16[16,32,256]{2,1,0:T(8,128)(2,1)S(1)}, u32[]{:S(2)}, u32[]{:S(2)}) %all-to-all-start) | async-done | bytes 262176 | tf_op jit(solution)/shard_map/all_to_all | solution.py:824
  66.8 0.7 owned_features.1
  (14 shorter events, 0.1 us)
Async XLA Ops:
  4.9 13.9 %collective-permute-start = (bf16[256,256]{1,0:T(8,128)(2,1)S(1)}, bf16[256,256]{1,0:T(8,128)(2,1)S(1)}, u32[]{:S(2)}, u32[]{:S(2)}) collective-permute-start(bf16[256,256]{1,0:T(8,128)(2,1)S(1)} %get-tuple-element.46), channel_id=1, source_target_pairs={{0,1},{1,0},{2,3},{3,2},{4,5},{5,4},{6,7},{7,6},{8,9},{9,8},{10,11... | collective-permute-start | bytes 393224 | tf_op jit(solution)/shard_map/ppermute | solution.py:121
  8.0 12.9 %collective-permute-start.1 = (bf16[256,256]{1,0:T(8,128)(2,1)S(1)}, bf16[256,256]{1,0:T(8,128)(2,1)S(1)}, u32[]{:S(2)}, u32[]{:S(2)}) collective-permute-start(bf16[256,256]{1,0:T(8,128)(2,1)S(1)} %get-tuple-element.47), channel_id=1, source_target_pairs={{0,2},{1,3},{2,0},{3,1},{4,6},{5,7},{6,4},{7,5},{8,10},{9,11},{10,... | collective-permute-start | bytes 393224 | tf_op jit(solution)/shard_map/ppermute | solution.py:121
  10.6 10.3 %collective-permute-start.2 = (bf16[256,256]{1,0:T(8,128)(2,1)S(1)}, bf16[256,256]{1,0:T(8,128)(2,1)S(1)}, u32[]{:S(2)}, u32[]{:S(2)}) collective-permute-start(bf16[256,256]{1,0:T(8,128)(2,1)S(1)} %get-tuple-element.48), channel_id=1, source_target_pairs={{0,3},{1,2},{2,1},{3,0},{4,7},{5,6},{6,5},{7,4},{8,11},{9,10},{10,... | collective-permute-start | bytes 393224 | tf_op jit(solution)/shard_map/ppermute | solution.py:121
  10.6 15.0 %copy-start.3 = (s32[1,2,16]{2,1,0:T(2,128)S(1)}, s32[1,2,16]{2,1,0:T(2,128)}, u32[]{:S(2)}) copy-start(s32[1,2,16]{2,1,0:T(2,128)} %bounds.7) | copy-start | bytes 388
  10.6 22.3 %collective-permute-start.6 = (bf16[2,2,64,1024]{3,2,1,0:T(8,128)(2,1)}, bf16[2,2,64,1024]{3,2,1,0:T(8,128)(2,1)S(1)}, u32[]{:S(2)}, u32[]{:S(2)}) collective-permute-start(bf16[2,2,64,1024]{3,2,1,0:T(8,128)(2,1)} %get-tuple-element.56), channel_id=1, source_target_pairs={{0,16},{16,0},{1,17},{17,1},{2,18},{18,2},{3,19},{19,3},{4,20},{20... | collective-permute-start | bytes 1572872 | tf_op jit(solution)/shard_map/ppermute | solution.py:126
  21.1 14.4 %collective-permute-start.3 = (bf16[256,256]{1,0:T(8,128)(2,1)S(1)}, bf16[256,256]{1,0:T(8,128)(2,1)S(1)}, u32[]{:S(2)}, u32[]{:S(2)}) collective-permute-start(bf16[256,256]{1,0:T(8,128)(2,1)S(1)} %total_low.1.rest_2_.rest_0_), channel_id=1, source_target_pairs={{0,1},{1,0},{2,3},{3,2},{4,5},{5,4},{6,7},{7,6},{8,9},{9,8},{10,11... | collective-permute-start | bytes 393224 | tf_op jit(solution)/shard_map/ppermute | solution.py:121
  23.1 12.4 %collective-permute-start.4 = (bf16[256,256]{1,0:T(8,128)(2,1)S(1)}, bf16[256,256]{1,0:T(8,128)(2,1)S(1)}, u32[]{:S(2)}, u32[]{:S(2)}) collective-permute-start(bf16[256,256]{1,0:T(8,128)(2,1)S(1)} %total_low.1.rest_2_.rest_0_), channel_id=1, source_target_pairs={{0,2},{1,3},{2,0},{3,1},{4,6},{5,7},{6,4},{7,5},{8,10},{9,11},{10,... | collective-permute-start | bytes 393224 | tf_op jit(solution)/shard_map/ppermute | solution.py:121
  24.2 11.3 %collective-permute-start.5 = (bf16[256,256]{1,0:T(8,128)(2,1)S(1)}, bf16[256,256]{1,0:T(8,128)(2,1)S(1)}, u32[]{:S(2)}, u32[]{:S(2)}) collective-permute-start(bf16[256,256]{1,0:T(8,128)(2,1)S(1)} %total_low.1.rest_2_.rest_0_), channel_id=1, source_target_pairs={{0,3},{1,2},{2,1},{3,0},{4,7},{5,6},{6,5},{7,4},{8,11},{9,10},{10,... | collective-permute-start | bytes 393224 | tf_op jit(solution)/shard_map/ppermute | solution.py:121
  26.9 6.1 %copy-start = (f32[2,64,1024]{2,1,0:T(8,128)S(1)}, f32[2,64,1024]{2,1,0:T(8,128)}, u32[]{:S(2)}) copy-start(f32[2,64,1024]{2,1,0:T(8,128)} %first.3) | copy-start | bytes 1572868
  26.9 6.1 %copy-start.1 = (f32[2,64,1024]{2,1,0:T(8,128)S(1)}, f32[2,64,1024]{2,1,0:T(8,128)}, u32[]{:S(2)}) copy-start(f32[2,64,1024]{2,1,0:T(8,128)} %second.3) | copy-start | bytes 1572868
  35.5 1.3 %copy-start.4 = (f32[16,128]{1,0:T(8,128)S(1)}, f32[16,128]{1,0:T(8,128)}, u32[]{:S(2)}) copy-start(f32[16,128]{1,0:T(8,128)} %rank_side.5) | copy-start | bytes 24580
  35.5 1.3 %copy-start.5 = (s32[1,16]{1,0:T(1,128)S(1)}, s32[1,16]{1,0:T(1,128)}, u32[]{:S(2)}) copy-start(s32[1,16]{1,0:T(1,128)} %owner.5) | copy-start | bytes 196
  36.7 5.7 %collective-permute-start.7 = (bf16[2,128,1024]{2,1,0:T(8,128)(2,1)S(1)}, bf16[2,128,1024]{2,1,0:T(8,128)(2,1)S(1)}, u32[]{:S(2)}, u32[]{:S(2)}) collective-permute-start(bf16[2,128,1024]{2,1,0:T(8,128)(2,1)S(1)} %get-tuple-element.74), channel_id=1, source_target_pairs={{0,4},{4,0},{12,8},{8,12},{1,5},{5,1},{13,9},{9,13},{2,6},{6,2},{1... | collective-permute-start | bytes 1572872 | tf_op jit(solution)/shard_map/ppermute | solution.py:793
  42.7 6.4 %collective-permute-start.8 = (bf16[2,64,1024]{2,1,0:T(8,128)(2,1)S(1)}, bf16[2,64,1024]{2,1,0:T(8,128)(2,1)S(1)}, u32[]{:S(2)}, u32[]{:S(2)}) collective-permute-start(bf16[2,64,1024]{2,1,0:T(8,128)(2,1)S(1)} %get-tuple-element.89), channel_id=1, source_target_pairs={{4,8},{8,4},{5,9},{9,5},{6,10},{10,6},{7,11},{11,7},{20,24},{24,20... | collective-permute-start | bytes 786440 | tf_op jit(solution)/shard_map/ppermute | solution.py:807
  49.1 7.6 %copy-start.2 = (bf16[1024,128]{1,0:T(8,128)(2,1)S(1)}, bf16[1024,128]{1,0:T(8,128)(2,1)}, u32[]{:S(2)}) copy-start(bf16[1024,128]{1,0:T(8,128)(2,1)} %down.3) | copy-start | bytes 786436
  50.5 16.3 %all-to-all-start = ((bf16[16,32,256]{2,1,0:T(8,128)(2,1)}), bf16[16,32,256]{2,1,0:T(8,128)(2,1)S(1)}, u32[]{:S(2)}, u32[]{:S(2)}) async-start(bf16[16,32,256]{2,1,0:T(8,128)(2,1)} %crossing_features.1), calls=%async_computation | async-start | bytes 524288 | tf_op jit(solution)/shard_map/all_to_all | solution.py:824
